TPU v7x, 32 devices: a whole 2x2x4 slice. The times are simulated.
32 devices in a mesh: gx: 8 (over z, x), gy: 4 (over y, core).
Axes of the slice: x: 2, y: 2, z: 4, core: 2. Of those that a mesh axis runs over, the one named last changes fastest.
Arguments:
- features: bfloat16 [16, 8, 16, 128], P('gx', 'gy'), may hold values from -6 to 6
- positions: float32 [16, 8, 3, 16], P('gx', 'gy')
- species: int32 [16, 8, 16], P('gx', 'gy'), may hold values from 0 to 5
- neighbours: int32 [16, 8, 16, 32], P('gx', 'gy'), may hold values from 0 to 143, as said below
- counts: int32 [16, 8, 16], P('gx', 'gy'), may hold values from 0 to 32, as said below
- species_gain: float32 [6, 128], replicated, may hold values from 0.1 to 1.9
- radial_in: float32 [2, 8, 64], replicated, may hold values from -4 to 4
- radial_out: float32 [2, 64, 384], replicated, may hold values from -1 to 1
- mixing: float32 [2, 384, 128], replicated, may hold values from -0.3125 to 0.3125
- readout: float32 [128], replicated, may hold values from -0.5 to 0.5
Outputs:
- energy: float32 [16, 8, 16], P('gx', 'gy')
- forces: float32 [16, 8, 3, 16], P('gx', 'gy')
- feature_grad: float32 [16, 8, 16, 128], P('gx', 'gy')
Inputs may be any that keep to these rules, and one draw needn't show every extreme that they name: `neighbours`: A code n names the atom in slot n % 16 of the column displaced by ((n // 16) // 3 - 1, (n // 16) % 3 - 1) columns, periodically; the codes of one atom are distinct and never name the atom itself. Neighbour slots 0 to counts - 1 of an atom are live, the rest padding.
All inputs are finite; a program needn't handle non-finite values.
Results may differ from a plain program's by a relative error of at most 0.007.
Values may be sent and summed in bfloat16 or wider, within the bound.
No kernel may reach another device: no remote copies, remote signals or barrier semaphores. Data moves between devices by JAX's collectives and lax.ppermute only.
A program may use at most 64 MiB of HBM per device.

v0:
```python
import jax
import jax.numpy as jnp
from jax import lax
from jax.sharding import PartitionSpec as P

column = 6.0
cutoff = 6.0
softening = 0.01
root_three = 3.0**0.5
highest = lax.Precision.HIGHEST


def extended(x, sides, width):
    for axis, dim in sides:
        devices, length = (lax.axis_size(axis), x.shape[dim])
        up = [(i, (i + 1) % devices) for i in range(devices)]
        down = [(j, i) for i, j in up]
        last = lax.slice_in_dim(x, length - width, length, axis=dim)
        initial = lax.slice_in_dim(x, 0, width, axis=dim)
        before = lax.ppermute(last, axis, up)
        after = lax.ppermute(initial, axis, down)
        x = jnp.concatenate([before, x, after], axis=dim)
    return x


def harmonics(unit_x, unit_y, unit_z):
    square = unit_x * unit_x + unit_y * unit_y + unit_z * unit_z
    return jnp.stack(
        [
            jnp.ones_like(unit_x),
            unit_x,
            unit_y,
            unit_z,
            root_three * unit_x * unit_y,
            root_three * unit_y * unit_z,
            0.5 * (3.0 * unit_z * unit_z - square),
            root_three * unit_x * unit_z,
            0.5 * root_three * (unit_x * unit_x - unit_y * unit_y),
        ],
        axis=1,
    )


def layer_block(
    own_x, own_y, own_z, own_feat, other_x, other_y, other_z, other_feat, live_mask, weights
):
    weight_in, weight_out, weight_mix = weights
    sep_x = other_x - own_x[:, None]
    sep_y = other_y - own_y[:, None]
    sep_z = other_z - own_z[:, None]
    dist_sq = sep_x * sep_x + sep_y * sep_y + sep_z * sep_z
    distance = jnp.sqrt(dist_sq + softening)
    envelope = jnp.square(jnp.maximum(1.0 - dist_sq / (cutoff * cutoff), 0.0)) * live_mask
    basis_count = weight_in.shape[0]
    spacing = cutoff / (basis_count - 1)
    centres = spacing * jnp.arange(basis_count, dtype=jnp.float32)
    radial_basis = jnp.exp(-jnp.square((distance[..., None] - centres) / spacing))
    hidden = jax.nn.silu(jnp.einsum("bkn,nh->bkh", radial_basis, weight_in, precision=highest))
    radial = jnp.einsum("bkh,hq->bkq", hidden, weight_out, precision=highest) * envelope[..., None]
    channels = other_feat.shape[-1]
    angular = harmonics(sep_x / cutoff, sep_y / cutoff, sep_z / cutoff)
    scalar = jnp.einsum(
        "bmk,bkc->bmc", angular[:, 0:1], radial[..., :channels] * other_feat, precision=highest
    )[:, 0]
    vector = jnp.einsum(
        "bmk,bkc->bmc",
        angular[:, 1:4],
        radial[..., channels : 2 * channels] * other_feat,
        precision=highest,
    )
    tensor = jnp.einsum(
        "bmk,bkc->bmc", angular[:, 4:9], radial[..., 2 * channels :] * other_feat, precision=highest
    )
    invariants = jnp.concatenate(
        [scalar, jnp.sum(vector * vector, axis=1), jnp.sum(tensor * tensor, axis=1)], axis=-1
    )
    return jnp.dot(invariants, weight_mix, precision=highest) + own_feat


def layer(pos_all, feat_all, own_pos, own_feat, edge_lists, weights):
    channels = feat_all.shape[-1]
    slot_count = own_feat.shape[2]
    columns = own_feat.shape[0] * own_feat.shape[1]
    flat_x = pos_all[:, :, 0, :].reshape(-1)
    flat_y = pos_all[:, :, 1, :].reshape(-1)
    flat_z = pos_all[:, :, 2, :].reshape(-1)
    flat_feat = feat_all.reshape(-1, channels)
    owned = (
        own_pos[:, :, 0, :].reshape(columns, slot_count),
        own_pos[:, :, 1, :].reshape(columns, slot_count),
        own_pos[:, :, 2, :].reshape(columns, slot_count),
        own_feat.reshape(columns, slot_count, channels),
    )

    def one_column(column_items):
        other_index, move_x, move_y, live_mask, own_x, own_y, own_z, own_rows = column_items
        return layer_block(
            own_x,
            own_y,
            own_z,
            own_rows,
            flat_x[other_index] + move_x,
            flat_y[other_index] + move_y,
            flat_z[other_index],
            flat_feat[other_index],
            live_mask,
            weights,
        )

    return lax.map(jax.checkpoint(one_column), edge_lists + owned).reshape(-1, channels)


def fold_rim(rimmed):
    row_count = rimmed.shape[0] - 4
    col_count = rimmed.shape[1] - 4
    interior = rimmed[2 : row_count + 2, 2 : col_count + 2]
    interior = interior.at[0].add(rimmed[0, 2 : col_count + 2])
    interior = interior.at[row_count - 1].add(rimmed[row_count + 3, 2 : col_count + 2])
    interior = interior.at[:, 0].add(rimmed[2 : row_count + 2, 0])
    interior = interior.at[:, col_count - 1].add(rimmed[2 : row_count + 2, col_count + 3])
    interior = interior.at[0, 0].add(rimmed[0, 0])
    interior = interior.at[0, col_count - 1].add(rimmed[0, col_count + 3])
    interior = interior.at[row_count - 1, 0].add(rimmed[row_count + 3, 0])
    interior = interior.at[row_count - 1, col_count - 1].add(rimmed[row_count + 3, col_count + 3])
    return interior


def send_back(feat_grad, pos_grad):
    rim_feat, rim_pos = (
        extended(feat_grad, (("gx", 0), ("gy", 1)), 1),
        extended(pos_grad, (("gx", 0), ("gy", 1)), 1),
    )
    return (fold_rim(rim_feat), fold_rim(rim_pos))


def shards(
    features,
    positions,
    species,
    neighbours,
    counts,
    species_gain,
    radial_in,
    radial_out,
    mixing,
    readout,
):
    cols_x, cols_y, slot_count, channels = features.shape
    neigh_count = neighbours.shape[-1]
    kind_count = species_gain.shape[0]
    onehot = (species[..., None] == jnp.arange(kind_count, dtype=jnp.int32)).astype(jnp.float32)
    gain_rows = jnp.einsum("abse,ec->absc", onehot, species_gain, precision=highest)
    layer_one = (features.astype(jnp.float32) * gain_rows).astype(jnp.bfloat16)
    ext_pos = extended(positions, (("gx", 0), ("gy", 1)), 1)
    ext_one = extended(layer_one, (("gx", 0), ("gy", 1)), 1)
    offsets = neighbours // slot_count
    slot_of = neighbours % slot_count
    step_x = offsets // 3 - 1
    step_y = offsets % 3 - 1
    col_x = jnp.arange(cols_x, dtype=jnp.int32)[:, None, None, None]
    col_y = jnp.arange(cols_y, dtype=jnp.int32)[None, :, None, None]
    other_atom = ((col_x + 1 + step_x) * (cols_y + 2) + col_y + 1 + step_y) * slot_count + slot_of
    shift_x = step_x.astype(jnp.float32) * column
    shift_y = step_y.astype(jnp.float32) * column
    validity = (jnp.arange(neigh_count, dtype=jnp.int32) < counts[..., None]).astype(jnp.float32)
    columns = cols_x * cols_y
    edge_lists = (
        other_atom.reshape(columns, slot_count, neigh_count),
        shift_x.reshape(columns, slot_count, neigh_count),
        shift_y.reshape(columns, slot_count, neigh_count),
        validity.reshape(columns, slot_count, neigh_count),
    )
    weights_one = (radial_in[0], radial_out[0], mixing[0])
    weights_two = (radial_in[1], radial_out[1], mixing[1])

    def first_layer(coords, values):
        return layer(
            coords, values, coords[1:-1, 1:-1], values[1:-1, 1:-1], edge_lists, weights_one
        )

    def second_layer(coords, values):
        return layer(
            coords, values, coords[1:-1, 1:-1], values[1:-1, 1:-1], edge_lists, weights_two
        )

    z_one, back_one = jax.vjp(first_layer, ext_pos, ext_one.astype(jnp.float32))
    layer_two = z_one.astype(jnp.bfloat16).reshape(cols_x, cols_y, slot_count, channels)
    ext_two = extended(layer_two, (("gx", 0), ("gy", 1)), 1)
    z_two, back_two = jax.vjp(second_layer, ext_pos, ext_two.astype(jnp.float32))
    energy = jnp.dot(jax.nn.silu(z_two), readout, precision=highest)
    sigmoid = jax.nn.sigmoid(z_two)
    z_grad = sigmoid * (1.0 + z_two * (1.0 - sigmoid)) * readout
    pos_two, feat_two = back_two(z_grad)
    owned_feat_two, owned_pos_two = send_back(feat_two, pos_two)
    pos_one, feat_one = back_one(owned_feat_two.reshape(-1, channels))
    owned_feat_one, owned_pos_one = send_back(feat_one, pos_one)
    forces = -(owned_pos_one + owned_pos_two)
    return (energy.reshape(cols_x, cols_y, slot_count), forces, owned_feat_one)


def solution(mesh):
    placed = (
        P("gx", "gy", None, None),
        P("gx", "gy", None, None),
        P("gx", "gy", None),
        P("gx", "gy", None, None),
        P("gx", "gy", None),
        P(),
        P(),
        P(),
        P(),
        P(),
    )
    return jax.shard_map(
        shards,
        mesh=mesh,
        in_specs=placed,
        out_specs=(P("gx", "gy", None), P("gx", "gy", None, None), P("gx", "gy", None, None)),
        check_vma=False,
    )
```

profile of v0, /device:TPU:0, one launch (start us, length us, event | category | flops | bytes accessed | tf_op | source)
XLA Modules:
  0.0 542.9 jit_solution(10393678512294926289)
XLA Ops:
  8.4 4.7 collective-permute-start.1
  22.4 62.2 %while.120 = (s32[]{:T(128)}, bf16[4,16,128]{2,1,0:T(8,128)(2,1)S(1)}, s32[4,16,32]{2,1,0:T(8,128)S(1)}, f32[256]{0:T(256)S(1)}, f32[4,16,32]{2,1,0:T(8,128)S(1)...) while((s32[]{:T(128)}, ...), condition=%wide.region_3.4_spmd.clone, body=%wide.region_0.3_spmd.clone.sunk | while | flops 171271184 | bytes 3836885 | solution.py:110
  22.5 3.5 gather_fusion.9
  26.1 3.5 gather_fusion.10
  38.1 3.5 gather_fusion.9
  45.2 3.5 gather_fusion.11
  53.6 3.5 gather_fusion.9
  57.2 3.5 gather_fusion.10
  60.8 3.5 gather_fusion.11
  69.2 3.5 gather_fusion.9
  76.3 3.5 gather_fusion.11
  85.2 4.7 collective-permute-start.9
  94.9 62.2 %while.121 = (s32[]{:T(128)}, f32[4,16,128]{2,1,0:T(8,128)S(1)}, s32[4,16,32]{2,1,0:T(8,128)S(1)}, f32[256]{0:T(256)S(1)}, f32[4,16,32]{2,1,0:T(8,128)S(1)}, /*i...) while((s32[]{:T(128)}, f32[4,16,128]{2,1,0:T(8,128)S(1)}, ...), condition=%wide.region_7.8_spmd.clone, body=%wide.region_4.7_spmd.clone.sunk | while | flops 171271184 | bytes 3836885 | solution.py:110
  95.0 3.5 gather_fusion.13
  98.6 3.5 gather_fusion.14
  102.2 3.5 gather_fusion.15
  110.6 3.5 gather_fusion.13
  114.2 3.5 gather_fusion.14
  126.1 3.5 gather_fusion.13
  129.7 3.5 gather_fusion.14
  141.7 3.5 gather_fusion.13
  148.8 3.5 gather_fusion.15
  160.2 169.1 %while.118 = (s32[]{:T(128)}, f32[256]{0:T(256)S(1)}, f32[256]{0:T(256)S(1)}, f32[256]{0:T(256)S(1)}, f32[256,128]{1,0:T(8,128)S(1)}, /*index=5*/f32[4,16]{1,0:T...) while((s32[]{:T(128)}, f32[256]{0:T(256)S(1)}, ...), condition=%wide.region_18.19_spmd, body=%wide.region_8.18_spmd.sunk | while | flops 340472832 | bytes 12468577 | solution.py:110
  161.9 3.5 gather_fusion.3
  165.5 3.5 gather_fusion.1
  169.1 3.5 gather_fusion
  182.6 4.1 scatter_fusion.2
  188.3 4.1 scatter_fusion.1
  192.7 4.1 scatter_fusion
  204.1 3.5 gather_fusion.3
  207.7 3.5 gather_fusion.1
  211.3 3.5 gather_fusion
  224.9 4.1 scatter_fusion.2
  230.5 4.1 scatter_fusion.1
  234.9 4.1 scatter_fusion
  246.3 3.5 gather_fusion.3
  249.9 3.5 gather_fusion.1
  267.1 4.1 scatter_fusion.2
  272.7 4.1 scatter_fusion.1
  277.1 4.1 scatter_fusion
  288.5 3.5 gather_fusion.3
  309.3 4.1 scatter_fusion.2
  314.9 4.1 scatter_fusion.1
  319.3 4.1 scatter_fusion
  331.8 4.8 collective-permute-start.21
  349.2 167.5 %while.119 = (s32[]{:T(128)}, f32[256]{0:T(256)S(1)}, f32[256]{0:T(256)S(1)}, f32[256]{0:T(256)S(1)}, f32[256,128]{1,0:T(8,128)S(1)}, /*index=5*/f32[4,16]{1,0:T...) while((s32[]{:T(128)}, f32[256]{0:T(256)S(1)}, ...), condition=%wide.region_29.30_spmd, body=%wide.region_19.29_spmd.sunk | while | flops 340472832 | bytes 12433593 | solution.py:110
  361.1 3.5 gather_fusion.7
  381.3 4.1 scatter_fusion.6
  385.8 4.1 scatter_fusion.5
  390.2 4.1 scatter_fusion.4
  400.4 3.5 gather_fusion.7
  420.6 4.1 scatter_fusion.6
  425.0 4.1 scatter_fusion.5
  429.4 4.1 scatter_fusion.4
  439.6 3.5 gather_fusion.7
  459.8 4.1 scatter_fusion.6
  464.2 4.1 scatter_fusion.5
  468.6 4.1 scatter_fusion.4
  478.8 3.5 gather_fusion.7
  499.1 4.1 scatter_fusion.6
  503.5 4.1 scatter_fusion.5
  507.9 4.1 scatter_fusion.4
  517.8 4.7 collective-permute-start.17
  522.6 4.7 collective-permute-start.25
  (960 shorter events, 297.6 us)
Async XLA Ops:
  2.3 6.1 %copy-start.22 = (f32[2,2,3,16]{3,1,2,0:T(2,128)S(1)}, f32[2,2,3,16]{3,1,2,0:T(2,128)}, u32[]{:S(2)}) copy-start(f32[2,2,3,16]{3,1,2,0:T(2,128)} %param.83) | copy-start | bytes 2308
  2.3 16.8 %collective-permute-start.4 = (bf16[1,2,16,128]{3,2,1,0:T(8,128)(2,1)S(1)}, bf16[1,2,16,128]{3,2,1,0:T(8,128)(2,1)S(1)}, u32[]{:S(2)}, u32[]{:S(2)}) collective-permute-start(bf16[1,2,16,128]{3,2,1,0:T(8,128)(2,1)S(1)} %get-tuple-element.2398), channel_id=1, source_target_pairs={{0,4},{4,8},{8,12},{12,16},{16,20},{20,24},{24,28},{28,0},{1,5},{5... | collective-permute-start | bytes 24584 | tf_op jit(solution)/shard_map/ppermute | solution.py:20
  5.3 7.9 %copy-start.19 = (s32[2,2,16,32]{3,2,1,0:T(8,128)S(1)}, s32[2,2,16,32]{3,2,1,0:T(8,128)}, u32[]{:S(2)}) copy-start(s32[2,2,16,32]{3,2,1,0:T(8,128)} %param.85) | copy-start | bytes 24580
  5.3 13.8 %collective-permute-start.5 = (bf16[1,2,16,128]{3,2,1,0:T(8,128)(2,1)S(1)}, bf16[1,2,16,128]{3,2,1,0:T(8,128)(2,1)S(1)}, u32[]{:S(2)}, u32[]{:S(2)}) collective-permute-start(bf16[1,2,16,128]{3,2,1,0:T(8,128)(2,1)S(1)} %get-tuple-element.2399), channel_id=1, source_target_pairs={{4,0},{8,4},{12,8},{16,12},{20,16},{24,20},{28,24},{0,28},{5,1},{9... | collective-permute-start | bytes 24584 | tf_op jit(solution)/shard_map/ppermute | solution.py:21
  8.4 7.4 %collective-permute-start = (f32[1,2,3,16]{3,1,2,0:T(2,128)S(1)}, f32[1,2,3,16]{3,1,2,0:T(2,128)S(1)}, u32[]{:S(2)}, u32[]{:S(2)}) collective-permute-start(f32[1,2,3,16]{3,1,2,0:T(2,128)S(1)} %get-tuple-element.2408), channel_id=1, source_target_pairs={{0,4},{4,8},{8,12},{12,16},{16,20},{20,24},{24,28},{28,0},{1,5},{5... | collective-permute-start | bytes 1160 | tf_op jit(solution)/shard_map/ppermute | solution.py:20
  8.4 7.4 %collective-permute-start.1 = (f32[1,2,3,16]{3,1,2,0:T(2,128)S(1)}, f32[1,2,3,16]{3,1,2,0:T(2,128)S(1)}, u32[]{:S(2)}, u32[]{:S(2)}) collective-permute-start(f32[1,2,3,16]{3,1,2,0:T(2,128)S(1)} %get-tuple-element.2407), channel_id=1, source_target_pairs={{4,0},{8,4},{12,8},{16,12},{20,16},{24,20},{28,24},{0,28},{5,1},{9... | collective-permute-start | bytes 1160 | tf_op jit(solution)/shard_map/ppermute | solution.py:21
  14.0 1.1 copy-start.18
  15.9 3.1 collective-permute-start.2
  15.9 3.1 collective-permute-start.3
  19.1 3.2 collective-permute-start.6
  20.9 1.5 collective-permute-start.7
  84.6 10.2 %copy-start.1 = (f32[256,128]{1,0:T(8,128)}, f32[256,128]{1,0:T(8,128)S(1)}, u32[]{:S(2)}) copy-start(f32[256,128]{1,0:T(8,128)S(1)} %get-tuple-element.3418) | copy-start | bytes 393220
  84.6 10.2 %copy-start.3 = (f32[384,128]{1,0:T(8,128)}, f32[384,128]{1,0:T(8,128)S(1)}, u32[]{:S(2)}) copy-start(f32[384,128]{1,0:T(8,128)S(1)} %get-tuple-element.3420) | copy-start | bytes 589828
  84.6 10.3 %copy-start.5 = (f32[64,384]{1,0:T(8,128)}, f32[64,384]{1,0:T(8,128)S(1)}, u32[]{:S(2)}) copy-start(f32[64,384]{1,0:T(8,128)S(1)} %get-tuple-element.3425) | copy-start | bytes 294916
  85.2 6.3 %collective-permute-start.8 = (bf16[1,2,16,128]{3,2,1,0:T(8,128)(2,1)S(1)}, bf16[1,2,16,128]{3,2,1,0:T(8,128)(2,1)S(1)}, u32[]{:S(2)}, u32[]{:S(2)}) collective-permute-start(bf16[1,2,16,128]{3,2,1,0:T(8,128)(2,1)S(1)} %get-tuple-element.2396), channel_id=1, source_target_pairs={{0,4},{4,8},{8,12},{12,16},{16,20},{20,24},{24,28},{28,0},{1,5},{5... | collective-permute-start | bytes 24584 | tf_op jit(solution)/shard_map/ppermute | solution.py:20
  85.2 6.3 %collective-permute-start.9 = (bf16[1,2,16,128]{3,2,1,0:T(8,128)(2,1)S(1)}, bf16[1,2,16,128]{3,2,1,0:T(8,128)(2,1)S(1)}, u32[]{:S(2)}, u32[]{:S(2)}) collective-permute-start(bf16[1,2,16,128]{3,2,1,0:T(8,128)(2,1)S(1)} %get-tuple-element.2397), channel_id=1, source_target_pairs={{4,0},{8,4},{12,8},{16,12},{20,16},{24,20},{28,24},{0,28},{5,1},{9... | collective-permute-start | bytes 24584 | tf_op jit(solution)/shard_map/ppermute | solution.py:21
  91.6 3.2 collective-permute-start.10
  92.2 2.6 collective-permute-start.11
  157.1 1.3 copy-start.20
  160.2 188.9 %copy-start.6 = (f32[64,384]{1,0:T(8,128)S(1)}, f32[64,384]{1,0:T(8,128)}, u32[]{:S(2)}) copy-start(f32[64,384]{1,0:T(8,128)} %copy-done.5) | copy-start | bytes 294916
  160.5 1.3 copy-start.30
  172.8 0.8 copy-start.11
  172.8 0.7 copy-start.13
  178.7 0.9 copy-start.14
  198.1 4.0 copy-start.8
  202.7 1.3 copy-start.30
  215.0 0.8 copy-start.11
  215.0 0.7 copy-start.13
  220.9 0.9 copy-start.14
  240.3 4.0 copy-start.8
  244.9 1.3 copy-start.30
  257.2 0.8 copy-start.11
  257.3 0.7 copy-start.13
  263.1 0.9 copy-start.14
  282.5 4.0 copy-start.8
  287.1 1.3 copy-start.30
  299.5 0.8 copy-start.11
  299.5 0.7 copy-start.13
  305.4 0.9 copy-start.14
  324.7 4.0 copy-start.8
  330.7 12.8 %collective-permute-start.12 = (f32[1,4,16,128]{3,2,1,0:T(8,128)S(1)}, f32[1,4,16,128]{3,2,1,0:T(8,128)S(1)}, u32[]{:S(2)}, u32[]{:S(2)}) collective-permute-start(f32[1,4,16,128]{3,2,1,0:T(8,128)S(1)} %get-tuple-element.2378), channel_id=1, source_target_pairs={{0,4},{4,8},{8,12},{12,16},{16,20},{20,24},{24,28},{28,0},{1,5},{5... | collective-permute-start | bytes 98312 | tf_op jit(solution)/shard_map/ppermute | solution.py:20
  331.7 4.9 copy-start.21
  331.8 7.9 %collective-permute-start.20 = (f32[1,4,3,16]{3,1,0,2:T(4,128)S(1)}, f32[1,4,3,16]{3,1,0,2:T(4,128)S(1)}, u32[]{:S(2)}, u32[]{:S(2)}) collective-permute-start(f32[1,4,3,16]{3,1,0,2:T(4,128)S(1)} %get-tuple-element.2390), channel_id=1, source_target_pairs={{0,4},{4,8},{8,12},{12,16},{16,20},{20,24},{24,28},{28,0},{1,5},{5... | collective-permute-start | bytes 2312 | tf_op jit(solution)/shard_map/ppermute | solution.py:20
  331.8 4.8 copy-start.34
  331.8 7.8 %collective-permute-start.21 = (f32[1,4,3,16]{3,1,0,2:T(4,128)S(1)}, f32[1,4,3,16]{3,1,0,2:T(4,128)S(1)}, u32[]{:S(2)}, u32[]{:S(2)}) collective-permute-start(f32[1,4,3,16]{3,1,0,2:T(4,128)S(1)} %get-tuple-element.2389), channel_id=1, source_target_pairs={{4,0},{8,4},{12,8},{16,12},{20,16},{24,20},{28,24},{0,28},{5,1},{9... | collective-permute-start | bytes 2312 | tf_op jit(solution)/shard_map/ppermute | solution.py:21
  337.6 5.9 %collective-permute-start.13 = (f32[1,4,16,128]{3,2,1,0:T(8,128)S(1)}, f32[1,4,16,128]{3,2,1,0:T(8,128)S(1)}, u32[]{:S(2)}, u32[]{:S(2)}) collective-permute-start(f32[1,4,16,128]{3,2,1,0:T(8,128)S(1)} %get-tuple-element.2377), channel_id=1, source_target_pairs={{4,0},{8,4},{12,8},{16,12},{20,16},{24,20},{28,24},{0,28},{5,1},{9... | collective-permute-start | bytes 98312 | tf_op jit(solution)/shard_map/ppermute | solution.py:21
  339.7 3.1 collective-permute-start.22
  340.6 2.3 collective-permute-start.23
  343.5 3.6 collective-permute-start.14
  345.3 1.8 collective-permute-start.15
  345.4 3.8 copy-start.4
  347.1 2.0 copy-start.2
  395.6 3.4 copy-start.10
  434.8 3.4 copy-start.10
  474.0 3.4 copy-start.10
  513.3 3.4 copy-start.10
  517.7 9.6 %collective-permute-start.16 = (f32[1,4,3,16]{3,1,0,2:T(4,128)S(1)}, f32[1,4,3,16]{3,1,0,2:T(4,128)S(1)}, u32[]{:S(2)}, u32[]{:S(2)}) collective-permute-start(f32[1,4,3,16]{3,1,0,2:T(4,128)S(1)} %get-tuple-element.2392), channel_id=1, source_target_pairs={{0,4},{4,8},{8,12},{12,16},{16,20},{20,24},{24,28},{28,0},{1,5},{5... | collective-permute-start | bytes 2312 | tf_op jit(solution)/shard_map/ppermute | solution.py:20
  517.8 9.5 %collective-permute-start.17 = (f32[1,4,3,16]{3,1,0,2:T(4,128)S(1)}, f32[1,4,3,16]{3,1,0,2:T(4,128)S(1)}, u32[]{:S(2)}, u32[]{:S(2)}) collective-permute-start(f32[1,4,3,16]{3,1,0,2:T(4,128)S(1)} %get-tuple-element.2391), channel_id=1, source_target_pairs={{4,0},{8,4},{12,8},{16,12},{20,16},{24,20},{28,24},{0,28},{5,1},{9... | collective-permute-start | bytes 2312 | tf_op jit(solution)/shard_map/ppermute | solution.py:21
  522.5 14.7 %collective-permute-start.24 = (f32[1,4,16,128]{3,2,1,0:T(8,128)S(1)}, f32[1,4,16,128]{3,2,1,0:T(8,128)S(1)}, u32[]{:S(2)}, u32[]{:S(2)}) collective-permute-start(f32[1,4,16,128]{3,2,1,0:T(8,128)S(1)} %get-tuple-element.2376), channel_id=1, source_target_pairs={{0,4},{4,8},{8,12},{12,16},{16,20},{20,24},{24,28},{28,0},{1,5},{5... | collective-permute-start | bytes 98312 | tf_op jit(solution)/shard_map/ppermute | solution.py:20
  522.6 14.6 %collective-permute-start.25 = (f32[1,4,16,128]{3,2,1,0:T(8,128)S(1)}, f32[1,4,16,128]{3,2,1,0:T(8,128)S(1)}, u32[]{:S(2)}, u32[]{:S(2)}) collective-permute-start(f32[1,4,16,128]{3,2,1,0:T(8,128)S(1)} %get-tuple-element.2375), channel_id=1, source_target_pairs={{4,0},{8,4},{12,8},{16,12},{20,16},{24,20},{28,24},{0,28},{5,1},{9... | collective-permute-start | bytes 98312 | tf_op jit(solution)/shard_map/ppermute | solution.py:21
  527.3 3.1 collective-permute-start.18
  528.0 2.5 collective-permute-start.19
  537.2 3.6 collective-permute-start.26
  538.9 1.8 collective-permute-start.27
  (29 other events, 18.8 us)
where the time goes:
time: 548 us; the launch traced here: 543 us
  local copies, waits for them, and re-layouts  243 us (44%)
  other arithmetic  145 us (26%)
  matrix products  83.8 us (15%)
  starting transfers between devices  44.7 us (8%)
  loops' own time  13.6 us (2%)
  waiting for transfers between devices  11.1 us (2%)
    gather x48, local copies, waits for them, and re-layouts, one_column(): flat_z[other_index]  58.5 us
    gather x40, local copies, waits for them, and re-layouts, one_column(): flat_x[other_index] + move_x  57.8 us
    gather x40, local copies, waits for them, and re-layouts, one_column(): flat_y[other_index] + move_y  57.8 us
    ppermute x14, starting transfers between devices, extended(): after = lax.ppermute(initial, axis, down)  33.9 us
    scatter-add x8, other arithmetic, one_column(): flat_z[other_index]  32.7 us
    scatter-add x8, other arithmetic, one_column(): flat_x[other_index] + move_x  32.7 us
    scatter-add x8, other arithmetic, one_column(): flat_y[other_index] + move_y  32.7 us
    scatter-add x8, other arithmetic, one_column(): flat_feat[other_index]  26.9 us
  transfers between devices with their start and end apart: 28, of which 9 were waited for; matrix products, arithmetic and copies ran while one was open for 2% of the time, Pallas kernels for 0%

commit v1 on v0

v1 whole, which is shorter than its diff:
```python
import functools

import jax
import jax.numpy as jnp
from jax import lax
from jax.experimental import pallas as pl
from jax.experimental.pallas import tpu as pltpu
from jax.sharding import PartitionSpec as P

column = 6.0
cutoff = 6.0
softening = 0.01
root_three = 3.0**0.5
f32 = jnp.float32
bf16 = jnp.bfloat16
dead_code = 255
code_lane = 32


def mm(a, b):
    return lax.dot_general(a, b, (((1,), (0,)), ((), ())), preferred_element_type=f32)


def nt(a, b):
    return lax.dot_general(a, b, (((1,), (1,)), ((), ())), preferred_element_type=f32)


def split(x):
    high = x.astype(bf16)
    return high, (x - high.astype(f32)).astype(bf16)


def three(product, a, b):
    a_high, a_low = split(a)
    b_high, b_low = split(b)
    return product(a_high, b_high) + product(a_low, b_high) + product(a_high, b_low)


def widened_in(weight):
    high, low = split(weight)
    high, low = high.astype(f32), low.astype(f32)
    stacked = jnp.concatenate([high, high, low, jnp.zeros_like(high)], axis=0)
    return stacked.T.astype(bf16)


def widened_out(weight):
    high, low = split(weight)
    high, low = high.astype(f32), low.astype(f32)
    stacked = jnp.concatenate([high, high, low], axis=0)
    return stacked.T.astype(bf16)


def atom_mask(slots, edges, neigh):
    lane = lax.broadcasted_iota(jnp.int32, (slots, edges), 1)
    row = lax.broadcasted_iota(jnp.int32, (slots, edges), 0)
    return (lane // neigh == row).astype(f32)


def harmonic_rows(ux, uy, uz):
    square = ux * ux + uy * uy + uz * uz
    return [
        jnp.ones_like(ux),
        ux,
        uy,
        uz,
        root_three * ux * uy,
        root_three * uy * uz,
        0.5 * (3.0 * uz * uz - square),
        root_three * ux * uz,
        0.5 * root_three * (ux * ux - uy * uy),
    ]


class Sizes:
    def __init__(self, cols_x, cols_y, slots, neigh, channels, basis, hidden):
        self.cols_x, self.cols_y = cols_x, cols_y
        self.slots, self.neigh, self.channels = slots, neigh, channels
        self.basis, self.hidden = basis, hidden
        self.inner_x, self.inner_y = cols_x + 2, cols_y + 2
        self.outer_y = cols_y + 4
        self.inner = self.inner_x * self.inner_y
        self.edges = slots * neigh
        self.window = 9 * slots

    def place(self, col):
        return lax.div(col, jnp.int32(self.inner_y)), lax.rem(col, jnp.int32(self.inner_y))

    def outer_row(self, a, b):
        return pl.multiple_of((a * self.outer_y + b) * self.slots, self.slots)

    def inner_row(self, a, b):
        return pl.multiple_of((a * self.inner_y + b) * self.slots, self.slots)


def loop(count, body, unroll):
    def step(i, carry):
        body(i)
        return carry

    lax.fori_loop(0, count, step, 0, unroll=unroll)


def gather_columns(sz, table, mask, mask_bf, code, sep, hot, xt):
    lane = lax.broadcasted_iota(jnp.int32, (sz.channels, sz.edges), 1)
    row = lax.broadcasted_iota(jnp.int32, (sz.channels, sz.edges), 0)
    spread = (row == code_lane + lane % sz.neigh).astype(bf16)
    target = lax.broadcasted_iota(jnp.int32, (sz.window, sz.edges), 0)
    ch, run = sz.channels, 3 * sz.slots

    def body(col):
        a, b = sz.place(col)
        meta = table[pl.ds(sz.outer_row(a + 1, b + 1), sz.slots), ch : 2 * ch]
        codes = jnp.sum(mm(meta, spread) * mask, axis=0, keepdims=True).astype(jnp.int32)
        code[pl.ds(col, 1), :] = codes
        one_hot = (target == codes).astype(f32).astype(bf16)
        hot[col] = one_hot
        own = mm(meta.astype(f32).T[:24].astype(bf16), mask_bf)
        window = jnp.concatenate(
            [table[pl.ds(sz.outer_row(a + d, b), run), :] for d in range(3)], axis=0
        )
        turned = window.astype(f32).T.astype(bf16)[: ch + 32]
        found = mm(turned, one_hot)
        xt[col] = found[:ch]
        diff = found[ch : ch + 24] - own
        total = diff[0:8] + diff[8:16] + diff[16:24]
        for d in range(3):
            sep[d, pl.ds(col, 1), :] = total[d : d + 1]

    loop(sz.inner, body, 4)


def geometry(code, sep, angular, dist, env):
    offset = code[...] >> 4
    step_x = (offset * 11) >> 5
    step_y = offset - 3 * step_x
    live = (code[...] != dead_code).astype(f32)
    sep_x = sep[0] + column * (step_x - 1).astype(f32)
    sep_y = sep[1] + column * (step_y - 1).astype(f32)
    sep_z = sep[2]
    sep[0] = sep_x
    sep[1] = sep_y
    dist_sq = sep_x * sep_x + sep_y * sep_y + sep_z * sep_z
    dist[...] = jnp.sqrt(dist_sq + softening)
    env[...] = jnp.square(jnp.maximum(1.0 - dist_sq / (cutoff * cutoff), 0.0)) * live
    rows = harmonic_rows(sep_x / cutoff, sep_y / cutoff, sep_z / cutoff)
    for m, value in enumerate(rows):
        angular[m] = value


def basis_rows(sz, dist_row):
    spacing = cutoff / (sz.basis - 1)
    centre = lax.broadcasted_iota(jnp.int32, (sz.basis, sz.edges), 0).astype(f32) * spacing
    shifted = (dist_row - centre) / spacing
    return jnp.exp(-shifted * shifted), shifted


def hidden_rows(sz, dist_row, env_row, weight_in):
    basis, _ = basis_rows(sz, dist_row)
    high = basis.astype(bf16).astype(f32)
    stacked = jnp.concatenate([high, basis - high, high, jnp.zeros_like(high)], axis=0)
    pre = mm(weight_in, stacked.astype(bf16))
    gate = 1.0 / (1.0 + jnp.exp(-pre))
    value = pre * gate
    weighted = value * env_row
    high, low = split(weighted)
    return jnp.concatenate([high, low, high], axis=0), value, gate * (1.0 + pre * (1.0 - gate))


def harmonic_blocks(sz, angular, col, mask):
    rows = [angular[m, pl.ds(col, 1), :] * mask for m in range(9)]
    return jnp.concatenate(rows, axis=0)


def messages(sz, blocks, radial, xt):
    ch, n = sz.channels, sz.slots
    high, low = split(blocks)
    out = []
    for l, (first, last) in enumerate(((0, 1), (1, 4), (4, 9))):
        product = (radial[l * ch : (l + 1) * ch] * xt).astype(bf16)
        both = jnp.concatenate(
            [high[first * n : last * n], low[first * n : last * n]], axis=0
        )
        got = nt(both, product)
        rows = (last - first) * n
        out.append(got[:rows] + got[rows:])
    return out


def invariants(sz, parts):
    n = sz.slots
    scalar, vector, tensor = parts
    squares = vector * vector
    second = squares[:n] + squares[n : 2 * n] + squares[2 * n :]
    squares = tensor * tensor
    third = squares[:n]
    for m in range(1, 5):
        third = third + squares[m * n : (m + 1) * n]
    return jnp.concatenate([scalar, second, third], axis=1)


def layer_forward(sz, col, angular, dist, env, mask, weight_in, weight_out, xt):
    dist_row, env_row = dist[pl.ds(col, 1), :], env[pl.ds(col, 1), :]
    weighted, _, _ = hidden_rows(sz, dist_row, env_row, weight_in)
    radial = mm(weight_out, weighted)
    return messages(sz, harmonic_blocks(sz, angular, col, mask), radial, xt)


def layer_backward(
    sz, col, angular, dist, env, mask, weight_in, weight_out, back_in, back_out, xt, one_hot,
    message, cotangent, ang_grad, dist_grad, env_grad,
):
    ch, n = sz.channels, sz.slots
    dist_row, env_row = dist[pl.ds(col, 1), :], env[pl.ds(col, 1), :]
    weighted, value, slope = hidden_rows(sz, dist_row, env_row, weight_in)
    radial = mm(weight_out, weighted)
    blocks = harmonic_blocks(sz, angular, col, mask).astype(bf16)
    scalar_cot = cotangent[:, :ch]
    vector_cot = 2.0 * cotangent[:, ch : 2 * ch]
    tensor_cot = 2.0 * cotangent[:, 2 * ch :]
    grads = [scalar_cot]
    grads += [message[m * n : (m + 1) * n] * vector_cot for m in range(1, 4)]
    grads += [message[m * n : (m + 1) * n] * tensor_cot for m in range(4, 9)]
    message_grad = jnp.concatenate(grads, axis=0)
    turned = message_grad.T
    grad_bf = message_grad.astype(bf16)
    lane = lax.broadcasted_iota(jnp.int32, turned.shape, 1)
    row_grads = []
    radial_grads = []
    input_grad = None
    for l, (first, last) in enumerate(((0, 1), (1, 4), (4, 9))):
        mine = jnp.where((lane >= first * n) & (lane < last * n), turned, 0.0).astype(bf16)
        product_grad = mm(mine, blocks)
        part = radial[l * ch : (l + 1) * ch]
        product = (part * xt).astype(bf16)
        row_grads.append(mm(grad_bf[first * n : last * n], product))
        radial_grads.append((product_grad * xt).astype(bf16))
        term = product_grad * part
        input_grad = term if input_grad is None else input_grad + term
    for l, (first, last) in enumerate(((0, 1), (1, 4), (4, 9))):
        for m in range(first, last):
            if m:
                got = row_grads[l][(m - first) * n : (m - first + 1) * n] * mask
                ang_grad[m, pl.ds(col, 1), :] = jnp.sum(got, axis=0, keepdims=True)
    both = mm(back_out, jnp.concatenate(radial_grads, axis=0))
    weighted_grad = both[: sz.hidden] + both[sz.hidden :]
    env_grad[pl.ds(col, 1), :] = jnp.sum(weighted_grad * value, axis=0, keepdims=True)
    pre_grad = (weighted_grad * env_row * slope).astype(bf16)
    both = mm(back_in, pre_grad)
    basis_grad = both[: sz.basis] + both[sz.basis : 2 * sz.basis]
    basis, shifted = basis_rows(sz, dist_row)
    spacing = cutoff / (sz.basis - 1)
    dist_grad[pl.ds(col, 1), :] = jnp.sum(
        basis_grad * basis * shifted * (-2.0 / spacing), axis=0, keepdims=True
    )
    return nt(one_hot, input_grad.astype(bf16))


def separation_grads(code, sep, dist, ang_grad, dist_grad, env_grad):
    sep_x, sep_y, sep_z = sep
    live = (code != dead_code).astype(f32)
    ux, uy, uz = sep_x / cutoff, sep_y / cutoff, sep_z / cutoff
    dist_sq = sep_x * sep_x + sep_y * sep_y + sep_z * sep_z
    inside = jnp.maximum(1.0 - dist_sq / (cutoff * cutoff), 0.0)
    sq_grad = dist_grad * (0.5 / dist) - env_grad * live * inside * (2.0 / (cutoff * cutoff))
    g = ang_grad
    r3 = root_three
    grad_x = g[1] + r3 * (uy * g[4] + uz * g[7] + ux * g[8]) - ux * g[6]
    grad_y = g[2] + r3 * (ux * g[4] + uz * g[5] - uy * g[8]) - uy * g[6]
    grad_z = g[3] + r3 * (uy * g[5] + ux * g[7]) + 2.0 * uz * g[6]
    return (
        2.0 * sep_x * sq_grad + grad_x / cutoff,
        2.0 * sep_y * sq_grad + grad_y / cutoff,
        2.0 * sep_z * sq_grad + grad_z / cutoff,
    )


def stacked_seps(sz, sep_grad, col):
    rows = [sep_grad[d, pl.ds(col, 1), :] for d in range(3)]
    full = jnp.concatenate(rows + [jnp.zeros((5, sz.edges), f32)], axis=0)
    high = full.astype(bf16).astype(f32)
    return jnp.concatenate([high, full - high], axis=0).astype(bf16)


def signed_hot(sz, one_hot, mask_bf):
    first = 4 * sz.slots
    return jnp.concatenate(
        [one_hot[:first], one_hot[first : first + sz.slots] - mask_bf, one_hot[first + sz.slots :]],
        axis=0,
    )


def stacked_back(weight):
    high, low = split(weight)
    return jnp.concatenate([high, low], axis=0)


def first_kernel(
    sz, table, radial_in, radial_out, mixing, readout,
    energy, back, kept,
    code, sep, hot, xt, angular, dist, env, inv, second, second_hot, second_xt, second_msg,
    ang_grad, dist_grad, env_grad, sep_grad, acc, acc_pos,
):
    ch, n = sz.channels, sz.slots
    run = 3 * n
    mask = atom_mask(n, sz.edges, sz.neigh)
    mask_bf = mask.astype(bf16)
    gather_columns(sz, table, mask, mask_bf, code, sep, hot, xt)
    geometry(code, sep, angular, dist, env)
    in_one, out_one = widened_in(radial_in[0]), widened_out(radial_out[0])

    def one(col):
        parts = layer_forward(
            sz, col, angular, dist, env, mask, in_one, out_one, xt[col]
        )
        kept[col] = jnp.concatenate(parts, axis=0)
        inv[pl.ds(pl.multiple_of(col * n, n), n), :] = invariants(sz, parts)

    loop(sz.inner, one, 2)
    own_rows = [
        table[(a * sz.outer_y + 1) * n : (a * sz.outer_y + 1 + sz.inner_y) * n, :ch]
        for a in range(1, 1 + sz.inner_x)
    ]
    first_out = three(mm, inv[...], mixing[0]) + jnp.concatenate(own_rows, axis=0).astype(f32)
    second[...] = first_out.astype(bf16)

    in_two, out_two = widened_in(radial_in[1]), widened_out(radial_out[1])
    back_in, back_out = stacked_back(radial_in[1]), stacked_back(radial_out[1])
    target = lax.broadcasted_iota(jnp.int32, (sz.window, sz.edges), 0)

    def spot(k):
        a = lax.div(k, jnp.int32(sz.cols_y)) + 1
        b = lax.rem(k, jnp.int32(sz.cols_y)) + 1
        return a, b, a * sz.inner_y + b

    owned = sz.cols_x * sz.cols_y

    def two(k):
        a, b, col = spot(k)
        window = jnp.concatenate(
            [second[pl.ds(sz.inner_row(a - 1 + d, b - 1), run), :] for d in range(3)], axis=0
        )
        turned = window.astype(f32).T.astype(bf16)
        found = mm(turned, hot[col])
        second_xt[k] = found
        parts = layer_forward(sz, col, angular, dist, env, mask, in_two, out_two, found)
        second_msg[k] = jnp.concatenate(parts, axis=0)
        inv[pl.ds(pl.multiple_of(k * n, n), n), :] = invariants(sz, parts)

    loop(owned, two, 2)
    own_rows = [
        second[(a * sz.inner_y + 1) * n : (a * sz.inner_y + 1 + sz.cols_y) * n, :]
        for a in range(1, 1 + sz.cols_x)
    ]
    out = three(mm, inv[: owned * n], mixing[1]) + jnp.concatenate(own_rows, axis=0).astype(f32)
    gate = 1.0 / (1.0 + jnp.exp(-out))
    weights = readout[...]
    energy[...] = three(nt, jnp.ones((8, ch), f32), out * gate * weights)
    out_grad = gate * (1.0 + out * (1.0 - gate)) * weights
    inv[: owned * n] = three(nt, out_grad, mixing[1])
    acc[...] = jnp.zeros_like(acc)
    acc_pos[...] = jnp.zeros_like(acc_pos)
    for a in range(sz.cols_x):
        first = ((a + 1) * sz.inner_y + 1) * n
        acc[first : first + sz.cols_y * n] = out_grad[a * sz.cols_y * n : (a + 1) * sz.cols_y * n]

    def two_back(k):
        a, b, col = spot(k)
        got = layer_backward(
            sz, col, angular, dist, env, mask, in_two, out_two, back_in, back_out,
            second_xt[k], hot[col], second_msg[k],
            inv[pl.ds(pl.multiple_of(k * n, n), n), :], ang_grad, dist_grad, env_grad,
        )
        for d in range(3):
            acc[pl.ds(sz.inner_row(a - 1 + d, b - 1), run), :] += got[d * run : (d + 1) * run]

    loop(owned, two_back, 2)
    grads = separation_grads(
        code[...], (sep[0], sep[1], sep[2]), dist[...], ang_grad, dist_grad[...], env_grad[...]
    )
    for d in range(3):
        sep_grad[d] = grads[d]

    def two_pos(k):
        a, b, col = spot(k)
        got = nt(signed_hot(sz, hot[col], mask_bf), stacked_seps(sz, sep_grad, col))
        got = got[:, :8] + got[:, 8:]
        for d in range(3):
            acc_pos[pl.ds(sz.inner_row(a - 1 + d, b - 1), run), :] += got[d * run : (d + 1) * run]

    loop(owned, two_pos, 4)
    back[:, :ch] = acc[...].astype(bf16)
    high = acc_pos[...].astype(bf16)
    low = (acc_pos[...] - high.astype(f32)).astype(f32)
    filler = jnp.zeros((acc_pos.shape[0], ch - 16), f32)
    back[:, ch:] = jnp.concatenate([high.astype(f32), low, filler], axis=1).astype(bf16)


def second_kernel(
    sz, table, cotangent, kept, radial_in, radial_out, mixing,
    feature_grad, forces,
    code, sep, hot, xt, angular, dist, env, inv,
    ang_grad, dist_grad, env_grad, sep_grad, acc, acc_pos,
):
    ch, n = sz.channels, sz.slots
    run = 3 * n
    mask = atom_mask(n, sz.edges, sz.neigh)
    mask_bf = mask.astype(bf16)
    gather_columns(sz, table, mask, mask_bf, code, sep, hot, xt)
    geometry(code, sep, angular, dist, env)
    in_one, out_one = widened_in(radial_in[0]), widened_out(radial_out[0])
    back_in, back_out = stacked_back(radial_in[0]), stacked_back(radial_out[0])
    inv[...] = three(nt, cotangent[:, :ch], mixing[0])
    acc[...] = jnp.zeros_like(acc)
    acc_pos[...] = jnp.zeros_like(acc_pos)

    def one_back(col):
        a, b = sz.place(col)
        got = layer_backward(
            sz, col, angular, dist, env, mask, in_one, out_one, back_in, back_out,
            xt[col], hot[col], kept[col],
            inv[pl.ds(pl.multiple_of(col * n, n), n), :], ang_grad, dist_grad, env_grad,
        )
        for d in range(3):
            acc[pl.ds(sz.outer_row(a + d, b), run), :] += got[d * run : (d + 1) * run]

    loop(sz.inner, one_back, 2)
    grads = separation_grads(
        code[...], (sep[0], sep[1], sep[2]), dist[...], ang_grad, dist_grad[...], env_grad[...]
    )
    for d in range(3):
        sep_grad[d] = grads[d]

    def one_pos(col):
        a, b = sz.place(col)
        got = nt(signed_hot(sz, hot[col], mask_bf), stacked_seps(sz, sep_grad, col))
        got = got[:, :8] + got[:, 8:]
        for d in range(3):
            acc_pos[pl.ds(sz.outer_row(a + d, b), run), :] += got[d * run : (d + 1) * run]

    loop(sz.inner, one_pos, 4)
    for a in range(sz.cols_x):
        outer = ((a + 2) * sz.outer_y + 2) * n
        inner = ((a + 1) * sz.inner_y + 1) * n
        rows = sz.cols_y * n
        feature_grad[a * rows : (a + 1) * rows] = (
            acc[outer : outer + rows] + cotangent[inner : inner + rows, :ch]
        )
        extra = cotangent[inner : inner + rows, ch : ch + 16]
        total = acc_pos[outer : outer + rows] + extra[:, :8] + extra[:, 8:]
        for b in range(sz.cols_y):
            forces[a * sz.cols_y + b] = -(total[b * n : (b + 1) * n].T)[:3]


def ring(axis):
    devices = lax.axis_size(axis)
    up = [(i, (i + 1) % devices) for i in range(devices)]
    return up, [(j, i) for i, j in up]


def extended(x, sides):
    for axis, dim in sides:
        up, down = ring(axis)
        length = x.shape[dim]
        last = lax.slice_in_dim(x, length - 2, length, axis=dim)
        initial = lax.slice_in_dim(x, 0, 2, axis=dim)
        before = lax.ppermute(last, axis, up)
        after = lax.ppermute(initial, axis, down)
        x = jnp.concatenate([before, x, after], axis=dim)
    return x


def summed(x, sides):
    total = x.astype(f32)
    for axis, dim in sides:
        up, down = ring(axis)
        length = x.shape[dim]
        sent = total.astype(bf16)
        last = lax.slice_in_dim(sent, length - 2, length, axis=dim)
        initial = lax.slice_in_dim(sent, 0, 2, axis=dim)
        before = lax.ppermute(last, axis, up).astype(f32)
        after = lax.ppermute(initial, axis, down).astype(f32)
        shape = list(x.shape)
        shape[dim] = length - 4
        parts = [before] + ([jnp.zeros(shape, f32)] if length > 4 else []) + [after]
        total = total + jnp.concatenate(parts, axis=dim)
    return total


def rounded(x):
    return lax.reduce_precision(x, 8, 7)


def shards(
    features, positions, species, neighbours, counts, species_gain, radial_in, radial_out, mixing, readout
):
    cols_x, cols_y, slots, channels = features.shape
    neigh = neighbours.shape[-1]
    kinds = species_gain.shape[0]
    basis, hidden = radial_in.shape[1:]
    sz = Sizes(cols_x, cols_y, slots, neigh, channels, basis, hidden)
    gain = jnp.zeros(features.shape, f32)
    for kind in range(kinds):
        gain = jnp.where((species == kind)[..., None], species_gain[kind], gain)
    layer_one = (features.astype(f32) * gain).astype(bf16)
    live = jnp.arange(neigh, dtype=jnp.int32) < counts[..., None]
    codes = jnp.where(live, neighbours, dead_code).astype(bf16)
    atoms = positions.transpose(0, 1, 3, 2)
    high = rounded(atoms)
    middle = rounded(atoms - high)
    low = atoms - high - middle
    gap = jnp.zeros(atoms.shape[:-1] + (5,), bf16)
    tail = jnp.zeros(atoms.shape[:-1] + (channels - code_lane - neigh,), bf16)
    block = jnp.concatenate(
        [
            layer_one,
            high.astype(bf16), gap, middle.astype(bf16), gap, low.astype(bf16), gap,
            jnp.zeros(atoms.shape[:-1] + (code_lane - 24,), bf16),
            codes,
            tail,
        ],
        axis=-1,
    )
    sides = (("gx", 0), ("gy", 1))
    table = extended(block, sides).reshape(-1, 2 * channels)

    inner_atoms = sz.inner * slots
    owned = cols_x * cols_y
    edges = sz.edges
    shared = [
        pltpu.VMEM((sz.inner, edges), jnp.int32),
        pltpu.VMEM((3, sz.inner, edges), f32),
        pltpu.VMEM((sz.inner, sz.window, edges), bf16),
        pltpu.VMEM((sz.inner, channels, edges), f32),
        pltpu.VMEM((9, sz.inner, edges), f32),
        pltpu.VMEM((sz.inner, edges), f32),
        pltpu.VMEM((sz.inner, edges), f32),
        pltpu.VMEM((inner_atoms, 3 * channels), f32),
    ]
    grads = [
        pltpu.VMEM((9, sz.inner, edges), f32),
        pltpu.VMEM((sz.inner, edges), f32),
        pltpu.VMEM((sz.inner, edges), f32),
        pltpu.VMEM((3, sz.inner, edges), f32),
    ]
    vmem = pl.BlockSpec(memory_space=pltpu.VMEM)
    params = pltpu.CompilerParams(vmem_limit_bytes=48 * 1024 * 1024)
    energy, back, kept = pl.pallas_call(
        functools.partial(first_kernel, sz),
        out_shape=(
            jax.ShapeDtypeStruct((8, owned * slots), f32),
            jax.ShapeDtypeStruct((inner_atoms, 2 * channels), bf16),
            jax.ShapeDtypeStruct((sz.inner, sz.window, channels), f32),
        ),
        in_specs=[vmem] * 5,
        out_specs=(vmem,) * 3,
        scratch_shapes=shared
        + [
            pltpu.VMEM((inner_atoms, channels), bf16),
            pltpu.VMEM((1, 8, 128), f32),
            pltpu.VMEM((owned, channels, edges), f32),
            pltpu.VMEM((owned, sz.window, channels), f32),
        ]
        + grads
        + [pltpu.VMEM((inner_atoms, channels), f32), pltpu.VMEM((inner_atoms, 8), f32)],
        compiler_params=params,
        name="forward_and_second_back",
    )(table, radial_in, radial_out, mixing, readout.reshape(1, -1))

    back = back.reshape(sz.inner_x, sz.inner_y, slots, 2 * channels)
    cotangent = summed(back, sides).reshape(inner_atoms, 2 * channels)
    outer_atoms = table.shape[0]
    feature_grad, forces = pl.pallas_call(
        functools.partial(second_kernel, sz),
        out_shape=(
            jax.ShapeDtypeStruct((owned * slots, channels), f32),
            jax.ShapeDtypeStruct((owned, 3, slots), f32),
        ),
        in_specs=[vmem] * 6,
        out_specs=(vmem,) * 2,
        scratch_shapes=shared
        + grads
        + [pltpu.VMEM((outer_atoms, channels), f32), pltpu.VMEM((outer_atoms, 8), f32)],
        compiler_params=params,
        name="first_back",
    )(table, cotangent, kept, radial_in, radial_out, mixing)
    return (
        energy[0].reshape(cols_x, cols_y, slots),
        forces.reshape(cols_x, cols_y, 3, slots),
        feature_grad.reshape(cols_x, cols_y, slots, channels),
    )


def solution(mesh):
    placed = (
        P("gx", "gy", None, None),
        P("gx", "gy", None, None),
        P("gx", "gy", None),
        P("gx", "gy", None, None),
        P("gx", "gy", None),
        P(),
        P(),
        P(),
        P(),
        P(),
    )
    return jax.shard_map(
        shards,
        mesh=mesh,
        in_specs=placed,
        out_specs=(P("gx", "gy", None), P("gx", "gy", None, None), P("gx", "gy", None, None)),
        check_vma=False,
    )
```

time: 548 us -> 77.2 us (0.14)
  local copies, waits for them, and re-layouts: 243 us -> 2.71 us
  other arithmetic: 145 us -> 3.23 us
  matrix products: 83.8 us -> 0 us
  Pallas kernels: 0 us -> 42 us
  starting transfers between devices: 44.7 us -> 10.4 us
  loops' own time: 13.6 us -> 0 us
  waiting for transfers between devices: 11.1 us -> 17.5 us
    gather x144 -> x0, local copies, waits for them, and re-layouts: 191 us -> none  [the longest x48 58.5 us: one_column(): flat_z[other_index]]
    scatter-add x52 -> x0, other arithmetic: 128 us -> none  [the longest x8 32.7 us: one_column(): flat_z[other_index]]
    dot_general x146 -> x0, matrix products: 83.8 us -> none  [the longest x24 20.7 us: layer_block(): jnp.einsum('bkn,nh->bkh', radial_basis, weight_in, precision=highest)]
    pallas_call x0 -> x2, Pallas kernels: none -> 42 us  [the longest x1 21.2 us: shards(): pl.pallas_call(functools.partial(second_kernel, sz), out_shape=(jax.Shape...]
    ppermute x14 -> x2, starting transfers between devices: 33.9 us -> 6.09 us  [extended(): after = lax.ppermute(initial, axis, down)]
    dynamic_update_slice x32 -> x0, local copies, waits for them, and re-layouts: 18.3 us -> none  [layer(): lax.map(jax.checkpoint(one_column), edge_lists + owned)]
    another operation x4 -> x0, loops' own time: 13.6 us -> none  [layer(): lax.map(jax.checkpoint(one_column), edge_lists + owned)]
    ppermute x14 -> x2, starting transfers between devices: 10.8 us -> 0.5 us  [extended(): before = lax.ppermute(last, axis, up)]
  transfers between devices with their start and end apart: 28 -> 8, of which waited for: 9 -> 7; matrix products, arithmetic and copies ran while one was open for 2% -> 1% of each run, Pallas kernels for 0% -> 0%
where the time goes in v1:
time: 77.2 us; the launch traced here: 76.7 us
  Pallas kernels  42 us (54%)
  waiting for transfers between devices  17.5 us (23%)
  starting transfers between devices  10.4 us (13%)
  other arithmetic  3.23 us (4%)
  local copies, waits for them, and re-layouts  2.71 us (4%)
  between operations  0.82 us (1%)
    pallas_call x1, Pallas kernels, shards(): pl.pallas_call(functools.partial(second_kernel, sz), out_shape=(jax.Shape...  21.2 us
    pallas_call x1, Pallas kernels, shards(): pl.pallas_call(functools.partial(first_kernel, sz), out_shape=(jax.ShapeD...  20.8 us
    ppermute x2, waiting for transfers between devices, extended(): before = lax.ppermute(last, axis, up)  7.94 us
    ppermute x2, starting transfers between devices, extended(): after = lax.ppermute(initial, axis, down)  6.09 us
    ppermute x2, waiting for transfers between devices, summed(): before = lax.ppermute(last, axis, up).astype(f32)  4.68 us
    ppermute x2, waiting for transfers between devices, extended(): after = lax.ppermute(initial, axis, down)  3.3 us
    ppermute x2, starting transfers between devices, summed(): before = lax.ppermute(last, axis, up).astype(f32)  2.07 us
    ppermute x2, starting transfers between devices, summed(): after = lax.ppermute(initial, axis, down).astype(f32)  1.79 us
  transfers between devices with their start and end apart: 8, of which 7 were waited for; matrix products, arithmetic and copies ran while one was open for 1% of the time, Pallas kernels for 0%

profile of v1, /device:TPU:0, one launch (start us, length us, event | category | flops | bytes accessed | tf_op | source)
XLA Modules:
  0.0 76.7 jit_solution(7567428963017655202)
XLA Ops:
  0.6 0.0 copy-start
  0.6 0.0 copy-start.1
  0.7 0.0 copy-start.2
  0.7 0.0 copy-start.3
  0.7 0.9 %slice_bitcast_fusion.5 = (f32[128]{0:T(128)S(1)}, f32[128]{0:T(128)S(1)}, f32[128]{0:T(128)S(1)}, f32[128]{0:T(128)S(1)}, f32[128]{0:T(128)S(1)}, /*index=5*/f32[128]{0:T(128)S(1)}) fusion(f32[6,128]{1,0:T(8,128)} %param.15), kind=kLoop, calls=%fused_computation.27 | loop fusion | bytes 6144 | tf_op jit(solution)/shard_map/squeeze | solution.py:503
  1.6 0.7 broadcast_compare_fusion.5
  2.3 0.7 fusion
  3.0 0.1 copy.15
  3.1 0.1 copy.14
  3.2 0.1 copy.13
  3.3 0.8 %select_convert_fusion = bf16[2,2,16,32]{3,2,1,0:T(8,128)(2,1)S(1)} fusion(s32[2,2,16,32]{3,2,1,0:T(8,128)} %param.13, s32[2,2,16]{2,1,0:T(2,128)} %param.14), kind=kLoop, calls=%fused_computation.7 | loop fusion | flops 6144 | bytes 12544 | tf_op jit(solution)/shard_map/convert_element_type | solution.py:506
  4.2 0.8 %multiply_convert_fusion = bf16[2,2,16,128]{3,2,1,0:T(8,128)(2,1)S(1)} fusion(bf16[2,2,16,128]{3,2,1,0:T(8,128)(2,1)} %param.10, f32[128]{0:T(128)S(1)} %get-tuple-element.27, f32[128]{0:T(128)S(1)} %get-tuple-element.28, f32[128]{0:T(128)S(1)} %get-tuple-element.24, f32[128]{0:T(128)S(1)} %get-tuple-element.25, f32[128]{0:T(128)S(1)} %get-tuple-element.26, ...), kind=kLoop, calls=%fused_computation.9 | loop fusion | flops 73728 | bytes 36224 | tf_op jit(solution)/shard_map/convert_element_type | solution.py:504
  5.1 0.1 concatenate.25
  5.2 6.0 %collective-permute-start.1 = (bf16[2,2,16,256]{3,2,1,0:T(8,128)(2,1)S(1)}, bf16[2,2,16,256]{3,2,1,0:T(8,128)(2,1)S(1)}, u32[]{:S(2)}, u32[]{:S(2)}) collective-permute-start(bf16[2,2,16,256]{3,2,1,0:T(8,128)(2,1)S(1)} %concatenate.25), channel_id=1, source_target_pairs={{4,0},{8,4},{12,8},{16,12},{20,16},{24,20},{28,24},{0,28},{5,1},{9... | collective-permute-start | bytes 98312 | tf_op jit(solution)/shard_map/ppermute | solution.py:467
  11.2 0.0 collective-permute-start
  11.2 1.6 %collective-permute-done.1 = bf16[2,2,16,256]{3,2,1,0:T(8,128)(2,1)S(1)} collective-permute-done((bf16[2,2,16,256]{3,2,1,0:T(8,128)(2,1)S(1)}, bf16[2,2,16,256]{3,2,1,0:T(8,128)(2,1)S(1)}, u32[]{:S(2)}, u32[]{:S(2)}) %collective-permute-start.1) | collective-permute-done | bytes 32800 | tf_op jit(solution)/shard_map/ppermute | solution.py:467
  12.8 5.0 %collective-permute-done = bf16[2,2,16,256]{3,2,1,0:T(8,128)(2,1)S(1)} collective-permute-done((bf16[2,2,16,256]{3,2,1,0:T(8,128)(2,1)S(1)}, bf16[2,2,16,256]{3,2,1,0:T(8,128)(2,1)S(1)}, u32[]{:S(2)}, u32[]{:S(2)}) %collective-permute-start) | collective-permute-done | bytes 32800 | tf_op jit(solution)/shard_map/ppermute | solution.py:466
  17.8 0.1 collective-permute-start.3
  17.9 0.5 collective-permute-start.2
  18.4 1.7 %collective-permute-done.3 = bf16[6,2,16,256]{3,2,1,0:T(8,128)(2,1)S(1)} collective-permute-done((bf16[6,2,16,256]{3,2,1,0:T(8,128)(2,1)S(1)}, bf16[6,2,16,256]{3,2,1,0:T(8,128)(2,1)S(1)}, u32[]{:S(2)}, u32[]{:S(2)}) %collective-permute-start.3) | collective-permute-done | bytes 98336 | tf_op jit(solution)/shard_map/ppermute | solution.py:467
  20.1 2.9 %collective-permute-done.2 = bf16[6,2,16,256]{3,2,1,0:T(8,128)(2,1)S(1)} collective-permute-done((bf16[6,2,16,256]{3,2,1,0:T(8,128)(2,1)S(1)}, bf16[6,2,16,256]{3,2,1,0:T(8,128)(2,1)S(1)}, u32[]{:S(2)}, u32[]{:S(2)}) %collective-permute-start.2) | collective-permute-done | bytes 98336 | tf_op jit(solution)/shard_map/ppermute | solution.py:466
  23.1 0.0 copy-done
  23.1 0.0 copy-done.1
  23.1 0.0 copy-done.2
  23.1 0.0 copy-done.3
  23.1 20.8 %forward_and_second_back.1 = (f32[8,64]{1,0:T(8,128)S(1)}, bf16[256,256]{1,0:T(8,128)(2,1)S(1)}, f32[16,144,128]{2,1,0:T(8,128)S(1)}) custom-call(bf16[576,256]{1,0:T(8,128)(2,1)S(1)} %bitcast.34, f32[2,8,64]{2,1,0:T(8,128)S(1)} %copy-done.2, f32[2,64,384]{2,1,0:T(8,128)S(1)} %copy-done.1, f32[2,384,128]{2,1,0:T(8,128)S(1)} %copy-done, f32[1,128]{1,0:T(1,128)S(1)} %bitcast.38), custom_call_target="tpu_custom_call" | custom-call | tf_op jit(solution)/shard_map/forward_and_second_back/pallas_call | solution.py:547
  43.9 0.1 collective-permute-start.5
  44.0 2.0 %collective-permute-start.4 = (bf16[2,4,16,256]{3,2,1,0:T(8,128)(2,1)S(1)}, bf16[2,4,16,256]{3,2,1,0:T(8,128)(2,1)S(1)}, u32[]{:S(2)}, u32[]{:S(2)}) collective-permute-start(bf16[2,4,16,256]{3,2,1,0:T(8,128)(2,1)S(1)} %bitcast.39), channel_id=1, source_target_pairs={{0,4},{4,8},{8,12},{12,16},{16,20},{20,24},{24,28},{28,0},{1,5},{5... | collective-permute-start | bytes 196616 | tf_op jit(solution)/shard_map/ppermute | solution.py:480
  46.0 0.7 reshape_squeeze.3
  46.7 1.6 %collective-permute-done.5 = bf16[2,4,16,256]{3,2,1,0:T(8,128)(2,1)S(1)} collective-permute-done((bf16[2,4,16,256]{3,2,1,0:T(8,128)(2,1)S(1)}, bf16[2,4,16,256]{3,2,1,0:T(8,128)(2,1)S(1)}, u32[]{:S(2)}, u32[]{:S(2)}) %collective-permute-start.5) | collective-permute-done | bytes 65568 | tf_op jit(solution)/shard_map/ppermute | solution.py:481
  48.2 2.8 %collective-permute-done.4 = bf16[2,4,16,256]{3,2,1,0:T(8,128)(2,1)S(1)} collective-permute-done((bf16[2,4,16,256]{3,2,1,0:T(8,128)(2,1)S(1)}, bf16[2,4,16,256]{3,2,1,0:T(8,128)(2,1)S(1)}, u32[]{:S(2)}, u32[]{:S(2)}) %collective-permute-start.4) | collective-permute-done | bytes 65568 | tf_op jit(solution)/shard_map/ppermute | solution.py:480
  51.1 0.1 collective-permute-start.6
  51.1 1.7 %collective-permute-start.7 = (bf16[4,2,16,256]{3,2,1,0:T(8,128)(2,1)S(1)}, bf16[4,2,16,256]{3,2,1,0:T(8,128)(2,1)S(1)}, u32[]{:S(2)}, u32[]{:S(2)}) collective-permute-start(bf16[4,2,16,256]{3,2,1,0:T(8,128)(2,1)S(1)} %get-tuple-element.17), channel_id=1, source_target_pairs={{1,0},{2,1},{3,2},{0,3},{5,4},{6,5},{7,6},{4,7},{9,8},{10,9},{11,1... | collective-permute-start | bytes 196616 | tf_op jit(solution)/shard_map/ppermute | solution.py:481
  52.9 1.9 %collective-permute-done.6 = bf16[4,2,16,256]{3,2,1,0:T(8,128)(2,1)S(1)} collective-permute-done((bf16[4,2,16,256]{3,2,1,0:T(8,128)(2,1)S(1)}, bf16[4,2,16,256]{3,2,1,0:T(8,128)(2,1)S(1)}, u32[]{:S(2)}, u32[]{:S(2)}) %collective-permute-start.6) | collective-permute-done | bytes 65568 | tf_op jit(solution)/shard_map/ppermute | solution.py:480
  54.8 0.0 collective-permute-done.7
  54.9 21.2 %first_back.1 = (f32[64,128]{1,0:T(8,128)}, f32[4,3,16]{2,1,0:T(4,128)S(1)}) custom-call(bf16[576,256]{1,0:T(8,128)(2,1)S(1)} %bitcast.35, f32[256,256]{1,0:T(8,128)S(1)} %convert_add_fusion.cotangent, f32[16,144,128]{2,1,0:T(8,128)S(1)} %get-tuple-element.10.kept, f32[2,8,64]{2,1,0:T(8,128)S(1)} %copy-done.2, f32[2,64,384]{2,1,0:T(8,128)S(1)} %copy-done.1, ...), custom_call_target="tpu_custom_call" | custom-call | tf_op jit(solution)/shard_map/first_back/pallas_call | solution.py:572
  76.1 0.6 copy.16
  (12 shorter events, 0.2 us)
Async XLA Ops:
  0.6 22.5 %copy-start = (f32[2,384,128]{2,1,0:T(8,128)S(1)}, f32[2,384,128]{2,1,0:T(8,128)}, u32[]{:S(2)}) copy-start(f32[2,384,128]{2,1,0:T(8,128)} %mixing.3) | copy-start | bytes 1179652
  0.6 22.5 %copy-start.1 = (f32[2,64,384]{2,1,0:T(8,128)S(1)}, f32[2,64,384]{2,1,0:T(8,128)}, u32[]{:S(2)}) copy-start(f32[2,64,384]{2,1,0:T(8,128)} %radial_out.3) | copy-start | bytes 589828
  0.7 22.5 %copy-start.2 = (f32[2,8,64]{2,1,0:T(8,128)S(1)}, f32[2,8,64]{2,1,0:T(8,128)}, u32[]{:S(2)}) copy-start(f32[2,8,64]{2,1,0:T(8,128)} %radial_in.3) | copy-start | bytes 12292
  0.7 22.5 %copy-start.3 = (f32[128]{0:T(128)S(1)}, f32[128]{0:T(128)}, u32[]{:S(2)}) copy-start(f32[128]{0:T(128)} %param.19) | copy-start | bytes 1540
  5.2 7.6 %collective-permute-start.1 = (bf16[2,2,16,256]{3,2,1,0:T(8,128)(2,1)S(1)}, bf16[2,2,16,256]{3,2,1,0:T(8,128)(2,1)S(1)}, u32[]{:S(2)}, u32[]{:S(2)}) collective-permute-start(bf16[2,2,16,256]{3,2,1,0:T(8,128)(2,1)S(1)} %concatenate.25), channel_id=1, source_target_pairs={{4,0},{8,4},{12,8},{16,12},{20,16},{24,20},{28,24},{0,28},{5,1},{9... | collective-permute-start | bytes 98312 | tf_op jit(solution)/shard_map/ppermute | solution.py:467
  11.2 6.6 %collective-permute-start = (bf16[2,2,16,256]{3,2,1,0:T(8,128)(2,1)S(1)}, bf16[2,2,16,256]{3,2,1,0:T(8,128)(2,1)S(1)}, u32[]{:S(2)}, u32[]{:S(2)}) collective-permute-start(bf16[2,2,16,256]{3,2,1,0:T(8,128)(2,1)S(1)} %concatenate.25), channel_id=1, source_target_pairs={{0,4},{4,8},{8,12},{12,16},{16,20},{20,24},{24,28},{28,0},{1,5},{5... | collective-permute-start | bytes 98312 | tf_op jit(solution)/shard_map/ppermute | solution.py:466
  17.8 2.3 %collective-permute-start.3 = (bf16[6,2,16,256]{3,2,1,0:T(8,128)(2,1)S(1)}, bf16[6,2,16,256]{3,2,1,0:T(8,128)(2,1)S(1)}, u32[]{:S(2)}, u32[]{:S(2)}) collective-permute-start(bf16[6,2,16,256]{3,2,1,0:T(8,128)(2,1)S(1)} %pad_maximum_fusion.2), channel_id=1, source_target_pairs={{1,0},{2,1},{3,2},{0,3},{5,4},{6,5},{7,6},{4,7},{9,8},{10,9},{11,1... | collective-permute-start | bytes 294920 | tf_op jit(solution)/shard_map/ppermute | solution.py:467
  17.9 5.1 %collective-permute-start.2 = (bf16[6,2,16,256]{3,2,1,0:T(8,128)(2,1)S(1)}, bf16[6,2,16,256]{3,2,1,0:T(8,128)(2,1)S(1)}, u32[]{:S(2)}, u32[]{:S(2)}) collective-permute-start(bf16[6,2,16,256]{3,2,1,0:T(8,128)(2,1)S(1)} %pad_maximum_fusion.2), channel_id=1, source_target_pairs={{0,1},{1,2},{2,3},{3,0},{4,5},{5,6},{6,7},{7,4},{8,9},{9,10},{10,1... | collective-permute-start | bytes 294920 | tf_op jit(solution)/shard_map/ppermute | solution.py:466
  43.9 4.3 %collective-permute-start.5 = (bf16[2,4,16,256]{3,2,1,0:T(8,128)(2,1)S(1)}, bf16[2,4,16,256]{3,2,1,0:T(8,128)(2,1)S(1)}, u32[]{:S(2)}, u32[]{:S(2)}) collective-permute-start(bf16[2,4,16,256]{3,2,1,0:T(8,128)(2,1)S(1)} %bitcast.40), channel_id=1, source_target_pairs={{4,0},{8,4},{12,8},{16,12},{20,16},{24,20},{28,24},{0,28},{5,1},{9... | collective-permute-start | bytes 196616 | tf_op jit(solution)/shard_map/ppermute | solution.py:481
  44.0 7.0 %collective-permute-start.4 = (bf16[2,4,16,256]{3,2,1,0:T(8,128)(2,1)S(1)}, bf16[2,4,16,256]{3,2,1,0:T(8,128)(2,1)S(1)}, u32[]{:S(2)}, u32[]{:S(2)}) collective-permute-start(bf16[2,4,16,256]{3,2,1,0:T(8,128)(2,1)S(1)} %bitcast.39), channel_id=1, source_target_pairs={{0,4},{4,8},{8,12},{12,16},{16,20},{20,24},{24,28},{28,0},{1,5},{5... | collective-permute-start | bytes 196616 | tf_op jit(solution)/shard_map/ppermute | solution.py:480
  51.1 3.7 %collective-permute-start.6 = (bf16[4,2,16,256]{3,2,1,0:T(8,128)(2,1)S(1)}, bf16[4,2,16,256]{3,2,1,0:T(8,128)(2,1)S(1)}, u32[]{:S(2)}, u32[]{:S(2)}) collective-permute-start(bf16[4,2,16,256]{3,2,1,0:T(8,128)(2,1)S(1)} %get-tuple-element.16), channel_id=1, source_target_pairs={{0,1},{1,2},{2,3},{3,0},{4,5},{5,6},{6,7},{7,4},{8,9},{9,10},{10,1... | collective-permute-start | bytes 196616 | tf_op jit(solution)/shard_map/ppermute | solution.py:480
  51.1 3.7 %collective-permute-start.7 = (bf16[4,2,16,256]{3,2,1,0:T(8,128)(2,1)S(1)}, bf16[4,2,16,256]{3,2,1,0:T(8,128)(2,1)S(1)}, u32[]{:S(2)}, u32[]{:S(2)}) collective-permute-start(bf16[4,2,16,256]{3,2,1,0:T(8,128)(2,1)S(1)} %get-tuple-element.17), channel_id=1, source_target_pairs={{1,0},{2,1},{3,2},{0,3},{5,4},{6,5},{7,6},{4,7},{9,8},{10,9},{11,1... | collective-permute-start | bytes 196616 | tf_op jit(solution)/shard_map/ppermute | solution.py:481

commit v2 on v1

v2 whole, which is shorter than its diff:
```python
import functools

import jax
import jax.numpy as jnp
from jax import lax
from jax.experimental import pallas as pl
from jax.experimental.pallas import tpu as pltpu
from jax.sharding import PartitionSpec as P

column = 6.0
cutoff = 6.0
softening = 0.01
root_three = 3.0**0.5
f32 = jnp.float32
bf16 = jnp.bfloat16
dead_code = 255
code_lane = 32
halo_lanes = 128


def mm(a, b):
    return lax.dot_general(a, b, (((1,), (0,)), ((), ())), preferred_element_type=f32)


def nt(a, b):
    return lax.dot_general(a, b, (((1,), (1,)), ((), ())), preferred_element_type=f32)


def split(x):
    high = x.astype(bf16)
    return high, (x - high.astype(f32)).astype(bf16)


def three(product, a, b):
    a_high, a_low = split(a)
    b_high, b_low = split(b) if b.dtype == f32 else (b[0], b[1])
    return product(a_high, b_high) + product(a_low, b_high) + product(a_high, b_low)


def parted(x):
    high = lax.reduce_precision(x, 8, 7)
    return high, x - high


def prepared(radial_in, radial_out, mixing):
    high, low = parted(radial_in)
    turned = jnp.concatenate([high, high, low, jnp.zeros_like(high)], axis=1).swapaxes(1, 2)
    back_in = jnp.concatenate([high, low], axis=1)
    high, low = parted(radial_out)
    wide = jnp.concatenate([high, high, low], axis=1).swapaxes(1, 2)
    high_mix, low_mix = parted(mixing)
    mix = jnp.stack([high_mix, low_mix], axis=1)
    return [x.astype(bf16) for x in (turned, wide, back_in, high, mix)]


def atom_mask(slots, edges, neigh):
    lane = lax.broadcasted_iota(jnp.int32, (slots, edges), 1)
    row = lax.broadcasted_iota(jnp.int32, (slots, edges), 0)
    return (lane // neigh == row).astype(f32)


def harmonic_rows(ux, uy, uz):
    square = ux * ux + uy * uy + uz * uz
    return [
        jnp.ones_like(ux),
        ux,
        uy,
        uz,
        root_three * ux * uy,
        root_three * uy * uz,
        0.5 * (3.0 * uz * uz - square),
        root_three * ux * uz,
        0.5 * root_three * (ux * ux - uy * uy),
    ]


class Sizes:
    def __init__(self, cols_x, cols_y, slots, neigh, channels, basis, hidden):
        self.cols_x, self.cols_y = cols_x, cols_y
        self.slots, self.neigh, self.channels = slots, neigh, channels
        self.basis, self.hidden = basis, hidden
        self.inner_x, self.inner_y = cols_x + 2, cols_y + 2
        self.outer_y = cols_y + 4
        self.inner = self.inner_x * self.inner_y
        self.edges = slots * neigh
        self.window = 9 * slots

        cells = [(a, b) for a in range(self.inner_x) for b in range(self.inner_y)]
        self.own = [c for c in cells if self.is_own(*c)]
        self.halo = [c for c in cells if not self.is_own(*c)]
        self.order = self.own + self.halo

    def is_own(self, a, b):
        return 1 <= a <= self.cols_x and 1 <= b <= self.cols_y

    def outer_row(self, a, b):
        return (a * self.outer_y + b) * self.slots

    def inner_row(self, a, b):
        return (a * self.inner_y + b) * self.slots


def each(compute):
    return lambda items: [compute(item) for item in items]


def loop(count, group, compute, store):
    for first in range(0, count, group):
        items = list(range(first, min(first + group, count)))
        for item, value in zip(items, compute(items)):
            store(item, value)


def window_of(sz, table, a, b):
    run = 3 * sz.slots
    return jnp.concatenate(
        [table[pl.ds(sz.outer_row(a + d, b), run), :] for d in range(3)], axis=0
    )


def gather_columns(sz, table, mask, mask_bf, code, sep, hot, xt):
    lane = lax.broadcasted_iota(jnp.int32, (sz.channels, sz.edges), 1)
    row = lax.broadcasted_iota(jnp.int32, (sz.channels, sz.edges), 0)
    spread = (row == code_lane + lane % sz.neigh).astype(bf16)
    target = lax.broadcasted_iota(jnp.int32, (sz.window, sz.edges), 0)
    ch = sz.channels

    def one(col):
        a, b = sz.order[col]
        meta = table[pl.ds(sz.outer_row(a + 1, b + 1), sz.slots), ch : 2 * ch]
        codes = jnp.sum(mm(meta, spread) * mask, axis=0, keepdims=True).astype(jnp.int32)
        one_hot = (target == codes).astype(f32).astype(bf16)
        own = mm(meta.astype(f32).T[:24].astype(bf16), mask_bf)
        window = window_of(sz, table, a, b)
        turned = window.astype(f32).T.astype(bf16)[: ch + 32]
        found = mm(turned, one_hot)
        diff = found[ch : ch + 24] - own
        return codes, one_hot, found[:ch], diff[0:8] + diff[8:16] + diff[16:24]

    def store(col, value):
        code[pl.ds(col, 1), :], one_hot, found, total = value
        if col < len(sz.own):
            hot[col] = one_hot
        xt[col] = found
        for d in range(3):
            sep[d, pl.ds(col, 1), :] = total[d : d + 1]

    loop(sz.inner, 4, each(one), store)


def shifted_seps(code, sep):
    offset = code[...] >> 4
    step_x = (offset * 11) >> 5
    step_y = offset - 3 * step_x
    sep[0] = sep[0] + column * (step_x - 1).astype(f32)
    sep[1] = sep[1] + column * (step_y - 1).astype(f32)


def geometry(live, seps, angular, dist, env):
    sep_x, sep_y, sep_z = seps
    dist_sq = sep_x * sep_x + sep_y * sep_y + sep_z * sep_z
    dist[...] = jnp.sqrt(dist_sq + softening)
    env[...] = jnp.square(jnp.maximum(1.0 - dist_sq / (cutoff * cutoff), 0.0)) * live
    rows = harmonic_rows(sep_x / cutoff, sep_y / cutoff, sep_z / cutoff)
    for m, value in enumerate(rows):
        angular[m] = value


def live_rows(code):
    return (code != dead_code).astype(f32)


def basis_rows(sz, dist_row):
    width = dist_row.shape[1]
    spacing = cutoff / (sz.basis - 1)
    centre = lax.broadcasted_iota(jnp.int32, (sz.basis, width), 0).astype(f32) * spacing
    shifted = (dist_row - centre) * (1.0 / spacing)
    return jnp.exp(-shifted * shifted), shifted


def sigmoid(x):
    return 0.5 * jnp.tanh(0.5 * x) + 0.5


def hidden_rows(sz, dist_row, env_row, weight_in):
    basis, _ = basis_rows(sz, dist_row)
    high = basis.astype(bf16).astype(f32)
    stacked = jnp.concatenate([high, basis - high, high, jnp.zeros_like(high)], axis=0)
    pre = mm(weight_in, stacked.astype(bf16))
    gate = sigmoid(pre)
    value = pre * gate
    weighted = value * env_row
    high, low = split(weighted)
    slope = gate * (1.0 + pre * (1.0 - gate)) * env_row
    return jnp.concatenate([high, low, high], axis=0), value, slope


def half_rows(sz, angular, col, half, first):
    edges = sz.edges // 2
    mask = atom_mask(sz.slots // 2, edges, sz.neigh)
    span = slice(half * edges, (half + 1) * edges)
    return [angular[m, pl.ds(col, 1), span] * mask for m in range(first, 9)]


def layer_forward(sz, cols, angular, dist, env, mask_bf, weight_in, weight_out, inputs):
    rows = [jnp.concatenate([ref[pl.ds(c, 1), :] for c in cols], axis=1) for ref in (dist, env)]
    weighted, value, slope = hidden_rows(sz, *rows, weight_in)
    out = []
    for k, (col, xt) in enumerate(zip(cols, inputs)):
        span = slice(k * sz.edges, (k + 1) * sz.edges)
        radial = mm(weight_out, weighted[:, span])
        parts = column_messages(sz, col, angular, mask_bf, radial, xt)
        kept = (weighted[: 2 * sz.hidden, span], value[:, span], slope[:, span])
        out.append((radial, kept, parts))
    return out


def column_messages(sz, col, angular, mask_bf, radial, xt):
    ch, edges = sz.channels, sz.edges // 2
    product = [(radial[l * ch : (l + 1) * ch] * xt).astype(bf16) for l in range(3)]
    scalar = nt(product[0], mask_bf).T
    count = 4 * sz.slots
    lane = lax.broadcasted_iota(jnp.int32, (ch, 2 * count), 1)
    vector_lane = lax.rem(lane, count) < 3 * sz.slots // 2
    out = [scalar]
    for half in range(2):
        span = slice(half * edges, (half + 1) * edges)
        blocks = jnp.concatenate(half_rows(sz, angular, col, half, 1), axis=0)
        high = blocks.astype(bf16).astype(f32)
        both = jnp.concatenate([high, blocks - high], axis=0).astype(bf16)
        got = jnp.where(vector_lane, nt(product[1][:, span], both), nt(product[2][:, span], both)).T
        out.append(got[:count] + got[count:])
    return out


def half_messages(sz, message, half):
    n = sz.slots // 2
    first = sz.slots + half * 8 * n
    return [message[first + m * n : first + (m + 1) * n] for m in range(8)]


def invariants(sz, parts):
    n = sz.slots // 2
    rows = []
    for half in range(2):
        squares = parts[1 + half] * parts[1 + half]
        got = [squares[m * n : (m + 1) * n] for m in range(8)]
        rows.append(
            jnp.concatenate(
                [
                    parts[0][half * n : (half + 1) * n],
                    got[0] + got[1] + got[2],
                    got[3] + got[4] + got[5] + got[6] + got[7],
                ],
                axis=1,
            )
        )
    return jnp.concatenate(rows, axis=0)


def radial_products(sz, product_grad, radial, xt):
    ch = sz.channels
    products, mine, input_grad = [], [], None
    for l in range(3):
        grad, part = product_grad[l * ch : (l + 1) * ch], radial[l * ch : (l + 1) * ch]
        if l:
            products.append((part * xt).astype(bf16))
        mine.append((grad * xt).astype(bf16))
        term = grad * part
        input_grad = term if input_grad is None else input_grad + term
    return products, jnp.concatenate(mine, axis=0), input_grad.astype(bf16)


def radial_backward(sz, dist_row, radial_grad, value, slope, back_in, back_out):
    weighted_grad = mm(back_out, radial_grad)
    env_row_grad = jnp.sum(weighted_grad * value, axis=0, keepdims=True)
    both = mm(back_in, (weighted_grad * slope).astype(bf16))
    basis_grad = both[: sz.basis] + both[sz.basis : 2 * sz.basis]
    basis, shifted = basis_rows(sz, dist_row)
    spacing = cutoff / (sz.basis - 1)
    dist_row_grad = jnp.sum(
        basis_grad * basis * shifted * (-2.0 / spacing), axis=0, keepdims=True
    )
    return dist_row_grad, env_row_grad


def layer_backward(
    sz, col, angular, dist, back_in, back_out, radial, value, slope, xt, one_hot,
    message, cotangent,
):
    ch, n, edges = sz.channels, sz.slots // 2, sz.edges // 2
    mask = atom_mask(n, edges, sz.neigh)
    input_grads, radial_grads, ang_grads = [], [], []
    for half in range(2):
        span = slice(half * edges, (half + 1) * edges)
        blocks = jnp.concatenate(half_rows(sz, angular, col, half, 0), axis=0).astype(bf16)
        cot = cotangent[half * n : (half + 1) * n]
        twice = 2.0 * cot[:, ch:]
        got = half_messages(sz, message, half)
        grads = [got[m] * (twice[:, :ch] if m < 3 else twice[:, ch:]) for m in range(8)]
        filler = jnp.zeros((ch - 9 * n, ch), f32)
        turned = jnp.concatenate([cot[:, :ch]] + grads + [filler], axis=0).T[:, : 9 * n]
        lane = lax.broadcasted_iota(jnp.int32, turned.shape, 1)
        lhs = jnp.concatenate(
            [
                jnp.where(lane < n, turned, 0.0),
                jnp.where((lane >= n) & (lane < 4 * n), turned, 0.0),
                jnp.where(lane >= 4 * n, turned, 0.0),
            ],
            axis=0,
        ).astype(bf16)
        product_grad = mm(lhs, blocks)
        products, mine, input_grad = radial_products(
            sz, product_grad, radial[:, span], xt[:, span]
        )
        input_grads.append(input_grad)
        radial_grads.append(mine)
        empty = jnp.zeros((n, ch), f32)
        wide = [
            jnp.concatenate([g, empty] if m < 3 else [empty, g], axis=1)
            for m, g in enumerate(grads)
        ]
        got = mm(jnp.concatenate(wide, axis=0).astype(bf16), jnp.concatenate(products, axis=0))
        ang_grads.append(
            [
                jnp.sum(got[m * n : (m + 1) * n] * mask, axis=0, keepdims=True)
                for m in range(8)
            ]
        )
    dist_row_grad, env_row_grad = radial_backward(
        sz, dist[pl.ds(col, 1), :], jnp.concatenate(radial_grads, axis=1),
        value, slope, back_in, back_out,
    )
    got = nt(one_hot, jnp.concatenate(input_grads, axis=1))
    return got, ang_grads, dist_row_grad, env_row_grad


def store_grads(sz, col, value, ang_grad, dist_grad, env_grad):
    got, ang_grads, dist_row_grad, env_row_grad = value
    edges = sz.edges // 2
    for half in range(2):
        for m in range(8):
            ang_grad[m + 1, pl.ds(col, 1), half * edges : (half + 1) * edges] = ang_grads[half][m]
    dist_grad[pl.ds(col, 1), :] = dist_row_grad
    env_grad[pl.ds(col, 1), :] = env_row_grad
    return got


def separation_grads(live, sep, dist, ang_grad, dist_grad, env_grad):
    sep_x, sep_y, sep_z = sep
    ux, uy, uz = sep_x / cutoff, sep_y / cutoff, sep_z / cutoff
    dist_sq = sep_x * sep_x + sep_y * sep_y + sep_z * sep_z
    inside = jnp.maximum(1.0 - dist_sq / (cutoff * cutoff), 0.0)
    sq_grad = dist_grad * (0.5 / dist) - env_grad * live * inside * (2.0 / (cutoff * cutoff))
    g = ang_grad
    r3 = root_three
    grad_x = g[1] + r3 * (uy * g[4] + uz * g[7] + ux * g[8]) - ux * g[6]
    grad_y = g[2] + r3 * (ux * g[4] + uz * g[5] - uy * g[8]) - uy * g[6]
    grad_z = g[3] + r3 * (uy * g[5] + ux * g[7]) + 2.0 * uz * g[6]
    return (
        2.0 * sep_x * sq_grad + grad_x / cutoff,
        2.0 * sep_y * sq_grad + grad_y / cutoff,
        2.0 * sep_z * sq_grad + grad_z / cutoff,
    )


def stacked_seps(rows):
    full = jnp.concatenate(rows + [jnp.zeros((5, rows[0].shape[1]), f32)], axis=0)
    high = full.astype(bf16).astype(f32)
    return jnp.concatenate([high, full - high], axis=0).astype(bf16)


def own_positions(
    sz, mask_bf, code, sep, dist, hot, ang_grad, dist_grad, env_grad, sep_grad, acc_pos
):
    owned, run = len(sz.own), 3 * sz.slots
    grads = separation_grads(
        live_rows(code[:owned]),
        [sep[d, :owned] for d in range(3)],
        dist[:owned],
        ang_grad,
        dist_grad[...],
        env_grad[...],
    )
    for d in range(3):
        sep_grad[d] = grads[d]
    for k, (a, b) in enumerate(sz.own):
        rows = [sep_grad[d, pl.ds(k, 1), :] for d in range(3)]
        got = nt(signed_hot(sz, hot[k], mask_bf), stacked_seps(rows))
        got = got[:, :8] + got[:, 8:]
        for d in range(3):
            acc_pos[pl.ds(sz.inner_row(a - 1 + d, b - 1), run), :] += got[d * run : (d + 1) * run]


def signed_hot(sz, one_hot, mask_bf):
    first = 4 * sz.slots
    return jnp.concatenate(
        [one_hot[:first], one_hot[first : first + sz.slots] - mask_bf, one_hot[first + sz.slots :]],
        axis=0,
    )


def fetch(sources, targets, sems):
    copies = [
        pltpu.make_async_copy(source, target, sems.at[k])
        for k, (source, target) in enumerate(zip(sources, targets))
    ]
    for copy in copies:
        copy.start()
    return copies


def block_kernel(sz, kinds, *refs):
    sources, block, held, sems = refs[:6], refs[6], refs[7:13], refs[13]
    for copy in fetch(sources, held, sems):
        copy.wait()
    features, positions, species, neighbours, counts, species_gain = held
    ch, n = sz.channels, sz.slots
    gains = species_gain[...]
    gain_high = gains.astype(bf16).astype(f32)
    rest = gains - gain_high
    gain_middle = rest.astype(bf16).astype(f32)
    parts = [gain_high, gain_middle, rest - gain_middle]
    above, below = jnp.zeros((24, ch), f32), jnp.zeros((8 - kinds, ch), f32)
    parts = [jnp.concatenate([above, part, below], axis=0).astype(bf16) for part in parts]
    kind = lax.broadcasted_iota(jnp.int32, (8, n), 0)
    neigh_lane = lax.broadcasted_iota(jnp.int32, (n, sz.neigh), 1)
    lane = lax.broadcasted_iota(jnp.int32, (n, code_lane), 1)
    gap = jnp.zeros((5, n), f32)
    for a in range(sz.cols_x):
        for b in range(sz.cols_y):
            atoms = positions[a, :, b, :]
            high = atoms.astype(bf16).astype(f32)
            rest = atoms - high
            middle = rest.astype(bf16).astype(f32)
            count = counts[a, pl.ds(b, 1), :]
            chosen = (kind == species[a, pl.ds(b, 1), :]).astype(f32)
            last = jnp.where(kind == 7, count.astype(f32), chosen)
            rows = [high, gap, middle, gap, rest - middle, gap, last]
            turned = jnp.concatenate(rows, axis=0).T
            picked = jnp.where((lane >= 24) & (lane < 24 + kinds), turned, 0.0).astype(bf16)
            gain = mm(picked, parts[0]) + mm(picked, parts[1]) + mm(picked, parts[2])
            live = neigh_lane.astype(f32) < turned[:, 31:32]
            codes = jnp.where(live, neighbours[a, b], dead_code).astype(f32)
            place = jnp.where(lane < 24, turned, 0.0)
            filler = jnp.zeros((n, ch - code_lane - sz.neigh), f32)
            block[a, b, :, :ch] = (features[a, b].astype(f32) * gain).astype(bf16)
            block[a, b, :, ch:] = jnp.concatenate([place, codes, filler], axis=1).astype(bf16)


def first_kernel(
    sz, table, wide_in, wide_out, turned_in, turned_out, mixing, readout,
    energy, back, kept, code, sep,
    hot, xt, angular, dist, env, inv, second, second_xt, second_msg, second_radial,
    second_value, second_slope, ang_grad, dist_grad, env_grad, sep_grad, acc, acc_pos,
):
    ch, n = sz.channels, sz.slots
    run = 3 * n
    owned = len(sz.own)
    mask = atom_mask(n, sz.edges, sz.neigh)
    mask_bf = mask.astype(bf16)
    gather_columns(sz, table, mask, mask_bf, code, sep, hot, xt)
    shifted_seps(code, sep)
    geometry(live_rows(code[...]), (sep[0], sep[1], sep[2]), angular, dist, env)
    in_one, out_one = wide_in[0], wide_out[0]

    def one(cols):
        inputs = [xt[col] for col in cols]
        return layer_forward(sz, cols, angular, dist, env, mask_bf, in_one, out_one, inputs)

    def one_store(col, got):
        _, _, parts = got
        kept[col] = jnp.concatenate(parts, axis=0)
        inv[sz.inner_row(*sz.order[col]) : sz.inner_row(*sz.order[col]) + n, :] = invariants(
            sz, parts
        )

    loop(sz.inner, 4, one, one_store)
    own_rows = [
        table[(a * sz.outer_y + 1) * n : (a * sz.outer_y + 1 + sz.inner_y) * n, :ch]
        for a in range(1, 1 + sz.inner_x)
    ]
    first_out = three(mm, inv[...], mixing[0]) + jnp.concatenate(own_rows, axis=0).astype(f32)
    second[...] = first_out.astype(bf16)

    in_two, out_two = wide_in[1], wide_out[1]
    back_in, back_out = turned_in[1], turned_out[1]

    def second_input(k):
        a, b = sz.own[k]
        window = jnp.concatenate(
            [second[pl.ds(sz.inner_row(a - 1 + d, b - 1), run), :] for d in range(3)], axis=0
        )
        return mm(window.astype(f32).T.astype(bf16), hot[k])

    def two(items):
        inputs = [second_input(k) for k in items]
        got = layer_forward(sz, items, angular, dist, env, mask_bf, in_two, out_two, inputs)
        return list(zip(inputs, got))

    def two_store(k, got):
        second_xt[k], (second_radial[k], hidden, parts) = got
        _, second_value[k], second_slope[k] = hidden
        second_msg[k] = jnp.concatenate(parts, axis=0)
        inv[k * n : (k + 1) * n, :] = invariants(sz, parts)

    loop(owned, 4, two, two_store)
    own_rows = [
        second[(a * sz.inner_y + 1) * n : (a * sz.inner_y + 1 + sz.cols_y) * n, :]
        for a in range(1, 1 + sz.cols_x)
    ]
    out = three(mm, inv[: owned * n], mixing[1]) + jnp.concatenate(own_rows, axis=0).astype(f32)
    gate = sigmoid(out)
    weights = readout[...]
    total = three(nt, jnp.ones((8, ch), f32), out * gate * weights)
    for k, (a, b) in enumerate(sz.own):
        energy[a - 1, b - 1 : b, :] = total[0:1, k * n : (k + 1) * n]
    out_grad = gate * (1.0 + out * (1.0 - gate)) * weights
    inv[: owned * n] = three(nt, out_grad, mixing[1])
    acc[...] = jnp.zeros_like(acc)
    acc_pos[...] = jnp.zeros_like(acc_pos)
    for a in range(sz.cols_x):
        first = ((a + 1) * sz.inner_y + 1) * n
        acc[first : first + sz.cols_y * n] = out_grad[a * sz.cols_y * n : (a + 1) * sz.cols_y * n]

    def two_back(k):
        return layer_backward(
            sz, k, angular, dist, back_in, back_out,
            second_radial[k], second_value[k], second_slope[k], second_xt[k], hot[k],
            second_msg[k], inv[k * n : (k + 1) * n, :],
        )

    def two_back_store(k, value):
        a, b = sz.own[k]
        got = store_grads(sz, k, value, ang_grad, dist_grad, env_grad)
        for d in range(3):
            acc[pl.ds(sz.inner_row(a - 1 + d, b - 1), run), :] += got[d * run : (d + 1) * run]

    loop(owned, 4, each(two_back), two_back_store)
    own_positions(
        sz, mask_bf, code, sep, dist, hot, ang_grad, dist_grad, env_grad, sep_grad, acc_pos
    )
    back[:, :ch] = acc[...].astype(bf16)
    high = acc_pos[...].astype(bf16)
    low = (acc_pos[...] - high.astype(f32)).astype(f32)
    filler = jnp.zeros((acc_pos.shape[0], ch - 16), f32)
    back[:, ch:] = jnp.concatenate([high.astype(f32), low, filler], axis=1).astype(bf16)


def packed_halo(sz, code):
    rows = len(sz.halo)
    first = len(sz.own)
    codes = code[first:]
    row = lax.broadcasted_iota(jnp.int32, (rows, sz.edges), 0)
    at_x, at_y = jnp.zeros_like(row), jnp.zeros_like(row)
    for h, (a, b) in enumerate(sz.halo):
        at_x, at_y = jnp.where(row == h, a, at_x), jnp.where(row == h, b, at_y)
    offset = codes >> 4
    step_x = (offset * 11) >> 5
    to_x = at_x + step_x - 2
    to_y = at_y + offset - 3 * step_x - 2
    inside = (to_x >= 0) & (to_x < sz.cols_x) & (to_y >= 0) & (to_y < sz.cols_y)
    inside = inside & (codes != dead_code)
    target = (to_x * sz.cols_y + to_y) * sz.slots + (codes & 15)
    target = jnp.where(inside, target, 0).astype(f32)
    lower = lax.broadcasted_iota(jnp.int32, (sz.edges, sz.edges), 0)
    upper = lax.broadcasted_iota(jnp.int32, (sz.edges, sz.edges), 1)
    running = mm(inside.astype(f32).astype(bf16), (lower <= upper).astype(f32).astype(bf16))
    place = jnp.where(inside, running - 1.0, -1.0)
    most = jnp.max(running).astype(jnp.int32)
    return target, place, (most + halo_lanes - 1) // halo_lanes


def halo_back(
    sz, part, table, cotangent, kept, sep, inv, weights,
    target, place, held, feature_acc, pos_acc,
):
    in_one, out_one, back_in, back_out = weights
    csep, ctarget, catom, cvalid, angular, dist, env, ang_grad, dist_grad, env_grad = held
    ch, n, lanes = sz.channels, sz.slots, halo_lanes
    first = len(sz.own)
    slot = lax.broadcasted_iota(jnp.int32, (lanes, sz.edges), 0).astype(f32)
    atom = (lax.broadcasted_iota(jnp.int32, (1, sz.edges), 1) // sz.neigh).astype(f32)
    ones = jnp.ones((1, sz.edges), f32)
    zeros = jnp.zeros((2, sz.edges), f32)
    wanted = slot + (part * lanes).astype(f32)
    for h in range(len(sz.halo)):
        pick = (place[h : h + 1] == wanted).astype(f32).astype(bf16)
        rows = jnp.concatenate(
            [sep[d, pl.ds(first + h, 1), :] for d in range(3)]
            + [target[h : h + 1], atom, ones, zeros],
            axis=0,
        )
        high = rows.astype(bf16).astype(f32)
        middle = (rows - high).astype(bf16).astype(f32)
        three_parts = jnp.concatenate([high, middle, rows - high - middle], axis=0).astype(bf16)
        got = nt(three_parts, pick)
        got = got[0:8] + got[8:16] + got[16:24]
        for d in range(3):
            csep[d, pl.ds(h, 1), :] = got[d : d + 1]
        ctarget[pl.ds(h, 1), :] = got[3:4]
        catom[pl.ds(h, 1), :] = got[4:5]
        cvalid[pl.ds(h, 1), :] = got[5:6]
    sep_x, sep_y, sep_z = csep[0], csep[1], csep[2]
    geometry(cvalid[...], (sep_x, sep_y, sep_z), angular, dist, env)
    own_rows = [
        table[sz.outer_row(a + 2, 2) : sz.outer_row(a + 2, 2) + sz.cols_y * n, :ch]
        for a in range(sz.cols_x)
    ]
    own_turned = jnp.concatenate(own_rows, axis=0).astype(f32).T.astype(bf16)
    own_index = lax.broadcasted_iota(jnp.int32, (len(sz.own) * n, 4 * lanes), 0).astype(f32)
    atom_index = lax.broadcasted_iota(jnp.int32, (n, lanes), 0).astype(f32)
    half = n // 2
    groups = [range(g, min(g + 4, len(sz.halo))) for g in range(0, len(sz.halo), 4)]

    def wide(ref, group):
        return jnp.concatenate([ref[pl.ds(h, 1), :] for h in group], axis=1)

    def one_hot_of(group):
        width = len(group) * lanes
        chosen = own_index[:, :width] == wide(ctarget, group)
        return jnp.where(chosen, wide(cvalid, group), 0.0).astype(bf16)

    results = []
    for group in groups:
        dist_row = wide(dist, group)
        weighted, value, slope = hidden_rows(sz, dist_row, wide(env, group), in_one)
        radial = mm(out_one, weighted)
        one_hot = one_hot_of(group)
        xt = mm(own_turned, one_hot)
        atoms, grads_of, product_grads = [], [], []
        for h in group:
            a, b = sz.halo[h]
            at = jnp.where(atom_index == catom[pl.ds(h, 1), :], cvalid[pl.ds(h, 1), :], 0.0)
            atoms.append(at)
            blocks = [at]
            rows = inv[sz.inner_row(a, b) : sz.inner_row(a, b) + n]
            message = kept[first + h]
            grads = []
            for side in range(2):
                mine = at[side * half : (side + 1) * half]
                cot = 2.0 * rows[side * half : (side + 1) * half, ch:]
                msgs = half_messages(sz, message, side)
                for m in range(8):
                    blocks.append(angular[m + 1, pl.ds(h, 1), :] * mine)
                    grads.append(msgs[m] * (cot[:, :ch] if m < 3 else cot[:, ch:]))
            blocks = jnp.concatenate(blocks, axis=0).astype(bf16)
            grads_of.append(grads)
            turned = jnp.concatenate([rows[:, :ch]] + grads, axis=0).T
            lane = lax.broadcasted_iota(jnp.int32, turned.shape, 1)
            vector = lax.rem(lane - n, 8 * half) < 3 * half
            lhs = jnp.concatenate(
                [
                    jnp.where(lane < n, turned, 0.0),
                    jnp.where((lane >= n) & vector, turned, 0.0),
                    jnp.where((lane >= n) & ~vector, turned, 0.0),
                ],
                axis=0,
            ).astype(bf16)
            product_grads.append(mm(lhs, blocks))
        product_grad = jnp.concatenate(product_grads, axis=1)
        products, mine, input_grad = radial_products(sz, product_grad, radial, xt)
        for k, h in enumerate(group):
            empty = jnp.zeros((half, ch), f32)
            rows = [
                jnp.concatenate([g, empty] if m % 8 < 3 else [empty, g], axis=1)
                for m, g in enumerate(grads_of[k])
            ]
            span = slice(k * lanes, (k + 1) * lanes)
            got = mm(
                jnp.concatenate(rows, axis=0).astype(bf16),
                jnp.concatenate([p[:, span] for p in products], axis=0),
            )
            for m in range(8):
                low = got[m * half : (m + 1) * half] * atoms[k][:half]
                high = got[(8 + m) * half : (9 + m) * half] * atoms[k][half:]
                ang_grad[m + 1, pl.ds(h, 1), :] = jnp.sum(low + high, axis=0, keepdims=True)
        dist_row_grad, env_row_grad = radial_backward(
            sz, dist_row, mine, value, slope, back_in, back_out
        )
        for k, h in enumerate(group):
            span = slice(k * lanes, (k + 1) * lanes)
            dist_grad[pl.ds(h, 1), :] = dist_row_grad[:, span]
            env_grad[pl.ds(h, 1), :] = env_row_grad[:, span]
        results.append(nt(one_hot, input_grad))
    for got in results:
        feature_acc[...] += got
    grads = separation_grads(
        cvalid[...], (sep_x, sep_y, sep_z), dist[...], ang_grad, dist_grad[...], env_grad[...]
    )
    for group in groups:
        rows = [
            jnp.concatenate([grad[h : h + 1] for h in group], axis=1) for grad in grads
        ]
        got = nt(one_hot_of(group), stacked_seps(rows))
        pos_acc[...] += got[:, :8] + got[:, 8:]


def second_kernel(
    sz, cotangent, table, kept, code, sep, wide_in, wide_out, turned_in, turned_out, mixing,
    feature_grad, forces,
    hot, xt, angular, dist, env, inv, ang_grad, dist_grad, env_grad, sep_grad,
    acc, acc_pos, halo_acc, halo_pos, *held,
):
    ch, n = sz.channels, sz.slots
    run = 3 * n
    mask_bf = atom_mask(n, sz.edges, sz.neigh).astype(bf16)
    inv[...] = three(nt, cotangent[:, :ch], mixing[0])
    target, place, parts = packed_halo(sz, code)
    in_one, out_one = wide_in[0], wide_out[0]
    back_in, back_out = turned_in[0], turned_out[0]
    owned = len(sz.own)
    seps = [sep[d, :owned] for d in range(3)]
    geometry(live_rows(code[:owned]), seps, angular, dist, env)
    index = lax.broadcasted_iota(jnp.int32, (sz.window, sz.edges), 0)

    def one_gather(k):
        window = window_of(sz, table, *sz.own[k])
        one_hot = (index == code[pl.ds(k, 1), :]).astype(f32).astype(bf16)
        return one_hot, mm(window[:, :ch].astype(f32).T.astype(bf16), one_hot)

    def one_gather_store(k, value):
        hot[k], xt[k] = value

    loop(owned, 4, each(one_gather), one_gather_store)
    acc[...] = jnp.zeros_like(acc)
    acc_pos[...] = jnp.zeros_like(acc_pos)
    halo_acc[...] = jnp.zeros_like(halo_acc)
    halo_pos[...] = jnp.zeros_like(halo_pos)

    def one_back(items):
        rows = [jnp.concatenate([ref[pl.ds(k, 1), :] for k in items], axis=1) for ref in (dist, env)]
        weighted, value, slope = hidden_rows(sz, *rows, in_one)
        out = []
        for k in items:
            span = slice((k - items[0]) * sz.edges, (k - items[0] + 1) * sz.edges)
            row = sz.inner_row(*sz.own[k])
            out.append(
                layer_backward(
                    sz, k, angular, dist, back_in, back_out,
                    mm(out_one, weighted[:, span]), value[:, span], slope[:, span],
                    xt[k], hot[k], kept[k], inv[row : row + n, :],
                )
            )
        return out

    def one_back_store(k, value):
        a, b = sz.own[k]
        got = store_grads(sz, k, value, ang_grad, dist_grad, env_grad)
        for d in range(3):
            acc[pl.ds(sz.inner_row(a - 1 + d, b - 1), run), :] += got[d * run : (d + 1) * run]

    loop(owned, 4, one_back, one_back_store)
    own_positions(
        sz, mask_bf, code, sep, dist, hot, ang_grad, dist_grad, env_grad, sep_grad, acc_pos
    )
    weights = (in_one, out_one, back_in, back_out)

    def halo_part(part, carry):
        halo_back(
            sz, part, table, cotangent, kept, sep, inv, weights,
            target, place, held, halo_acc, halo_pos,
        )
        return carry

    lax.fori_loop(0, parts, halo_part, 0)
    for a in range(sz.cols_x):
        inner = sz.inner_row(a + 1, 1)
        rows = sz.cols_y * n
        mine = slice(a * rows, (a + 1) * rows)
        feature_grad[mine] = (
            acc[inner : inner + rows] + cotangent[inner : inner + rows, :ch] + halo_acc[mine]
        )
        extra = cotangent[inner : inner + rows, ch : ch + 16]
        total = acc_pos[inner : inner + rows] + extra[:, :8] + extra[:, 8:] + halo_pos[mine]
        for b in range(sz.cols_y):
            forces[a, :, b, :] = -(total[b * n : (b + 1) * n].T)[:3]


def ring(axis):
    devices = lax.axis_size(axis)
    up = [(i, (i + 1) % devices) for i in range(devices)]
    return up, [(j, i) for i, j in up]


def extended(x, sides):
    for axis, dim in sides:
        up, down = ring(axis)
        length = x.shape[dim]
        last = lax.slice_in_dim(x, length - 2, length, axis=dim)
        initial = lax.slice_in_dim(x, 0, 2, axis=dim)
        before = lax.ppermute(last, axis, up)
        after = lax.ppermute(initial, axis, down)
        x = jnp.concatenate([before, x, after], axis=dim)
    return x


def summed(x, sides):
    total = x.astype(f32)
    for axis, dim in sides:
        up, down = ring(axis)
        length = x.shape[dim]
        sent = total.astype(bf16)
        last = lax.slice_in_dim(sent, length - 2, length, axis=dim)
        initial = lax.slice_in_dim(sent, 0, 2, axis=dim)
        before = lax.ppermute(last, axis, up).astype(f32)
        after = lax.ppermute(initial, axis, down).astype(f32)
        shape = list(x.shape)
        shape[dim] = length - 4
        parts = [before] + ([jnp.zeros(shape, f32)] if length > 4 else []) + [after]
        total = total + jnp.concatenate(parts, axis=dim)
    return total


def shards(
    features, positions, species, neighbours, counts, species_gain, radial_in, radial_out, mixing, readout
):
    cols_x, cols_y, slots, channels = features.shape
    neigh = neighbours.shape[-1]
    basis, hidden = radial_in.shape[1:]
    sz = Sizes(cols_x, cols_y, slots, neigh, channels, basis, hidden)
    vmem = pl.BlockSpec(memory_space=pltpu.VMEM)
    in_hbm = pl.BlockSpec(memory_space=pltpu.HBM)
    params = pltpu.CompilerParams(vmem_limit_bytes=40 * 1024 * 1024)
    given = (features, positions.transpose(0, 2, 1, 3), species, neighbours, counts, species_gain)
    block = pl.pallas_call(
        functools.partial(block_kernel, sz, species_gain.shape[0]),
        out_shape=jax.ShapeDtypeStruct((cols_x, cols_y, slots, 2 * channels), bf16),
        in_specs=[in_hbm] * 6,
        out_specs=vmem,
        scratch_shapes=[pltpu.VMEM(x.shape, x.dtype) for x in given]
        + [pltpu.SemaphoreType.DMA((6,))],
        compiler_params=pltpu.CompilerParams(vmem_limit_bytes=60 * 1024 * 1024),
        name="block_of_atoms",
    )(*given)
    sides = (("gx", 0), ("gy", 1))
    table = extended(block, sides).reshape(-1, 2 * channels)

    inner_atoms = sz.inner * slots
    owned = cols_x * cols_y
    edges = sz.edges
    columns, hidden_edges = sz.inner, (hidden, edges)
    grads = [
        pltpu.VMEM((9, owned, edges), f32),
        pltpu.VMEM((owned, edges), f32),
        pltpu.VMEM((owned, edges), f32),
        pltpu.VMEM((3, owned, edges), f32),
    ]
    weights = prepared(radial_in, radial_out, mixing)
    kept_shapes = [
        ((columns, sz.window, channels), f32),
        ((columns, edges), jnp.int32),
        ((3, columns, edges), f32),
    ]

    def edge_scratch(count):
        return [
            pltpu.VMEM((owned, sz.window, edges), bf16),
            pltpu.VMEM((count, channels, edges), f32),
            pltpu.VMEM((9, count, edges), f32),
            pltpu.VMEM((count, edges), f32),
            pltpu.VMEM((count, edges), f32),
            pltpu.VMEM((inner_atoms, 3 * channels), f32),
        ]

    energy, back, *kept = pl.pallas_call(
        functools.partial(first_kernel, sz),
        out_shape=[
            jax.ShapeDtypeStruct((cols_x, cols_y, slots), f32),
            jax.ShapeDtypeStruct((inner_atoms, 2 * channels), bf16),
        ]
        + [jax.ShapeDtypeStruct(*item) for item in kept_shapes],
        in_specs=[vmem] * 7,
        out_specs=[vmem] * 5,
        scratch_shapes=edge_scratch(columns)
        + [
            pltpu.VMEM((inner_atoms, channels), bf16),
            pltpu.VMEM((owned, channels, edges), f32),
            pltpu.VMEM((owned, sz.window, channels), f32),
            pltpu.VMEM((owned, 3 * channels, edges), f32),
            pltpu.VMEM((owned,) + hidden_edges, f32),
            pltpu.VMEM((owned,) + hidden_edges, f32),
        ]
        + grads
        + [pltpu.VMEM((inner_atoms, channels), f32), pltpu.VMEM((inner_atoms, 8), f32)],
        compiler_params=params,
        name="forward_and_second_back",
    )(table, *weights, readout.reshape(1, -1))

    back = back.reshape(sz.inner_x, sz.inner_y, slots, 2 * channels)
    cotangent = summed(back, sides).reshape(inner_atoms, 2 * channels)
    feature_grad, forces = pl.pallas_call(
        functools.partial(second_kernel, sz),
        out_shape=(
            jax.ShapeDtypeStruct((owned * slots, channels), f32),
            jax.ShapeDtypeStruct((cols_x, 3, cols_y, slots), f32),
        ),
        in_specs=[vmem] * 10,
        out_specs=(vmem,) * 2,
        scratch_shapes=edge_scratch(owned)
        + grads
        + [
            pltpu.VMEM((rows, width), f32)
            for rows in (inner_atoms, owned * slots)
            for width in (channels, 8)
        ]
        + [
            pltpu.VMEM(shape + (len(sz.halo), halo_lanes), f32)
            for shape in ((3,), (), (), (), (9,), (), (), (9,), (), ())
        ],
        compiler_params=params,
        name="first_back",
    )(cotangent, table, *kept, *weights)
    return (
        energy,
        forces.transpose(0, 2, 1, 3),
        feature_grad.reshape(cols_x, cols_y, slots, channels),
    )


def solution(mesh):
    placed = (
        P("gx", "gy", None, None),
        P("gx", "gy", None, None),
        P("gx", "gy", None),
        P("gx", "gy", None, None),
        P("gx", "gy", None),
        P(),
        P(),
        P(),
        P(),
        P(),
    )
    return jax.shard_map(
        shards,
        mesh=mesh,
        in_specs=placed,
        out_specs=(P("gx", "gy", None), P("gx", "gy", None, None), P("gx", "gy", None, None)),
        check_vma=False,
    )
```

time: 77.2 us -> 54.2 us (0.70)
  Pallas kernels: 42 us -> 22.2 us
  local copies, waits for them, and re-layouts: 2.71 us -> 0.4 us
  waiting for transfers between devices: 17.5 us -> 16.4 us
    pallas_call x1, Pallas kernels: 21.2 us -> 7.61 us  [shards(): pl.pallas_call(functools.partial(second_kernel, sz), out_shape=(jax.Shape...]
    pallas_call x1 -> x2, Pallas kernels: 20.8 us -> 14.6 us  [the longest x1 12.9 us: shards(): pl.pallas_call(functools.partial(first_kernel, sz), out_shape=[jax.ShapeD...]
    another operation x0 -> x4, other arithmetic: none -> 2.76 us
    convert_element_type x3 -> x2, other arithmetic: 2.38 us -> 0.1 us  [prepared(): return [x.astype(bf16) for x in (turned, wide, back_in, high, mix)]]
    ppermute x2, waiting for transfers between devices: 3.3 us -> 1.71 us  [extended(): after = lax.ppermute(initial, axis, down)]
    ppermute x2, waiting for transfers between devices: 7.94 us -> 6.46 us  [extended(): before = lax.ppermute(last, axis, up)]
    ppermute x2, starting transfers between devices: 1.79 us -> 3.19 us  [summed(): after = lax.ppermute(initial, axis, down).astype(f32)]
    ppermute x2, starting transfers between devices: 2.07 us -> 0.68 us  [summed(): before = lax.ppermute(last, axis, up).astype(f32)]
  transfers between devices with their start and end apart: 8 -> 8, of which waited for: 7 -> 6; matrix products, arithmetic and copies ran while one was open for 1% -> 6% of each run, Pallas kernels for 0% -> 0%
where the time goes in v2:
time: 54.2 us; the launch traced here: 53.3 us
  Pallas kernels  22.2 us (41%)
  waiting for transfers between devices  16.4 us (30%)
  starting transfers between devices  10.5 us (19%)
  other arithmetic  3.04 us (6%)
  between operations  0.76 us (1%)
    pallas_call x1, Pallas kernels, shards(): pl.pallas_call(functools.partial(first_kernel, sz), out_shape=[jax.ShapeD...  12.9 us
    pallas_call x1, Pallas kernels, shards(): pl.pallas_call(functools.partial(second_kernel, sz), out_shape=(jax.Shape...  7.61 us
    ppermute x2, waiting for transfers between devices, extended(): before = lax.ppermute(last, axis, up)  6.46 us
    ppermute x2, starting transfers between devices, extended(): after = lax.ppermute(initial, axis, down)  6.09 us
    ppermute x2, waiting for transfers between devices, summed(): before = lax.ppermute(last, axis, up).astype(f32)  6.02 us
    ppermute x2, starting transfers between devices, summed(): after = lax.ppermute(initial, axis, down).astype(f32)  3.19 us
    ppermute x2, waiting for transfers between devices, summed(): after = lax.ppermute(initial, axis, down).astype(f32)  2.24 us
    pallas_call x1, Pallas kernels, shards(): pl.pallas_call(functools.partial(block_kernel, sz, species_gain.shape[0])...  1.72 us
  transfers between devices with their start and end apart: 8, of which 6 were waited for; matrix products, arithmetic and copies ran while one was open for 6% of the time, Pallas kernels for 0%

profile of v2, /device:TPU:0, one launch (start us, length us, event | category | flops | bytes accessed | tf_op | source)
XLA Modules:
  0.0 53.3 jit_solution(14937236896086723317)
XLA Ops:
  0.6 1.7 %block_of_atoms.1 = bf16[2,2,16,256]{3,2,1,0:T(8,128)(2,1)} custom-call(bf16[2,2,16,128]{3,2,1,0:T(8,128)(2,1)} %refs_0_.1, f32[2,3,2,16]{3,2,1,0:T(2,128)} %bitcast.32, s32[2,2,16]{2,1,0:T(2,128)} %refs_2_.1, s32[2,2,16,32]{3,2,1,0:T(8,128)} %refs_3_.1, s32[2,2,16]{2,1,0:T(2,128)} %refs_4_.1, f32[6,128]{1,0:T(8,128)} %refs_5_.1), custom_call_target="tpu_custom_call" | custom-call | tf_op jit(solution)/shard_map/block_of_atoms/pallas_call | solution.py:826
  2.4 6.0 %collective-permute-start.1 = (bf16[2,2,16,256]{3,2,1,0:T(8,128)(2,1)}, bf16[2,2,16,256]{3,2,1,0:T(8,128)(2,1)S(1)}, u32[]{:S(2)}, u32[]{:S(2)}) collective-permute-start(bf16[2,2,16,256]{3,2,1,0:T(8,128)(2,1)} %block_of_atoms.1), channel_id=1, source_target_pairs={{4,0},{8,4},{12,8},{16,12},{20,16},{24,20},{28,24},{0,28},{5,1},{9... | collective-permute-start | bytes 98312 | tf_op jit(solution)/shard_map/ppermute | solution.py:793
  8.4 0.0 collective-permute-start
  8.4 0.7 %reduce-precision_convert_fusion.2 = (bf16[2,8,64]{2,1,0:T(8,128)(2,1)S(1)}, bf16[2,8,64]{2,1,0:T(8,128)(2,1)S(1)}) fusion(f32[2,8,64]{2,1,0:T(8,128)} %param.16), kind=kLoop, calls=%fused_computation.19 | loop fusion | flops 4096 | bytes 8192 | tf_op jit(solution)/shard_map/convert.13
  9.1 1.0 %reduce-precision_convert_fusion.1 = (bf16[2,64,384]{2,1,0:T(8,128)(2,1)S(1)}, bf16[2,64,384]{2,1,0:T(8,128)(2,1)S(1)}) fusion(f32[2,64,384]{2,1,0:T(8,128)} %param.17), kind=kLoop, calls=%fused_computation.7 | loop fusion | flops 196608 | bytes 393216 | tf_op jit(solution)/shard_map/convert.10
  10.1 1.1 %fusion.3 = (bf16[2,1,384,128]{3,2,1,0:T(8,128)(2,1)S(1)}, bf16[2,1,384,128]{3,2,1,0:T(8,128)(2,1)S(1)}) fusion(f32[2,384,128]{2,1,0:T(8,128)} %param.18), kind=kLoop, calls=%fused_computation.13 | loop fusion | flops 393216 | bytes 786432 | tf_op jit(solution)/shard_map/stack | solution.py:52
  11.1 0.0 copy-start.1
  11.1 0.1 pad.14.clone
  11.3 0.0 copy-start
  11.3 0.1 maximum_bitcast_fusion.1
  11.4 0.1 copy.14.wide_in
  11.5 0.2 copy.15.wide_out
  11.7 0.0 collective-permute-done.1
  11.7 3.5 %collective-permute-done = bf16[2,2,16,256]{3,2,1,0:T(8,128)(2,1)S(1)} collective-permute-done((bf16[2,2,16,256]{3,2,1,0:T(8,128)(2,1)}, bf16[2,2,16,256]{3,2,1,0:T(8,128)(2,1)S(1)}, u32[]{:S(2)}, u32[]{:S(2)}) %collective-permute-start) | collective-permute-done | bytes 32800 | tf_op jit(solution)/shard_map/ppermute | solution.py:792
  15.2 0.0 copy-done.1
  15.2 0.1 collective-permute-start.3
  15.3 0.5 collective-permute-start.2
  15.8 1.7 %collective-permute-done.3 = bf16[6,2,16,256]{3,2,1,0:T(8,128)(2,1)S(1)} collective-permute-done((bf16[6,2,16,256]{3,2,1,0:T(8,128)(2,1)S(1)}, bf16[6,2,16,256]{3,2,1,0:T(8,128)(2,1)S(1)}, u32[]{:S(2)}, u32[]{:S(2)}) %collective-permute-start.3) | collective-permute-done | bytes 98336 | tf_op jit(solution)/shard_map/ppermute | solution.py:793
  17.5 2.9 %collective-permute-done.2 = bf16[6,2,16,256]{3,2,1,0:T(8,128)(2,1)S(1)} collective-permute-done((bf16[6,2,16,256]{3,2,1,0:T(8,128)(2,1)S(1)}, bf16[6,2,16,256]{3,2,1,0:T(8,128)(2,1)S(1)}, u32[]{:S(2)}, u32[]{:S(2)}) %collective-permute-start.2) | collective-permute-done | bytes 98336 | tf_op jit(solution)/shard_map/ppermute | solution.py:792
  20.5 0.0 copy-done
  20.5 12.9 %forward_and_second_back.1 = (f32[2,2,16]{2,1,0:T(2,128)}, bf16[256,256]{1,0:T(8,128)(2,1)S(1)}, f32[16,144,128]{2,1,0:T(8,128)S(1)}, s32[16,512]{1,0:T(8,128)S(1)}, f32[3,16,512]{2,1,0:T(8,128)S(1)}) custom-call(bf16[576,256]{1,0:T(8,128)(2,1)S(1)} %bitcast.26, bf16[2,64,32]{2,1,0:T(8,128)(2,1)S(1)} %copy.14.wide_in, ...), custom_call_target="tpu_custom_call" | custom-call | tf_op jit(solution)/shard_map/forward_and_second_back/pallas_call | solution.py:866
  33.4 1.5 %collective-permute-start.5 = (bf16[2,4,16,256]{3,2,1,0:T(8,128)(2,1)S(1)}, bf16[2,4,16,256]{3,2,1,0:T(8,128)(2,1)S(1)}, u32[]{:S(2)}, u32[]{:S(2)}) collective-permute-start(bf16[2,4,16,256]{3,2,1,0:T(8,128)(2,1)S(1)} %bitcast.31), channel_id=1, source_target_pairs={{4,0},{8,4},{12,8},{16,12},{20,16},{24,20},{28,24},{0,28},{5,1},{9... | collective-permute-start | bytes 196616 | tf_op jit(solution)/shard_map/ppermute | solution.py:807
  34.8 0.6 %collective-permute-start.4 = (bf16[2,4,16,256]{3,2,1,0:T(8,128)(2,1)S(1)}, bf16[2,4,16,256]{3,2,1,0:T(8,128)(2,1)S(1)}, u32[]{:S(2)}, u32[]{:S(2)}) collective-permute-start(bf16[2,4,16,256]{3,2,1,0:T(8,128)(2,1)S(1)} %bitcast.30), channel_id=1, source_target_pairs={{0,4},{4,8},{8,12},{12,16},{16,20},{20,24},{24,28},{28,0},{1,5},{5... | collective-permute-start | bytes 196616 | tf_op jit(solution)/shard_map/ppermute | solution.py:806
  35.5 2.2 %collective-permute-done.5 = bf16[2,4,16,256]{3,2,1,0:T(8,128)(2,1)S(1)} collective-permute-done((bf16[2,4,16,256]{3,2,1,0:T(8,128)(2,1)S(1)}, bf16[2,4,16,256]{3,2,1,0:T(8,128)(2,1)S(1)}, u32[]{:S(2)}, u32[]{:S(2)}) %collective-permute-start.5) | collective-permute-done | bytes 65568 | tf_op jit(solution)/shard_map/ppermute | solution.py:807
  37.7 4.1 %collective-permute-done.4 = bf16[2,4,16,256]{3,2,1,0:T(8,128)(2,1)S(1)} collective-permute-done((bf16[2,4,16,256]{3,2,1,0:T(8,128)(2,1)S(1)}, bf16[2,4,16,256]{3,2,1,0:T(8,128)(2,1)S(1)}, u32[]{:S(2)}, u32[]{:S(2)}) %collective-permute-start.4) | collective-permute-done | bytes 65568 | tf_op jit(solution)/shard_map/ppermute | solution.py:806
  41.9 0.1 collective-permute-start.6
  41.9 1.7 %collective-permute-start.7 = (bf16[4,2,16,256]{3,2,1,0:T(8,128)(2,1)S(1)}, bf16[4,2,16,256]{3,2,1,0:T(8,128)(2,1)S(1)}, u32[]{:S(2)}, u32[]{:S(2)}) collective-permute-start(bf16[4,2,16,256]{3,2,1,0:T(8,128)(2,1)S(1)} %get-tuple-element.22), channel_id=1, source_target_pairs={{1,0},{2,1},{3,2},{0,3},{5,4},{6,5},{7,6},{4,7},{9,8},{10,9},{11,1... | collective-permute-start | bytes 196616 | tf_op jit(solution)/shard_map/ppermute | solution.py:807
  43.7 1.9 %collective-permute-done.6 = bf16[4,2,16,256]{3,2,1,0:T(8,128)(2,1)S(1)} collective-permute-done((bf16[4,2,16,256]{3,2,1,0:T(8,128)(2,1)S(1)}, bf16[4,2,16,256]{3,2,1,0:T(8,128)(2,1)S(1)}, u32[]{:S(2)}, u32[]{:S(2)}) %collective-permute-start.6) | collective-permute-done | bytes 65568 | tf_op jit(solution)/shard_map/ppermute | solution.py:806
  45.6 0.0 collective-permute-done.7
  45.6 0.1 convert_add_fusion.cotangent
  45.7 7.6 %first_back.1 = (f32[64,128]{1,0:T(8,128)}, f32[2,3,2,16]{3,2,1,0:T(2,128)}) custom-call(f32[256,256]{1,0:T(8,128)S(1)} %convert_add_fusion.cotangent, bf16[576,256]{1,0:T(8,128)(2,1)S(1)} %bitcast.27, f32[16,144,128]{2,1,0:T(8,128)S(1)} %get-tuple-element.12.kept, s32[16,512]{1,0:T(8,128)S(1)} %get-tuple-element.13.code, ...), custom_call_target="tpu_custom_call" | custom-call | tf_op jit(solution)/shard_map/first_back/pallas_call | solution.py:892
  (11 shorter events, 0.2 us)
Async XLA Ops:
  2.4 9.3 %collective-permute-start.1 = (bf16[2,2,16,256]{3,2,1,0:T(8,128)(2,1)}, bf16[2,2,16,256]{3,2,1,0:T(8,128)(2,1)S(1)}, u32[]{:S(2)}, u32[]{:S(2)}) collective-permute-start(bf16[2,2,16,256]{3,2,1,0:T(8,128)(2,1)} %block_of_atoms.1), channel_id=1, source_target_pairs={{4,0},{8,4},{12,8},{16,12},{20,16},{24,20},{28,24},{0,28},{5,1},{9... | collective-permute-start | bytes 98312 | tf_op jit(solution)/shard_map/ppermute | solution.py:793
  8.4 6.8 %collective-permute-start = (bf16[2,2,16,256]{3,2,1,0:T(8,128)(2,1)}, bf16[2,2,16,256]{3,2,1,0:T(8,128)(2,1)S(1)}, u32[]{:S(2)}, u32[]{:S(2)}) collective-permute-start(bf16[2,2,16,256]{3,2,1,0:T(8,128)(2,1)} %block_of_atoms.1), channel_id=1, source_target_pairs={{0,4},{4,8},{8,12},{12,16},{16,20},{20,24},{24,28},{28,0},{1,5},{5... | collective-permute-start | bytes 98312 | tf_op jit(solution)/shard_map/ppermute | solution.py:792
  11.1 4.1 %copy-start.1 = (bf16[2,2,16,256]{3,2,1,0:T(8,128)(2,1)S(1)}, bf16[2,2,16,256]{3,2,1,0:T(8,128)(2,1)}, u32[]{:S(2)}) copy-start(bf16[2,2,16,256]{3,2,1,0:T(8,128)(2,1)} %block_of_atoms.1) | copy-start | bytes 98308
  11.3 9.2 %copy-start = (f32[128]{0:T(128)S(1)}, f32[128]{0:T(128)}, u32[]{:S(2)}) copy-start(f32[128]{0:T(128)} %param.19) | copy-start | bytes 1540
  15.2 2.3 %collective-permute-start.3 = (bf16[6,2,16,256]{3,2,1,0:T(8,128)(2,1)S(1)}, bf16[6,2,16,256]{3,2,1,0:T(8,128)(2,1)S(1)}, u32[]{:S(2)}, u32[]{:S(2)}) collective-permute-start(bf16[6,2,16,256]{3,2,1,0:T(8,128)(2,1)S(1)} %pad_maximum_fusion.3), channel_id=1, source_target_pairs={{1,0},{2,1},{3,2},{0,3},{5,4},{6,5},{7,6},{4,7},{9,8},{10,9},{11,1... | collective-permute-start | bytes 294920 | tf_op jit(solution)/shard_map/ppermute | solution.py:793
  15.3 5.1 %collective-permute-start.2 = (bf16[6,2,16,256]{3,2,1,0:T(8,128)(2,1)S(1)}, bf16[6,2,16,256]{3,2,1,0:T(8,128)(2,1)S(1)}, u32[]{:S(2)}, u32[]{:S(2)}) collective-permute-start(bf16[6,2,16,256]{3,2,1,0:T(8,128)(2,1)S(1)} %pad_maximum_fusion.3), channel_id=1, source_target_pairs={{0,1},{1,2},{2,3},{3,0},{4,5},{5,6},{6,7},{7,4},{8,9},{9,10},{10,1... | collective-permute-start | bytes 294920 | tf_op jit(solution)/shard_map/ppermute | solution.py:792
  33.4 4.3 %collective-permute-start.5 = (bf16[2,4,16,256]{3,2,1,0:T(8,128)(2,1)S(1)}, bf16[2,4,16,256]{3,2,1,0:T(8,128)(2,1)S(1)}, u32[]{:S(2)}, u32[]{:S(2)}) collective-permute-start(bf16[2,4,16,256]{3,2,1,0:T(8,128)(2,1)S(1)} %bitcast.31), channel_id=1, source_target_pairs={{4,0},{8,4},{12,8},{16,12},{20,16},{24,20},{28,24},{0,28},{5,1},{9... | collective-permute-start | bytes 196616 | tf_op jit(solution)/shard_map/ppermute | solution.py:807
  34.8 7.0 %collective-permute-start.4 = (bf16[2,4,16,256]{3,2,1,0:T(8,128)(2,1)S(1)}, bf16[2,4,16,256]{3,2,1,0:T(8,128)(2,1)S(1)}, u32[]{:S(2)}, u32[]{:S(2)}) collective-permute-start(bf16[2,4,16,256]{3,2,1,0:T(8,128)(2,1)S(1)} %bitcast.30), channel_id=1, source_target_pairs={{0,4},{4,8},{8,12},{12,16},{16,20},{20,24},{24,28},{28,0},{1,5},{5... | collective-permute-start | bytes 196616 | tf_op jit(solution)/shard_map/ppermute | solution.py:806
  41.9 3.7 %collective-permute-start.6 = (bf16[4,2,16,256]{3,2,1,0:T(8,128)(2,1)S(1)}, bf16[4,2,16,256]{3,2,1,0:T(8,128)(2,1)S(1)}, u32[]{:S(2)}, u32[]{:S(2)}) collective-permute-start(bf16[4,2,16,256]{3,2,1,0:T(8,128)(2,1)S(1)} %get-tuple-element.21), channel_id=1, source_target_pairs={{0,1},{1,2},{2,3},{3,0},{4,5},{5,6},{6,7},{7,4},{8,9},{9,10},{10,1... | collective-permute-start | bytes 196616 | tf_op jit(solution)/shard_map/ppermute | solution.py:806
  41.9 3.7 %collective-permute-start.7 = (bf16[4,2,16,256]{3,2,1,0:T(8,128)(2,1)S(1)}, bf16[4,2,16,256]{3,2,1,0:T(8,128)(2,1)S(1)}, u32[]{:S(2)}, u32[]{:S(2)}) collective-permute-start(bf16[4,2,16,256]{3,2,1,0:T(8,128)(2,1)S(1)} %get-tuple-element.22), channel_id=1, source_target_pairs={{1,0},{2,1},{3,2},{0,3},{5,4},{6,5},{7,6},{4,7},{9,8},{10,9},{11,1... | collective-permute-start | bytes 196616 | tf_op jit(solution)/shard_map/ppermute | solution.py:807

commit v3 on v2

v3 whole, which is shorter than its diff:
```python
import functools

import jax
import jax.numpy as jnp
from jax import lax
from jax.experimental import pallas as pl
from jax.experimental.pallas import tpu as pltpu
from jax.sharding import PartitionSpec as P

column = 6.0
cutoff = 6.0
softening = 0.01
root_three = 3.0**0.5
f32 = jnp.float32
bf16 = jnp.bfloat16
code_lane = 32
part_lanes = 256


def mm(a, b):
    return lax.dot_general(a, b, (((1,), (0,)), ((), ())), preferred_element_type=f32)


def nt(a, b):
    return lax.dot_general(a, b, (((1,), (1,)), ((), ())), preferred_element_type=f32)


def split(x):
    high = x.astype(bf16)
    return high, (x - high.astype(f32)).astype(bf16)


def three(product, a, b):
    a_high, a_low = split(a)
    b_high, b_low = split(b) if b.dtype == f32 else (b[0], b[1])
    return product(a_high, b_high) + product(a_low, b_high) + product(a_high, b_low)


def parted(x):
    high = lax.reduce_precision(x, 8, 7)
    return high, x - high


def prepared(radial_in, radial_out, mixing):
    high, low = parted(radial_in)
    turned = jnp.concatenate([high, high, low, jnp.zeros_like(high)], axis=1).swapaxes(1, 2)
    back_in = jnp.concatenate([high, low], axis=1)
    high, low = parted(radial_out)
    wide = jnp.concatenate([high, high, low], axis=1).swapaxes(1, 2)
    high_mix, low_mix = parted(mixing)
    mix = jnp.stack([high_mix, low_mix], axis=1)
    return [x.astype(bf16) for x in (turned, wide, back_in, high, mix)]


def harmonic_rows(ux, uy, uz):
    square = ux * ux + uy * uy + uz * uz
    return [
        jnp.ones_like(ux),
        ux,
        uy,
        uz,
        root_three * ux * uy,
        root_three * uy * uz,
        0.5 * (3.0 * uz * uz - square),
        root_three * ux * uz,
        0.5 * root_three * (ux * ux - uy * uy),
    ]


class Sizes:
    def __init__(self, cols_x, cols_y, slots, neigh, channels, basis, hidden):
        self.cols_x, self.cols_y = cols_x, cols_y
        self.slots, self.neigh, self.channels = slots, neigh, channels
        self.basis, self.hidden = basis, hidden
        self.inner_x, self.inner_y = cols_x + 2, cols_y + 2
        self.outer_y = cols_y + 4
        self.inner = self.inner_x * self.inner_y
        self.edges = part_lanes
        self.window = 9 * slots

        cells = [(a, b) for a in range(self.inner_x) for b in range(self.inner_y)]
        self.own = [c for c in cells if self.is_own(*c)]
        self.halo = [c for c in cells if not self.is_own(*c)]
        self.order = self.own + self.halo

    def is_own(self, a, b):
        return 1 <= a <= self.cols_x and 1 <= b <= self.cols_y

    def outer_row(self, a, b):
        return (a * self.outer_y + b) * self.slots

    def inner_row(self, a, b):
        return (a * self.inner_y + b) * self.slots


def each(compute):
    return lambda items: [compute(item) for item in items]


def loop(count, group, compute, store):
    for first in range(0, count, group):
        items = list(range(first, min(first + group, count)))
        for item, value in zip(items, compute(items)):
            store(item, value)


def window_of(sz, table, a, b):
    run = 3 * sz.slots
    return jnp.concatenate(
        [table[pl.ds(sz.outer_row(a + d, b), run), :] for d in range(3)], axis=0
    )


def iota(shape, dim):
    return lax.broadcasted_iota(jnp.int32, shape, dim).astype(f32)


def bounds_of(sz, table):
    n, ch = sz.slots, sz.channels
    rows = [sz.outer_row(a + 1, b + 1) for a, b in sz.order]
    metas = jnp.concatenate([table[row : row + n, ch:] for row in rows], axis=0)
    shape = (sz.inner * n, sz.inner * n)
    left = lax.broadcasted_iota(jnp.int32, shape, 0)
    right = lax.broadcasted_iota(jnp.int32, shape, 1)
    earlier = (left // n == right // n) & (right < left)
    sums = mm(earlier.astype(f32).astype(bf16), metas)
    lane = code_lane + sz.neigh
    low = sums[:, lane : lane + 1]
    return low, low + metas[:, lane : lane + 1].astype(f32)


def gather_columns(sz, part, table, low, high, code, atom, sep, hot, xt):
    ch, n = sz.channels, sz.slots
    lane = iota((n, sz.edges), 1) + (part * sz.edges).astype(f32)
    row = iota((n, sz.edges), 0)
    slot = iota((sz.neigh, sz.edges), 0)
    target = iota((sz.window, sz.edges), 0)

    def one(col):
        a, b = sz.order[col]
        meta = table[pl.ds(sz.outer_row(a + 1, b + 1), n), ch : 2 * ch]
        mine = slice(col * n, (col + 1) * n)
        at = ((lane >= low[mine]) & (lane < high[mine])).astype(f32)
        valid = jnp.sum(at, axis=0, keepdims=True) - 1.0
        which = lane[:1] - jnp.sum(at * low[mine], axis=0, keepdims=True)
        spread = mm(meta.astype(f32).T[: 2 * code_lane].astype(bf16), at.astype(bf16))
        picked = jnp.where(slot == which, spread[code_lane:], 0.0)
        codes = jnp.sum(picked, axis=0, keepdims=True) + valid
        atoms = jnp.sum(at * row, axis=0, keepdims=True) + valid
        one_hot = (target == codes).astype(f32).astype(bf16)
        turned = window_of(sz, table, a, b).astype(f32).T.astype(bf16)[: ch + 32]
        found = mm(turned, one_hot)
        diff = found[ch : ch + 24] - spread[:24]
        return codes, atoms, one_hot, found[:ch], diff[0:8] + diff[8:16] + diff[16:24]

    def store(col, value):
        code[part, pl.ds(col, 1), :], atom[part, pl.ds(col, 1), :], one_hot, found, total = value
        if col < len(sz.own):
            hot[part, col] = one_hot
        xt[col] = found
        for d in range(3):
            sep[part, d, pl.ds(col, 1), :] = total[d : d + 1]

    loop(sz.inner, 4, each(one), store)


def shifted_seps(part, code, sep):
    offset = code[part].astype(jnp.int32) >> 4
    step_x = (offset * 11) >> 5
    step_y = offset - 3 * step_x
    sep[part, 0] = sep[part, 0] + column * (step_x - 1).astype(f32)
    sep[part, 1] = sep[part, 1] + column * (step_y - 1).astype(f32)


def geometry(live, seps):
    sep_x, sep_y, sep_z = seps
    dist_sq = sep_x * sep_x + sep_y * sep_y + sep_z * sep_z
    env = jnp.square(jnp.maximum(1.0 - dist_sq / (cutoff * cutoff), 0.0)) * live
    rows = harmonic_rows(sep_x / cutoff, sep_y / cutoff, sep_z / cutoff)
    return jnp.sqrt(dist_sq + softening), env, rows


def store_geometry(part, live, seps, dist, env, angular):
    dist[part], env[part], rows = geometry(live, seps)
    for m, row in enumerate(rows):
        angular[part, m] = row


def live_rows(code):
    return (code >= 0.0).astype(f32)


def basis_rows(sz, dist_row):
    width = dist_row.shape[1]
    spacing = cutoff / (sz.basis - 1)
    centre = lax.broadcasted_iota(jnp.int32, (sz.basis, width), 0).astype(f32) * spacing
    shifted = (dist_row - centre) * (1.0 / spacing)
    return jnp.exp(-shifted * shifted), shifted


def sigmoid(x):
    return 0.5 * jnp.tanh(0.5 * x) + 0.5


def hidden_rows(sz, dist_row, env_row, weight_in):
    basis, _ = basis_rows(sz, dist_row)
    high = basis.astype(bf16).astype(f32)
    stacked = jnp.concatenate([high, basis - high, high, jnp.zeros_like(high)], axis=0)
    pre = mm(weight_in, stacked.astype(bf16))
    gate = sigmoid(pre)
    value = pre * gate
    weighted = value * env_row
    high, low = split(weighted)
    slope = gate * (1.0 + pre * (1.0 - gate)) * env_row
    return jnp.concatenate([high, low, high], axis=0), value, slope


def atoms_at(sz, atom, part, col):
    return (iota((sz.slots, sz.edges), 0) == atom[part, pl.ds(col, 1), :]).astype(f32)


def block_rows(angular, part, col, at):
    return [angular[part, m, pl.ds(col, 1), :] * at for m in range(1, 9)]


def layer_forward(sz, part, cols, angular, dist, env, atom, weight_in, weight_out, inputs):
    rows = [jnp.concatenate([ref[part, pl.ds(c, 1), :] for c in cols], axis=1) for ref in (dist, env)]
    weighted, value, slope = hidden_rows(sz, *rows, weight_in)
    out = []
    for k, (col, xt) in enumerate(zip(cols, inputs)):
        span = slice(k * sz.edges, (k + 1) * sz.edges)
        radial = mm(weight_out, weighted[:, span])
        message = column_messages(sz, part, col, angular, atom, radial, xt)
        out.append((radial, value[:, span], slope[:, span], message))
    return out


def column_messages(sz, part, col, angular, atom, radial, xt):
    ch, n = sz.channels, sz.slots
    product = [(radial[l * ch : (l + 1) * ch] * xt).astype(bf16) for l in range(3)]
    at = atoms_at(sz, atom, part, col)
    scalar = nt(product[0], at.astype(bf16)).T
    blocks = jnp.concatenate(block_rows(angular, part, col, at), axis=0)
    high = blocks.astype(bf16).astype(f32)
    both = jnp.concatenate([high, blocks - high], axis=0).astype(bf16)
    count = 8 * n
    vector, tensor = nt(product[1], both), nt(product[2], both)
    vector = vector[:, :count] + vector[:, count:]
    tensor = tensor[:, :count] + tensor[:, count:]
    lane = lax.broadcasted_iota(jnp.int32, (ch, count), 1)
    return jnp.concatenate([scalar, jnp.where(lane < 3 * n, vector, tensor).T], axis=0)


def invariants(sz, message):
    n = sz.slots
    squares = message * message
    got = [squares[m * n : (m + 1) * n] for m in range(9)]
    return jnp.concatenate(
        [message[:n], got[1] + got[2] + got[3], got[4] + got[5] + got[6] + got[7] + got[8]],
        axis=1,
    )


def message_grads(sz, message, cotangent):
    ch, n = sz.channels, sz.slots
    twice = 2.0 * cotangent[:, ch:]
    parts = [
        message[m * n : (m + 1) * n] * (twice[:, :ch] if m < 4 else twice[:, ch:])
        for m in range(1, 9)
    ]
    return [cotangent[:, :ch]] + parts


def radial_products(sz, product_grad, radial, xt):
    ch = sz.channels
    products, mine, input_grad = [], [], None
    for l in range(3):
        grad, part = product_grad[l * ch : (l + 1) * ch], radial[l * ch : (l + 1) * ch]
        if l:
            products.append((part * xt).astype(bf16))
        mine.append((grad * xt).astype(bf16))
        term = grad * part
        input_grad = term if input_grad is None else input_grad + term
    return products, jnp.concatenate(mine, axis=0), input_grad.astype(bf16)


def radial_backward(sz, dist_row, radial_grad, value, slope, back_in, back_out):
    weighted_grad = mm(back_out, radial_grad)
    env_row_grad = jnp.sum(weighted_grad * value, axis=0, keepdims=True)
    both = mm(back_in, (weighted_grad * slope).astype(bf16))
    basis_grad = both[: sz.basis] + both[sz.basis : 2 * sz.basis]
    basis, shifted = basis_rows(sz, dist_row)
    spacing = cutoff / (sz.basis - 1)
    dist_row_grad = jnp.sum(
        basis_grad * basis * shifted * (-2.0 / spacing), axis=0, keepdims=True
    )
    return dist_row_grad, env_row_grad


def layer_backward(
    sz, part, cols, angular, dist, atom, back_in, back_out, radials, value, slope, inputs, hots,
    messages, cotangents,
):
    ch, n = sz.channels, sz.slots
    mine, windows, ang_grads = [], [], []
    for k, col in enumerate(cols):
        at = atoms_at(sz, atom, part, col)
        blocks = jnp.concatenate([at] + block_rows(angular, part, col, at), axis=0).astype(bf16)
        grads = message_grads(sz, messages[k], cotangents[k])
        turned = jnp.concatenate(grads, axis=0).T
        lane = lax.broadcasted_iota(jnp.int32, turned.shape, 1)
        lhs = jnp.concatenate(
            [
                jnp.where(lane < n, turned, 0.0),
                jnp.where((lane >= n) & (lane < 4 * n), turned, 0.0),
                jnp.where(lane >= 4 * n, turned, 0.0),
            ],
            axis=0,
        ).astype(bf16)
        products, radial_grad, input_grad = radial_products(
            sz, mm(lhs, blocks), radials[k], inputs[k]
        )
        mine.append(radial_grad)
        windows.append(nt(hots[k], input_grad))
        empty = jnp.zeros((n, ch), f32)
        wide = [
            jnp.concatenate([g, empty] if m < 3 else [empty, g], axis=1)
            for m, g in enumerate(grads[1:])
        ]
        got = mm(jnp.concatenate(wide, axis=0).astype(bf16), jnp.concatenate(products, axis=0))
        ang_grads.append(
            [jnp.sum(got[m * n : (m + 1) * n] * at, axis=0, keepdims=True) for m in range(8)]
        )
    dist_row = jnp.concatenate([dist[part, pl.ds(col, 1), :] for col in cols], axis=1)
    dist_row_grad, env_row_grad = radial_backward(
        sz, dist_row, jnp.concatenate(mine, axis=1), value, slope, back_in, back_out
    )
    out = []
    for k in range(len(cols)):
        span = slice(k * sz.edges, (k + 1) * sz.edges)
        out.append((windows[k], ang_grads[k], dist_row_grad[:, span], env_row_grad[:, span]))
    return out


def store_grads(sz, col, value, ang_grad, dist_grad, env_grad, acc):
    window, ang_grads, dist_row_grad, env_row_grad = value
    for m in range(8):
        ang_grad[m + 1, pl.ds(col, 1), :] = ang_grads[m]
    dist_grad[pl.ds(col, 1), :] = dist_row_grad
    env_grad[pl.ds(col, 1), :] = env_row_grad
    add_window(sz, sz.own[col], window, acc)


def add_window(sz, place, window, acc):
    a, b = place
    run = 3 * sz.slots
    for d in range(3):
        acc[pl.ds(sz.inner_row(a - 1 + d, b - 1), run), :] += window[d * run : (d + 1) * run]


def separation_grads(live, sep, dist, ang_grad, dist_grad, env_grad):
    sep_x, sep_y, sep_z = sep
    ux, uy, uz = sep_x / cutoff, sep_y / cutoff, sep_z / cutoff
    dist_sq = sep_x * sep_x + sep_y * sep_y + sep_z * sep_z
    inside = jnp.maximum(1.0 - dist_sq / (cutoff * cutoff), 0.0)
    sq_grad = dist_grad * (0.5 / dist) - env_grad * live * inside * (2.0 / (cutoff * cutoff))
    g = ang_grad
    r3 = root_three
    grad_x = g[1] + r3 * (uy * g[4] + uz * g[7] + ux * g[8]) - ux * g[6]
    grad_y = g[2] + r3 * (ux * g[4] + uz * g[5] - uy * g[8]) - uy * g[6]
    grad_z = g[3] + r3 * (uy * g[5] + ux * g[7]) + 2.0 * uz * g[6]
    return (
        2.0 * sep_x * sq_grad + grad_x / cutoff,
        2.0 * sep_y * sq_grad + grad_y / cutoff,
        2.0 * sep_z * sq_grad + grad_z / cutoff,
    )


def stacked_seps(rows):
    full = jnp.concatenate(rows + [jnp.zeros((5, rows[0].shape[1]), f32)], axis=0)
    high = full.astype(bf16).astype(f32)
    return jnp.concatenate([high, full - high], axis=0).astype(bf16)


def own_positions(
    sz, part, code, atom, sep, dist, hot, ang_grad, dist_grad, env_grad, sep_grad, acc_pos
):
    owned = len(sz.own)
    grads = separation_grads(
        live_rows(code[part, :owned]),
        [sep[part, d, :owned] for d in range(3)],
        dist[part, :owned],
        ang_grad,
        dist_grad[...],
        env_grad[...],
    )
    for d in range(3):
        sep_grad[d] = grads[d]
    for k, place in enumerate(sz.own):
        rows = [sep_grad[d, pl.ds(k, 1), :] for d in range(3)]
        signed = signed_hot(sz, hot[part, k], atoms_at(sz, atom, part, k).astype(bf16))
        got = nt(signed, stacked_seps(rows))
        add_window(sz, place, got[:, :8] + got[:, 8:], acc_pos)


def signed_hot(sz, one_hot, mask_bf):
    first = 4 * sz.slots
    return jnp.concatenate(
        [one_hot[:first], one_hot[first : first + sz.slots] - mask_bf, one_hot[first + sz.slots :]],
        axis=0,
    )


def fetch(sources, targets, sems):
    copies = [
        pltpu.make_async_copy(source, target, sems.at[k])
        for k, (source, target) in enumerate(zip(sources, targets))
    ]
    for copy in copies:
        copy.start()
    return copies


def block_kernel(sz, kinds, *refs):
    sources, block, held, sems = refs[:6], refs[6], refs[7:13], refs[13]
    for copy in fetch(sources, held, sems):
        copy.wait()
    features, positions, species, neighbours, counts, species_gain = held
    ch, n = sz.channels, sz.slots
    gains = species_gain[...]
    gain_high = gains.astype(bf16).astype(f32)
    rest = gains - gain_high
    gain_middle = rest.astype(bf16).astype(f32)
    parts = [gain_high, gain_middle, rest - gain_middle]
    above, below = jnp.zeros((24, ch), f32), jnp.zeros((8 - kinds, ch), f32)
    parts = [jnp.concatenate([above, part, below], axis=0).astype(bf16) for part in parts]
    kind = lax.broadcasted_iota(jnp.int32, (8, n), 0)
    tail_lane = lax.broadcasted_iota(jnp.int32, (n, ch - code_lane - sz.neigh), 1)
    lane = lax.broadcasted_iota(jnp.int32, (n, code_lane), 1)
    gap = jnp.zeros((5, n), f32)
    for a in range(sz.cols_x):
        for b in range(sz.cols_y):
            atoms = positions[a, :, b, :]
            high = atoms.astype(bf16).astype(f32)
            rest = atoms - high
            middle = rest.astype(bf16).astype(f32)
            chosen = (kind == species[a, pl.ds(b, 1), :]).astype(f32)
            last = jnp.where(kind == 7, counts[a, pl.ds(b, 1), :].astype(f32), chosen)
            rows = [high, gap, middle, gap, rest - middle, gap, last]
            turned = jnp.concatenate(rows, axis=0).T
            picked = jnp.where((lane >= 24) & (lane < 24 + kinds), turned, 0.0).astype(bf16)
            gain = mm(picked, parts[0]) + mm(picked, parts[1]) + mm(picked, parts[2])
            place = jnp.where(lane < 24, turned, 0.0)
            count = jnp.where(tail_lane == 0, turned[:, 31:32], 0.0)
            block[a, b, :, :ch] = (features[a, b].astype(f32) * gain).astype(bf16)
            block[a, b, :, ch:] = jnp.concatenate(
                [place, neighbours[a, b].astype(f32), count], axis=1
            ).astype(bf16)


def first_kernel(
    sz, table, wide_in, wide_out, turned_in, turned_out, mixing, readout,
    energy, back, kept, code, atom, sep,
    hot, xt, angular, dist, env, second, second_xt, second_msg, second_radial,
    second_value, second_slope, ang_grad, dist_grad, env_grad, sep_grad, acc, acc_pos,
):
    ch, n = sz.channels, sz.slots
    owned = len(sz.own)
    low, high = bounds_of(sz, table)
    most = jnp.maximum(jnp.max(high).astype(jnp.int32), 1)
    parts = (most + sz.edges - 1) // sz.edges
    in_one, out_one = wide_in[0], wide_out[0]
    code[...] = jnp.full_like(code, -1.0)
    kept[...] = jnp.zeros_like(kept)

    def first_part(part, carry):
        gather_columns(sz, part, table, low, high, code, atom, sep, hot, xt)
        shifted_seps(part, code, sep)
        seps = [sep[part, d] for d in range(3)]
        store_geometry(part, live_rows(code[part]), seps, dist, env, angular)

        def one(cols):
            inputs = [xt[col] for col in cols]
            return layer_forward(
                sz, part, cols, angular, dist, env, atom, in_one, out_one, inputs
            )

        def one_store(col, got):
            kept[col] += got[3]

        loop(sz.inner, 4, one, one_store)
        return carry

    lax.fori_loop(0, parts, first_part, 0)
    rows = [None] * sz.inner
    for col, (a, b) in enumerate(sz.order):
        rows[a * sz.inner_y + b] = invariants(sz, kept[col])
    own_rows = [
        table[(a * sz.outer_y + 1) * n : (a * sz.outer_y + 1 + sz.inner_y) * n, :ch]
        for a in range(1, 1 + sz.inner_x)
    ]
    first_out = three(mm, jnp.concatenate(rows, axis=0), mixing[0])
    first_out = first_out + jnp.concatenate(own_rows, axis=0).astype(f32)
    second[...] = first_out.astype(bf16)

    in_two, out_two = wide_in[1], wide_out[1]
    back_in, back_out = turned_in[1], turned_out[1]
    second_msg[...] = jnp.zeros_like(second_msg)
    every = list(range(owned))

    def second_part(part, carry):
        def second_input(k):
            a, b = sz.own[k]
            window = jnp.concatenate(
                [second[pl.ds(sz.inner_row(a - 1 + d, b - 1), 3 * n), :] for d in range(3)],
                axis=0,
            )
            return mm(window.astype(f32).T.astype(bf16), hot[part, k])

        inputs = [second_input(k) for k in every]
        got = layer_forward(sz, part, every, angular, dist, env, atom, in_two, out_two, inputs)
        for k, (radial, value, slope, message) in zip(every, got):
            second_xt[part, k], second_radial[part, k] = inputs[k], radial
            second_value[part, k], second_slope[part, k] = value, slope
            second_msg[k] += message
        return carry

    lax.fori_loop(0, parts, second_part, 0)
    inv = jnp.concatenate([invariants(sz, second_msg[k]) for k in every], axis=0)
    own_rows = [
        second[(a * sz.inner_y + 1) * n : (a * sz.inner_y + 1 + sz.cols_y) * n, :]
        for a in range(1, 1 + sz.cols_x)
    ]
    out = three(mm, inv, mixing[1]) + jnp.concatenate(own_rows, axis=0).astype(f32)
    gate = sigmoid(out)
    weights = readout[...]
    total = three(nt, jnp.ones((8, ch), f32), out * gate * weights)
    for k, (a, b) in enumerate(sz.own):
        energy[a - 1, b - 1 : b, :] = total[0:1, k * n : (k + 1) * n]
    out_grad = gate * (1.0 + out * (1.0 - gate)) * weights
    cotangents = three(nt, out_grad, mixing[1])
    acc[...] = jnp.zeros_like(acc)
    acc_pos[...] = jnp.zeros_like(acc_pos)
    for a in range(sz.cols_x):
        first = ((a + 1) * sz.inner_y + 1) * n
        acc[first : first + sz.cols_y * n] = out_grad[a * sz.cols_y * n : (a + 1) * sz.cols_y * n]

    def back_part(part, carry):
        got = layer_backward(
            sz, part, every, angular, dist, atom, back_in, back_out,
            [second_radial[part, k] for k in every],
            jnp.concatenate([second_value[part, k] for k in every], axis=1),
            jnp.concatenate([second_slope[part, k] for k in every], axis=1),
            [second_xt[part, k] for k in every],
            [hot[part, k] for k in every],
            [second_msg[k] for k in every],
            [cotangents[k * n : (k + 1) * n] for k in every],
        )
        for k, value in zip(every, got):
            store_grads(sz, k, value, ang_grad, dist_grad, env_grad, acc)
        own_positions(
            sz, part, code, atom, sep, dist, hot, ang_grad, dist_grad, env_grad, sep_grad, acc_pos
        )
        return carry

    lax.fori_loop(0, parts, back_part, 0)
    back[:, :ch] = acc[...].astype(bf16)
    high = acc_pos[...].astype(bf16)
    low = (acc_pos[...] - high.astype(f32)).astype(f32)
    filler = jnp.zeros((acc_pos.shape[0], ch - 16), f32)
    back[:, ch:] = jnp.concatenate([high.astype(f32), low, filler], axis=1).astype(bf16)


def packed_halo(sz, code, target, place):
    rows = len(sz.halo)
    first = len(sz.own)
    row = lax.broadcasted_iota(jnp.int32, (rows, sz.edges), 0)
    at_x, at_y = jnp.zeros_like(row), jnp.zeros_like(row)
    for h, (a, b) in enumerate(sz.halo):
        at_x, at_y = jnp.where(row == h, a, at_x), jnp.where(row == h, b, at_y)
    shape = (sz.edges, sz.edges)
    before = iota(shape, 0) <= iota(shape, 1)
    above = iota((rows, rows), 1) < iota((rows, rows), 0)
    count = jnp.zeros((1, 1), f32)
    for part in range(2):
        codes = code[part, first:].astype(jnp.int32)
        offset = codes >> 4
        step_x = (offset * 11) >> 5
        to_x = at_x + step_x - 2
        to_y = at_y + offset - 3 * step_x - 2
        inside = (to_x >= 0) & (to_x < sz.cols_x) & (to_y >= 0) & (to_y < sz.cols_y)
        flags = (inside & (codes >= 0)).astype(f32)
        wanted = (to_x * sz.cols_y + to_y) * sz.slots + (codes & 15)
        target[part] = flags * wanted.astype(f32)
        flags_bf = flags.astype(bf16)
        running = mm(flags_bf, before.astype(f32).astype(bf16)) - 1.0
        earlier = jnp.sum(mm(above.astype(f32).astype(bf16), flags_bf), axis=1, keepdims=True)
        place[part] = jnp.where(flags > 0.0, running + earlier + count, -1.0)
        count = count + jnp.sum(jnp.sum(flags, axis=1, keepdims=True), axis=0, keepdims=True)
    return (jnp.max(count).astype(jnp.int32) + sz.edges - 1) // sz.edges


def halo_back(
    sz, part, edge_parts, own_turned, atom, sep, gathered, weights, target, place,
    feature_acc, pos_acc,
):
    in_one, out_one, back_in, back_out = weights
    ch, n, lanes = sz.channels, sz.slots, sz.edges
    first = len(sz.own)
    count = len(sz.halo) * n
    wanted = iota((lanes, lanes), 0) + (part * lanes).astype(f32)
    ones, zeros = jnp.ones((1, lanes), f32), jnp.zeros((2, lanes), f32)

    def packed(edge_part, total):
        picks, sides = [], []
        for h in range(len(sz.halo)):
            pick = place[edge_part, pl.ds(h, 1), :] == wanted
            picks.append(pick.astype(f32).astype(bf16))
            rows = jnp.concatenate(
                [sep[edge_part, d, pl.ds(first + h, 1), :] for d in range(3)]
                + [
                    target[edge_part, pl.ds(h, 1), :],
                    atom[edge_part, pl.ds(first + h, 1), :] + float(h * n),
                    ones,
                    zeros,
                ],
                axis=0,
            )
            high = rows.astype(bf16).astype(f32)
            middle = (rows - high).astype(bf16).astype(f32)
            sides.append(
                jnp.concatenate([high, middle, rows - high - middle], axis=0).astype(bf16)
            )
        return total + nt(jnp.concatenate(sides, axis=1), jnp.concatenate(picks, axis=1))

    got = lax.fori_loop(0, edge_parts, packed, jnp.zeros((24, lanes), f32))
    got = got[0:8] + got[8:16] + got[16:24]
    seps = [got[d : d + 1] for d in range(3)]
    target_row, atom_row, valid = got[3:4], got[4:5], got[5:6]
    dist_row, env_row, angular = geometry(valid, seps)
    weighted, value, slope = hidden_rows(sz, dist_row, env_row, in_one)
    radial = mm(out_one, weighted)
    chosen = iota((first * n, lanes), 0) == target_row
    one_hot = jnp.where(chosen, valid, 0.0).astype(bf16)
    xt = mm(own_turned, one_hot)
    sources = jnp.where(iota((count, lanes), 0) == atom_row, valid, 0.0).astype(bf16)
    spread = mm(gathered[...], sources)
    parts = [spread[m * ch : (m + 1) * ch] for m in range(9)]
    vector = angular[1] * parts[1] + angular[2] * parts[2] + angular[3] * parts[3]
    tensor = angular[4] * parts[4]
    for m in range(5, 9):
        tensor = tensor + angular[m] * parts[m]
    product_grad = jnp.concatenate([parts[0], vector, tensor], axis=0)
    _, radial_grad, input_grad = radial_products(sz, product_grad, radial, xt)
    products = [radial[l * ch : (l + 1) * ch] * xt for l in range(3)]
    ang_grad = [None] + [
        jnp.sum(parts[m] * products[1 if m < 4 else 2], axis=0, keepdims=True)
        for m in range(1, 9)
    ]
    dist_grad, env_grad = radial_backward(
        sz, dist_row, radial_grad, value, slope, back_in, back_out
    )
    grads = separation_grads(valid, seps, dist_row, ang_grad, dist_grad, env_grad)
    feature_acc[...] += nt(one_hot, input_grad)
    got = nt(one_hot, stacked_seps(list(grads)))
    pos_acc[...] += got[:, :8] + got[:, 8:]


def second_kernel(
    sz, cotangent, table, kept, code, atom, sep,
    wide_in, wide_out, turned_in, turned_out, mixing,
    feature_grad, forces,
    hot, xt, angular, dist, env, ang_grad, dist_grad, env_grad, sep_grad,
    acc, acc_pos, halo_acc, halo_pos, target, place, gathered,
):
    ch, n = sz.channels, sz.slots
    inv = three(nt, cotangent[:, :ch], mixing[0])
    halo_parts = packed_halo(sz, code, target, place)
    second_used = (jnp.max(code[1]) >= 0.0).astype(jnp.int32)
    edge_parts = 1 + second_used
    in_one, out_one = wide_in[0], wide_out[0]
    back_in, back_out = turned_in[0], turned_out[0]
    owned = len(sz.own)
    every = list(range(owned))
    index = iota((sz.window, sz.edges), 0)
    acc[...] = jnp.zeros_like(acc)
    acc_pos[...] = jnp.zeros_like(acc_pos)
    halo_acc[...] = jnp.zeros_like(halo_acc)
    halo_pos[...] = jnp.zeros_like(halo_pos)

    def inv_rows(a, b):
        row = sz.inner_row(a, b)
        return inv[row : row + n]

    turned = [window_of(sz, table, *place_)[:, :ch].astype(f32).T.astype(bf16) for place_ in sz.own]

    def back_part(part, carry):
        seps = [sep[part, d, :owned] for d in range(3)]
        store_geometry(part, live_rows(code[part, :owned]), seps, dist, env, angular)
        hots = [
            (index == code[part, pl.ds(k, 1), :]).astype(f32).astype(bf16) for k in every
        ]
        for k in every:
            hot[part, k] = hots[k]
        rows = [
            jnp.concatenate([ref[part, pl.ds(k, 1), :] for k in every], axis=1)
            for ref in (dist, env)
        ]
        weighted, value, slope = hidden_rows(sz, *rows, in_one)
        got = layer_backward(
            sz, part, every, angular, dist, atom, back_in, back_out,
            [mm(out_one, weighted[:, k * sz.edges : (k + 1) * sz.edges]) for k in every],
            value, slope,
            [mm(turned[k], hots[k]) for k in every],
            hots,
            [kept[k] for k in every],
            [inv_rows(*sz.own[k]) for k in every],
        )
        for k, value in zip(every, got):
            store_grads(sz, k, value, ang_grad, dist_grad, env_grad, acc)
        own_positions(
            sz, part, code, atom, sep, dist, hot, ang_grad, dist_grad, env_grad, sep_grad, acc_pos
        )
        return carry

    lax.fori_loop(0, edge_parts, back_part, 0)
    halo_grads = [
        message_grads(sz, kept[owned + h], inv_rows(a, b)) for h, (a, b) in enumerate(sz.halo)
    ]
    for m in range(9):
        rows = jnp.concatenate([grads[m] for grads in halo_grads], axis=0)
        gathered[m * ch : (m + 1) * ch, :] = rows.T.astype(bf16)
    own_rows = [
        table[sz.outer_row(a + 2, 2) : sz.outer_row(a + 2, 2) + sz.cols_y * n, :ch]
        for a in range(sz.cols_x)
    ]
    own_turned = jnp.concatenate(own_rows, axis=0).astype(f32).T.astype(bf16)
    weights = (in_one, out_one, back_in, back_out)

    def halo_part(part, carry):
        halo_back(
            sz, part, edge_parts, own_turned, atom, sep, gathered, weights, target, place,
            halo_acc, halo_pos,
        )
        return carry

    lax.fori_loop(0, halo_parts, halo_part, 0)
    for a in range(sz.cols_x):
        inner = sz.inner_row(a + 1, 1)
        rows = sz.cols_y * n
        mine = slice(a * rows, (a + 1) * rows)
        feature_grad[mine] = (
            acc[inner : inner + rows] + cotangent[inner : inner + rows, :ch] + halo_acc[mine]
        )
        extra = cotangent[inner : inner + rows, ch : ch + 16]
        total = acc_pos[inner : inner + rows] + extra[:, :8] + extra[:, 8:] + halo_pos[mine]
        for b in range(sz.cols_y):
            forces[a, :, b, :] = -(total[b * n : (b + 1) * n].T)[:3]


def ring(axis):
    devices = lax.axis_size(axis)
    up = [(i, (i + 1) % devices) for i in range(devices)]
    return up, [(j, i) for i, j in up]


def extended(x, sides):
    for axis, dim in sides:
        up, down = ring(axis)
        length = x.shape[dim]
        last = lax.slice_in_dim(x, length - 2, length, axis=dim)
        initial = lax.slice_in_dim(x, 0, 2, axis=dim)
        before = lax.ppermute(last, axis, up)
        after = lax.ppermute(initial, axis, down)
        x = jnp.concatenate([before, x, after], axis=dim)
    return x


def summed(x, sides):
    total = x.astype(f32)
    for axis, dim in sides:
        up, down = ring(axis)
        length = x.shape[dim]
        sent = total.astype(bf16)
        last = lax.slice_in_dim(sent, length - 2, length, axis=dim)
        initial = lax.slice_in_dim(sent, 0, 2, axis=dim)
        before = lax.ppermute(last, axis, up).astype(f32)
        after = lax.ppermute(initial, axis, down).astype(f32)
        shape = list(x.shape)
        shape[dim] = length - 4
        parts = [before] + ([jnp.zeros(shape, f32)] if length > 4 else []) + [after]
        total = total + jnp.concatenate(parts, axis=dim)
    return total


def shards(
    features, positions, species, neighbours, counts, species_gain, radial_in, radial_out, mixing, readout
):
    cols_x, cols_y, slots, channels = features.shape
    neigh = neighbours.shape[-1]
    basis, hidden = radial_in.shape[1:]
    sz = Sizes(cols_x, cols_y, slots, neigh, channels, basis, hidden)
    vmem = pl.BlockSpec(memory_space=pltpu.VMEM)
    in_hbm = pl.BlockSpec(memory_space=pltpu.HBM)
    params = pltpu.CompilerParams(vmem_limit_bytes=40 * 1024 * 1024)
    given = (features, positions.transpose(0, 2, 1, 3), species, neighbours, counts, species_gain)
    block = pl.pallas_call(
        functools.partial(block_kernel, sz, species_gain.shape[0]),
        out_shape=jax.ShapeDtypeStruct((cols_x, cols_y, slots, 2 * channels), bf16),
        in_specs=[in_hbm] * 6,
        out_specs=vmem,
        scratch_shapes=[pltpu.VMEM(x.shape, x.dtype) for x in given]
        + [pltpu.SemaphoreType.DMA((6,))],
        compiler_params=pltpu.CompilerParams(vmem_limit_bytes=60 * 1024 * 1024),
        name="block_of_atoms",
    )(*given)
    sides = (("gx", 0), ("gy", 1))
    table = extended(block, sides).reshape(-1, 2 * channels)

    inner_atoms = sz.inner * slots
    owned = cols_x * cols_y
    edges = sz.edges
    columns = sz.inner
    grads = [
        pltpu.VMEM((9, owned, edges), f32),
        pltpu.VMEM((owned, edges), f32),
        pltpu.VMEM((owned, edges), f32),
        pltpu.VMEM((3, owned, edges), f32),
    ]
    weights = prepared(radial_in, radial_out, mixing)
    assert slots * neigh <= 2 * edges
    kept_shapes = [
        (columns, sz.window, channels),
        (2, columns, edges),
        (2, columns, edges),
        (2, 3, columns, edges),
    ]

    def edge_scratch(count):
        return [
            pltpu.VMEM((2, owned, sz.window, edges), bf16),
            pltpu.VMEM((count, channels, edges), f32),
            pltpu.VMEM((2, 9, count, edges), f32),
            pltpu.VMEM((2, count, edges), f32),
            pltpu.VMEM((2, count, edges), f32),
        ]

    energy, back, *kept = pl.pallas_call(
        functools.partial(first_kernel, sz),
        out_shape=[
            jax.ShapeDtypeStruct((cols_x, cols_y, slots), f32),
            jax.ShapeDtypeStruct((inner_atoms, 2 * channels), bf16),
        ]
        + [jax.ShapeDtypeStruct(shape, f32) for shape in kept_shapes],
        in_specs=[vmem] * 7,
        out_specs=[vmem] * 6,
        scratch_shapes=edge_scratch(columns)
        + [
            pltpu.VMEM((inner_atoms, channels), bf16),
            pltpu.VMEM((2, owned, channels, edges), f32),
            pltpu.VMEM((owned, sz.window, channels), f32),
            pltpu.VMEM((2, owned, 3 * channels, edges), f32),
            pltpu.VMEM((2, owned, hidden, edges), f32),
            pltpu.VMEM((2, owned, hidden, edges), f32),
        ]
        + grads
        + [pltpu.VMEM((inner_atoms, channels), f32), pltpu.VMEM((inner_atoms, 8), f32)],
        compiler_params=params,
        name="forward_and_second_back",
    )(table, *weights, readout.reshape(1, -1))

    back = back.reshape(sz.inner_x, sz.inner_y, slots, 2 * channels)
    cotangent = summed(back, sides).reshape(inner_atoms, 2 * channels)
    feature_grad, forces = pl.pallas_call(
        functools.partial(second_kernel, sz),
        out_shape=(
            jax.ShapeDtypeStruct((owned * slots, channels), f32),
            jax.ShapeDtypeStruct((cols_x, 3, cols_y, slots), f32),
        ),
        in_specs=[vmem] * 11,
        out_specs=(vmem,) * 2,
        scratch_shapes=edge_scratch(owned)
        + grads
        + [
            pltpu.VMEM((rows, width), f32)
            for rows in (inner_atoms, owned * slots)
            for width in (channels, 8)
        ]
        + [
            pltpu.VMEM((2, len(sz.halo), edges), f32),
            pltpu.VMEM((2, len(sz.halo), edges), f32),
            pltpu.VMEM((9 * channels, len(sz.halo) * slots), bf16),
        ],
        compiler_params=params,
        name="first_back",
    )(cotangent, table, *kept, *weights)
    return (
        energy,
        forces.transpose(0, 2, 1, 3),
        feature_grad.reshape(cols_x, cols_y, slots, channels),
    )


def solution(mesh):
    placed = (
        P("gx", "gy", None, None),
        P("gx", "gy", None, None),
        P("gx", "gy", None),
        P("gx", "gy", None, None),
        P("gx", "gy", None),
        P(),
        P(),
        P(),
        P(),
        P(),
    )
    return jax.shard_map(
        shards,
        mesh=mesh,
        in_specs=placed,
        out_specs=(P("gx", "gy", None), P("gx", "gy", None, None), P("gx", "gy", None, None)),
        check_vma=False,
    )
```

time: 54.2 us -> 50.1 us (0.924)
  Pallas kernels: 22.2 us -> 18.1 us
    pallas_call x1, Pallas kernels: 7.61 us -> 5.13 us  [shards(): pl.pallas_call(functools.partial(second_kernel, sz), out_shape=(jax.Shape...]
    pallas_call x1, Pallas kernels: 12.9 us -> 11.3 us  [shards(): pl.pallas_call(functools.partial(first_kernel, sz), out_shape=[jax.ShapeD...]
  transfers between devices with their start and end apart: 8 -> 8, of which waited for: 6 -> 6; matrix products, arithmetic and copies ran while one was open for 6% -> 7% of each run, Pallas kernels for 0% -> 0%
where the time goes in v3:
time: 50.1 us; the launch traced here: 49.2 us
  Pallas kernels  18.1 us (36%)
  waiting for transfers between devices  16.4 us (33%)
  starting transfers between devices  10.5 us (21%)
  other arithmetic  3.04 us (6%)
  between operations  0.76 us (2%)
    pallas_call x1, Pallas kernels, shards(): pl.pallas_call(functools.partial(first_kernel, sz), out_shape=[jax.ShapeD...  11.3 us
    ppermute x2, waiting for transfers between devices, extended(): before = lax.ppermute(last, axis, up)  6.46 us
    ppermute x2, starting transfers between devices, extended(): after = lax.ppermute(initial, axis, down)  6.09 us
    ppermute x2, waiting for transfers between devices, summed(): before = lax.ppermute(last, axis, up).astype(f32)  6.02 us
    pallas_call x1, Pallas kernels, shards(): pl.pallas_call(functools.partial(second_kernel, sz), out_shape=(jax.Shape...  5.13 us
    ppermute x2, starting transfers between devices, summed(): after = lax.ppermute(initial, axis, down).astype(f32)  3.19 us
    ppermute x2, waiting for transfers between devices, summed(): after = lax.ppermute(initial, axis, down).astype(f32)  2.24 us
    pallas_call x1, Pallas kernels, shards(): pl.pallas_call(functools.partial(block_kernel, sz, species_gain.shape[0])...  1.72 us
  transfers between devices with their start and end apart: 8, of which 6 were waited for; matrix products, arithmetic and copies ran while one was open for 7% of the time, Pallas kernels for 0%

profile of v3, /device:TPU:0, one launch (start us, length us, event | category | flops | bytes accessed | tf_op | source)
XLA Modules:
  0.0 49.2 jit_solution(15550826560090756330)
XLA Ops:
  0.6 1.7 %block_of_atoms.1 = bf16[2,2,16,256]{3,2,1,0:T(8,128)(2,1)} custom-call(bf16[2,2,16,128]{3,2,1,0:T(8,128)(2,1)} %refs_0_.1, f32[2,3,2,16]{3,2,1,0:T(2,128)} %bitcast.32, s32[2,2,16]{2,1,0:T(2,128)} %refs_2_.1, s32[2,2,16,32]{3,2,1,0:T(8,128)} %refs_3_.1, s32[2,2,16]{2,1,0:T(2,128)} %refs_4_.1, f32[6,128]{1,0:T(8,128)} %refs_5_.1), custom_call_target="tpu_custom_call" | custom-call | tf_op jit(solution)/shard_map/block_of_atoms/pallas_call | solution.py:807
  2.4 6.0 %collective-permute-start.1 = (bf16[2,2,16,256]{3,2,1,0:T(8,128)(2,1)}, bf16[2,2,16,256]{3,2,1,0:T(8,128)(2,1)S(1)}, u32[]{:S(2)}, u32[]{:S(2)}) collective-permute-start(bf16[2,2,16,256]{3,2,1,0:T(8,128)(2,1)} %block_of_atoms.1), channel_id=1, source_target_pairs={{4,0},{8,4},{12,8},{16,12},{20,16},{24,20},{28,24},{0,28},{5,1},{9... | collective-permute-start | bytes 98312 | tf_op jit(solution)/shard_map/ppermute | solution.py:774
  8.4 0.0 collective-permute-start
  8.4 0.7 %reduce-precision_convert_fusion.2 = (bf16[2,8,64]{2,1,0:T(8,128)(2,1)S(1)}, bf16[2,8,64]{2,1,0:T(8,128)(2,1)S(1)}) fusion(f32[2,8,64]{2,1,0:T(8,128)} %param.16), kind=kLoop, calls=%fused_computation.19 | loop fusion | flops 4096 | bytes 8192 | tf_op jit(solution)/shard_map/convert.13
  9.1 1.0 %reduce-precision_convert_fusion.1 = (bf16[2,64,384]{2,1,0:T(8,128)(2,1)S(1)}, bf16[2,64,384]{2,1,0:T(8,128)(2,1)S(1)}) fusion(f32[2,64,384]{2,1,0:T(8,128)} %param.17), kind=kLoop, calls=%fused_computation.7 | loop fusion | flops 196608 | bytes 393216 | tf_op jit(solution)/shard_map/convert.10
  10.1 1.1 %fusion.3 = (bf16[2,1,384,128]{3,2,1,0:T(8,128)(2,1)S(1)}, bf16[2,1,384,128]{3,2,1,0:T(8,128)(2,1)S(1)}) fusion(f32[2,384,128]{2,1,0:T(8,128)} %param.18), kind=kLoop, calls=%fused_computation.13 | loop fusion | flops 393216 | bytes 786432 | tf_op jit(solution)/shard_map/stack | solution.py:51
  11.1 0.0 copy-start.1
  11.1 0.1 pad.14.clone
  11.3 0.0 copy-start
  11.3 0.1 maximum_bitcast_fusion.1
  11.4 0.1 copy.14.wide_in
  11.5 0.2 copy.15.wide_out
  11.7 0.0 collective-permute-done.1
  11.7 3.5 %collective-permute-done = bf16[2,2,16,256]{3,2,1,0:T(8,128)(2,1)S(1)} collective-permute-done((bf16[2,2,16,256]{3,2,1,0:T(8,128)(2,1)}, bf16[2,2,16,256]{3,2,1,0:T(8,128)(2,1)S(1)}, u32[]{:S(2)}, u32[]{:S(2)}) %collective-permute-start) | collective-permute-done | bytes 32800 | tf_op jit(solution)/shard_map/ppermute | solution.py:773
  15.2 0.0 copy-done.1
  15.2 0.1 collective-permute-start.3
  15.3 0.5 %collective-permute-start.2 = (bf16[6,2,16,256]{3,2,1,0:T(8,128)(2,1)S(1)}, bf16[6,2,16,256]{3,2,1,0:T(8,128)(2,1)S(1)}, u32[]{:S(2)}, u32[]{:S(2)}) collective-permute-start(bf16[6,2,16,256]{3,2,1,0:T(8,128)(2,1)S(1)} %pad_maximum_fusion.3), channel_id=1, source_target_pairs={{0,1},{1,2},{2,3},{3,0},{4,5},{5,6},{6,7},{7,4},{8,9},{9,10},{10,1... | collective-permute-start | bytes 294920 | tf_op jit(solution)/shard_map/ppermute | solution.py:773
  15.8 1.7 %collective-permute-done.3 = bf16[6,2,16,256]{3,2,1,0:T(8,128)(2,1)S(1)} collective-permute-done((bf16[6,2,16,256]{3,2,1,0:T(8,128)(2,1)S(1)}, bf16[6,2,16,256]{3,2,1,0:T(8,128)(2,1)S(1)}, u32[]{:S(2)}, u32[]{:S(2)}) %collective-permute-start.3) | collective-permute-done | bytes 98336 | tf_op jit(solution)/shard_map/ppermute | solution.py:774
  17.5 2.9 %collective-permute-done.2 = bf16[6,2,16,256]{3,2,1,0:T(8,128)(2,1)S(1)} collective-permute-done((bf16[6,2,16,256]{3,2,1,0:T(8,128)(2,1)S(1)}, bf16[6,2,16,256]{3,2,1,0:T(8,128)(2,1)S(1)}, u32[]{:S(2)}, u32[]{:S(2)}) %collective-permute-start.2) | collective-permute-done | bytes 98336 | tf_op jit(solution)/shard_map/ppermute | solution.py:773
  20.5 0.0 copy-done
  20.5 11.3 %forward_and_second_back.1 = (f32[2,2,16]{2,1,0:T(2,128)}, bf16[256,256]{1,0:T(8,128)(2,1)S(1)}, f32[16,144,128]{2,1,0:T(8,128)S(1)}, f32[2,16,256]{2,1,0:T(8,12...) custom-call(bf16[576,256]{1,0:T(8,128)(2,1)S(1)} %bitcast.26, bf16[2,64,32]{2,1,0:T(8,128)(2,1)S(1)} %copy.14.wide_in, ...), custom_call_target="tpu_custom_call" | custom-call | tf_op jit(solution)/shard_map/forward_and_second_back/pallas_call | solution.py:848
  31.8 1.5 %collective-permute-start.5 = (bf16[2,4,16,256]{3,2,1,0:T(8,128)(2,1)S(1)}, bf16[2,4,16,256]{3,2,1,0:T(8,128)(2,1)S(1)}, u32[]{:S(2)}, u32[]{:S(2)}) collective-permute-start(bf16[2,4,16,256]{3,2,1,0:T(8,128)(2,1)S(1)} %bitcast.31), channel_id=1, source_target_pairs={{4,0},{8,4},{12,8},{16,12},{20,16},{24,20},{28,24},{0,28},{5,1},{9... | collective-permute-start | bytes 196616 | tf_op jit(solution)/shard_map/ppermute | solution.py:788
  33.2 0.6 %collective-permute-start.4 = (bf16[2,4,16,256]{3,2,1,0:T(8,128)(2,1)S(1)}, bf16[2,4,16,256]{3,2,1,0:T(8,128)(2,1)S(1)}, u32[]{:S(2)}, u32[]{:S(2)}) collective-permute-start(bf16[2,4,16,256]{3,2,1,0:T(8,128)(2,1)S(1)} %bitcast.30), channel_id=1, source_target_pairs={{0,4},{4,8},{8,12},{12,16},{16,20},{20,24},{24,28},{28,0},{1,5},{5... | collective-permute-start | bytes 196616 | tf_op jit(solution)/shard_map/ppermute | solution.py:787
  33.8 2.2 %collective-permute-done.5 = bf16[2,4,16,256]{3,2,1,0:T(8,128)(2,1)S(1)} collective-permute-done((bf16[2,4,16,256]{3,2,1,0:T(8,128)(2,1)S(1)}, bf16[2,4,16,256]{3,2,1,0:T(8,128)(2,1)S(1)}, u32[]{:S(2)}, u32[]{:S(2)}) %collective-permute-start.5) | collective-permute-done | bytes 65568 | tf_op jit(solution)/shard_map/ppermute | solution.py:788
  36.1 4.1 %collective-permute-done.4 = bf16[2,4,16,256]{3,2,1,0:T(8,128)(2,1)S(1)} collective-permute-done((bf16[2,4,16,256]{3,2,1,0:T(8,128)(2,1)S(1)}, bf16[2,4,16,256]{3,2,1,0:T(8,128)(2,1)S(1)}, u32[]{:S(2)}, u32[]{:S(2)}) %collective-permute-start.4) | collective-permute-done | bytes 65568 | tf_op jit(solution)/shard_map/ppermute | solution.py:787
  40.2 0.1 collective-permute-start.6
  40.3 1.7 %collective-permute-start.7 = (bf16[4,2,16,256]{3,2,1,0:T(8,128)(2,1)S(1)}, bf16[4,2,16,256]{3,2,1,0:T(8,128)(2,1)S(1)}, u32[]{:S(2)}, u32[]{:S(2)}) collective-permute-start(bf16[4,2,16,256]{3,2,1,0:T(8,128)(2,1)S(1)} %get-tuple-element.24), channel_id=1, source_target_pairs={{1,0},{2,1},{3,2},{0,3},{5,4},{6,5},{7,6},{4,7},{9,8},{10,9},{11,1... | collective-permute-start | bytes 196616 | tf_op jit(solution)/shard_map/ppermute | solution.py:788
  42.1 1.9 %collective-permute-done.6 = bf16[4,2,16,256]{3,2,1,0:T(8,128)(2,1)S(1)} collective-permute-done((bf16[4,2,16,256]{3,2,1,0:T(8,128)(2,1)S(1)}, bf16[4,2,16,256]{3,2,1,0:T(8,128)(2,1)S(1)}, u32[]{:S(2)}, u32[]{:S(2)}) %collective-permute-start.6) | collective-permute-done | bytes 65568 | tf_op jit(solution)/shard_map/ppermute | solution.py:787
  44.0 0.0 collective-permute-done.7
  44.0 0.1 convert_add_fusion.cotangent
  44.1 5.1 %first_back.1 = (f32[64,128]{1,0:T(8,128)}, f32[2,3,2,16]{3,2,1,0:T(2,128)}) custom-call(f32[256,256]{1,0:T(8,128)S(1)} %convert_add_fusion.cotangent, bf16[576,256]{1,0:T(8,128)(2,1)S(1)} %bitcast.27, f32[16,144,128]{2,1,0:T(8,128)S(1)} %get-tuple-element.13.kept, f32[2,16,256]{2,1,0:T(8,128)S(1)} %get-tuple-element.14.code, ...), custom_call_target="tpu_custom_call" | custom-call | tf_op jit(solution)/shard_map/first_back/pallas_call | solution.py:874
  (11 shorter events, 0.2 us)
Async XLA Ops:
  2.4 9.3 %collective-permute-start.1 = (bf16[2,2,16,256]{3,2,1,0:T(8,128)(2,1)}, bf16[2,2,16,256]{3,2,1,0:T(8,128)(2,1)S(1)}, u32[]{:S(2)}, u32[]{:S(2)}) collective-permute-start(bf16[2,2,16,256]{3,2,1,0:T(8,128)(2,1)} %block_of_atoms.1), channel_id=1, source_target_pairs={{4,0},{8,4},{12,8},{16,12},{20,16},{24,20},{28,24},{0,28},{5,1},{9... | collective-permute-start | bytes 98312 | tf_op jit(solution)/shard_map/ppermute | solution.py:774
  8.4 6.8 %collective-permute-start = (bf16[2,2,16,256]{3,2,1,0:T(8,128)(2,1)}, bf16[2,2,16,256]{3,2,1,0:T(8,128)(2,1)S(1)}, u32[]{:S(2)}, u32[]{:S(2)}) collective-permute-start(bf16[2,2,16,256]{3,2,1,0:T(8,128)(2,1)} %block_of_atoms.1), channel_id=1, source_target_pairs={{0,4},{4,8},{8,12},{12,16},{16,20},{20,24},{24,28},{28,0},{1,5},{5... | collective-permute-start | bytes 98312 | tf_op jit(solution)/shard_map/ppermute | solution.py:773
  11.1 4.1 %copy-start.1 = (bf16[2,2,16,256]{3,2,1,0:T(8,128)(2,1)S(1)}, bf16[2,2,16,256]{3,2,1,0:T(8,128)(2,1)}, u32[]{:S(2)}) copy-start(bf16[2,2,16,256]{3,2,1,0:T(8,128)(2,1)} %block_of_atoms.1) | copy-start | bytes 98308
  11.3 9.2 %copy-start = (f32[128]{0:T(128)S(1)}, f32[128]{0:T(128)}, u32[]{:S(2)}) copy-start(f32[128]{0:T(128)} %param.19) | copy-start | bytes 1540
  15.2 2.3 %collective-permute-start.3 = (bf16[6,2,16,256]{3,2,1,0:T(8,128)(2,1)S(1)}, bf16[6,2,16,256]{3,2,1,0:T(8,128)(2,1)S(1)}, u32[]{:S(2)}, u32[]{:S(2)}) collective-permute-start(bf16[6,2,16,256]{3,2,1,0:T(8,128)(2,1)S(1)} %pad_maximum_fusion.3), channel_id=1, source_target_pairs={{1,0},{2,1},{3,2},{0,3},{5,4},{6,5},{7,6},{4,7},{9,8},{10,9},{11,1... | collective-permute-start | bytes 294920 | tf_op jit(solution)/shard_map/ppermute | solution.py:774
  15.3 5.1 %collective-permute-start.2 = (bf16[6,2,16,256]{3,2,1,0:T(8,128)(2,1)S(1)}, bf16[6,2,16,256]{3,2,1,0:T(8,128)(2,1)S(1)}, u32[]{:S(2)}, u32[]{:S(2)}) collective-permute-start(bf16[6,2,16,256]{3,2,1,0:T(8,128)(2,1)S(1)} %pad_maximum_fusion.3), channel_id=1, source_target_pairs={{0,1},{1,2},{2,3},{3,0},{4,5},{5,6},{6,7},{7,4},{8,9},{9,10},{10,1... | collective-permute-start | bytes 294920 | tf_op jit(solution)/shard_map/ppermute | solution.py:773
  31.8 4.3 %collective-permute-start.5 = (bf16[2,4,16,256]{3,2,1,0:T(8,128)(2,1)S(1)}, bf16[2,4,16,256]{3,2,1,0:T(8,128)(2,1)S(1)}, u32[]{:S(2)}, u32[]{:S(2)}) collective-permute-start(bf16[2,4,16,256]{3,2,1,0:T(8,128)(2,1)S(1)} %bitcast.31), channel_id=1, source_target_pairs={{4,0},{8,4},{12,8},{16,12},{20,16},{24,20},{28,24},{0,28},{5,1},{9... | collective-permute-start | bytes 196616 | tf_op jit(solution)/shard_map/ppermute | solution.py:788
  33.2 7.0 %collective-permute-start.4 = (bf16[2,4,16,256]{3,2,1,0:T(8,128)(2,1)S(1)}, bf16[2,4,16,256]{3,2,1,0:T(8,128)(2,1)S(1)}, u32[]{:S(2)}, u32[]{:S(2)}) collective-permute-start(bf16[2,4,16,256]{3,2,1,0:T(8,128)(2,1)S(1)} %bitcast.30), channel_id=1, source_target_pairs={{0,4},{4,8},{8,12},{12,16},{16,20},{20,24},{24,28},{28,0},{1,5},{5... | collective-permute-start | bytes 196616 | tf_op jit(solution)/shard_map/ppermute | solution.py:787
  40.2 3.7 %collective-permute-start.6 = (bf16[4,2,16,256]{3,2,1,0:T(8,128)(2,1)S(1)}, bf16[4,2,16,256]{3,2,1,0:T(8,128)(2,1)S(1)}, u32[]{:S(2)}, u32[]{:S(2)}) collective-permute-start(bf16[4,2,16,256]{3,2,1,0:T(8,128)(2,1)S(1)} %get-tuple-element.23), channel_id=1, source_target_pairs={{0,1},{1,2},{2,3},{3,0},{4,5},{5,6},{6,7},{7,4},{8,9},{9,10},{10,1... | collective-permute-start | bytes 196616 | tf_op jit(solution)/shard_map/ppermute | solution.py:787
  40.3 3.7 %collective-permute-start.7 = (bf16[4,2,16,256]{3,2,1,0:T(8,128)(2,1)S(1)}, bf16[4,2,16,256]{3,2,1,0:T(8,128)(2,1)S(1)}, u32[]{:S(2)}, u32[]{:S(2)}) collective-permute-start(bf16[4,2,16,256]{3,2,1,0:T(8,128)(2,1)S(1)} %get-tuple-element.24), channel_id=1, source_target_pairs={{1,0},{2,1},{3,2},{0,3},{5,4},{6,5},{7,6},{4,7},{9,8},{10,9},{11,1... | collective-permute-start | bytes 196616 | tf_op jit(solution)/shard_map/ppermute | solution.py:788

commit v4 on v3

--- a/solution.py
+++ b/solution.py
@@ -14,6 +14,7 @@
 f32 = jnp.float32
 bf16 = jnp.bfloat16
 code_lane = 32
+count_lane = 31
 part_lanes = 256
 
 
@@ -111,6 +112,11 @@
     )
 
 
+def inner_window(sz, table, a, b):
+    rows = [sz.inner_row(a - 1 + d, b - 1) for d in range(3)]
+    return jnp.concatenate([table[row : row + 3 * sz.slots, :] for row in rows], axis=0)
+
+
 def iota(shape, dim):
     return lax.broadcasted_iota(jnp.int32, shape, dim).astype(f32)
 
@@ -124,9 +130,8 @@
     right = lax.broadcasted_iota(jnp.int32, shape, 1)
     earlier = (left // n == right // n) & (right < left)
     sums = mm(earlier.astype(f32).astype(bf16), metas)
-    lane = code_lane + sz.neigh
-    low = sums[:, lane : lane + 1]
-    return low, low + metas[:, lane : lane + 1].astype(f32)
+    low = sums[:, count_lane : count_lane + 1]
+    return low, low + metas[:, count_lane : count_lane + 1].astype(f32)
 
 
 def gather_columns(sz, part, table, low, high, code, atom, sep, hot, xt):
@@ -226,10 +231,11 @@
 def layer_forward(sz, part, cols, angular, dist, env, atom, weight_in, weight_out, inputs):
     rows = [jnp.concatenate([ref[part, pl.ds(c, 1), :] for c in cols], axis=1) for ref in (dist, env)]
     weighted, value, slope = hidden_rows(sz, *rows, weight_in)
+    radials = mm(weight_out, weighted)
     out = []
     for k, (col, xt) in enumerate(zip(cols, inputs)):
         span = slice(k * sz.edges, (k + 1) * sz.edges)
-        radial = mm(weight_out, weighted[:, span])
+        radial = radials[:, span]
         message = column_messages(sz, part, col, angular, atom, radial, xt)
         out.append((radial, value[:, span], slope[:, span], message))
     return out
@@ -237,18 +243,18 @@
 
 def column_messages(sz, part, col, angular, atom, radial, xt):
     ch, n = sz.channels, sz.slots
-    product = [(radial[l * ch : (l + 1) * ch] * xt).astype(bf16) for l in range(3)]
+    product = (radial * jnp.concatenate([xt] * 3, axis=0)).astype(bf16)
     at = atoms_at(sz, atom, part, col)
-    scalar = nt(product[0], at.astype(bf16)).T
     blocks = jnp.concatenate(block_rows(angular, part, col, at), axis=0)
     high = blocks.astype(bf16).astype(f32)
-    both = jnp.concatenate([high, blocks - high], axis=0).astype(bf16)
-    count = 8 * n
-    vector, tensor = nt(product[1], both), nt(product[2], both)
-    vector = vector[:, :count] + vector[:, count:]
-    tensor = tensor[:, :count] + tensor[:, count:]
-    lane = lax.broadcasted_iota(jnp.int32, (ch, count), 1)
-    return jnp.concatenate([scalar, jnp.where(lane < 3 * n, vector, tensor).T], axis=0)
+    low = blocks - high
+    out = [nt(at.astype(bf16), product[:ch])]
+    for l, rows in ((1, slice(0, 3 * n)), (2, slice(3 * n, 8 * n))):
+        both = jnp.concatenate([high[rows], low[rows]], axis=0).astype(bf16)
+        got = nt(both, product[l * ch : (l + 1) * ch])
+        count = got.shape[0] // 2
+        out.append(got[:count] + got[count:])
+    return jnp.concatenate(out, axis=0)
 
 
 def invariants(sz, message):
@@ -435,10 +441,10 @@
     above, below = jnp.zeros((24, ch), f32), jnp.zeros((8 - kinds, ch), f32)
     parts = [jnp.concatenate([above, part, below], axis=0).astype(bf16) for part in parts]
     kind = lax.broadcasted_iota(jnp.int32, (8, n), 0)
-    tail_lane = lax.broadcasted_iota(jnp.int32, (n, ch - code_lane - sz.neigh), 1)
     lane = lax.broadcasted_iota(jnp.int32, (n, code_lane), 1)
     gap = jnp.zeros((5, n), f32)
     for a in range(sz.cols_x):
+        sides = []
         for b in range(sz.cols_y):
             atoms = positions[a, :, b, :]
             high = atoms.astype(bf16).astype(f32)
@@ -450,22 +456,33 @@
             turned = jnp.concatenate(rows, axis=0).T
             picked = jnp.where((lane >= 24) & (lane < 24 + kinds), turned, 0.0).astype(bf16)
             gain = mm(picked, parts[0]) + mm(picked, parts[1]) + mm(picked, parts[2])
-            place = jnp.where(lane < 24, turned, 0.0)
-            count = jnp.where(tail_lane == 0, turned[:, 31:32], 0.0)
-            block[a, b, :, :ch] = (features[a, b].astype(f32) * gain).astype(bf16)
-            block[a, b, :, ch:] = jnp.concatenate(
-                [place, neighbours[a, b].astype(f32), count], axis=1
-            ).astype(bf16)
+            place = jnp.where((lane < 24) | (lane == count_lane), turned, 0.0)
+            sides.append(jnp.concatenate([place, neighbours[a, b].astype(f32)], axis=1))
+            block[a, b] = (features[a, b].astype(f32) * gain).astype(bf16)
+        block[a, sz.cols_y] = jnp.concatenate(sides, axis=1).astype(bf16)
+
+
+def fill_table(sz, strips, table):
+    ch, n = sz.channels, sz.slots
+    for a in range(sz.cols_x + 4):
+        for k, strip in enumerate(strips):
+            meta = strip[a, sz.cols_y].astype(f32)
+            for b in range(sz.cols_y):
+                row = sz.outer_row(a, k * sz.cols_y + b)
+                mine = meta if b == 0 else pltpu.roll(meta, ch - b * 2 * code_lane, 1)
+                table[row : row + n, :ch] = strip[a, b]
+                table[row : row + n, ch:] = mine.astype(bf16)
 
 
 def first_kernel(
-    sz, table, wide_in, wide_out, turned_in, turned_out, mixing, readout,
-    energy, back, kept, code, atom, sep,
+    sz, before, middle, after, wide_in, wide_out, turned_in, turned_out, mixing, readout,
+    energy, back, kept, code, atom, sep, inputs_kept, table,
     hot, xt, angular, dist, env, second, second_xt, second_msg, second_radial,
     second_value, second_slope, ang_grad, dist_grad, env_grad, sep_grad, acc, acc_pos,
 ):
     ch, n = sz.channels, sz.slots
     owned = len(sz.own)
+    fill_table(sz, (before, middle, after), table)
     low, high = bounds_of(sz, table)
     most = jnp.maximum(jnp.max(high).astype(jnp.int32), 1)
     parts = (most + sz.edges - 1) // sz.edges
@@ -488,7 +505,7 @@
         def one_store(col, got):
             kept[col] += got[3]
 
-        loop(sz.inner, 4, one, one_store)
+        loop(sz.inner, 8, one, one_store)
         return carry
 
     lax.fori_loop(0, parts, first_part, 0)
@@ -500,7 +517,8 @@
         for a in range(1, 1 + sz.inner_x)
     ]
     first_out = three(mm, jnp.concatenate(rows, axis=0), mixing[0])
-    first_out = first_out + jnp.concatenate(own_rows, axis=0).astype(f32)
+    inputs_kept[...] = jnp.concatenate(own_rows, axis=0)
+    first_out = first_out + inputs_kept[...].astype(f32)
     second[...] = first_out.astype(bf16)
 
     in_two, out_two = wide_in[1], wide_out[1]
@@ -510,11 +528,7 @@
 
     def second_part(part, carry):
         def second_input(k):
-            a, b = sz.own[k]
-            window = jnp.concatenate(
-                [second[pl.ds(sz.inner_row(a - 1 + d, b - 1), 3 * n), :] for d in range(3)],
-                axis=0,
-            )
+            window = inner_window(sz, second, *sz.own[k])
             return mm(window.astype(f32).T.astype(bf16), hot[part, k])
 
         inputs = [second_input(k) for k in every]
@@ -564,11 +578,16 @@
         return carry
 
     lax.fori_loop(0, parts, back_part, 0)
-    back[:, :ch] = acc[...].astype(bf16)
-    high = acc_pos[...].astype(bf16)
-    low = (acc_pos[...] - high.astype(f32)).astype(f32)
-    filler = jnp.zeros((acc_pos.shape[0], ch - 16), f32)
-    back[:, ch:] = jnp.concatenate([high.astype(f32), low, filler], axis=1).astype(bf16)
+    for a in range(sz.inner_x):
+        places = []
+        for b in range(sz.inner_y):
+            row = sz.inner_row(a, b)
+            back[a, b + (b >= 2)] = acc[row : row + n].astype(bf16)
+            full = acc_pos[row : row + n]
+            high = full.astype(bf16).astype(f32)
+            places += [high, full - high]
+        filler = jnp.zeros((n, ch - 16 * sz.inner_y), f32)
+        back[a, 2] = jnp.concatenate(places + [filler], axis=1).astype(bf16)
 
 
 def packed_halo(sz, code, target, place):
@@ -667,14 +686,20 @@
 
 
 def second_kernel(
-    sz, cotangent, table, kept, code, atom, sep,
+    sz, total, before, after, kept, code, atom, sep, table,
     wide_in, wide_out, turned_in, turned_out, mixing,
     feature_grad, forces,
     hot, xt, angular, dist, env, ang_grad, dist_grad, env_grad, sep_grad,
     acc, acc_pos, halo_acc, halo_pos, target, place, gathered,
 ):
     ch, n = sz.channels, sz.slots
-    inv = three(nt, cotangent[:, :ch], mixing[0])
+    cells = []
+    for a in range(sz.inner_x):
+        for b in range(sz.inner_y):
+            far = before[a, b + 1] if b < 2 else after[a, b - 2]
+            cells.append(total[a, b + (b >= 2)] + far.astype(f32))
+    cotangent = jnp.concatenate(cells, axis=0)
+    inv = three(nt, cotangent, mixing[0])
     halo_parts = packed_halo(sz, code, target, place)
     second_used = (jnp.max(code[1]) >= 0.0).astype(jnp.int32)
     edge_parts = 1 + second_used
@@ -692,7 +717,7 @@
         row = sz.inner_row(a, b)
         return inv[row : row + n]
 
-    turned = [window_of(sz, table, *place_)[:, :ch].astype(f32).T.astype(bf16) for place_ in sz.own]
+    turned = [inner_window(sz, table, a, b).astype(f32).T.astype(bf16) for a, b in sz.own]
 
     def back_part(part, carry):
         seps = [sep[part, d, :owned] for d in range(3)]
@@ -707,9 +732,10 @@
             for ref in (dist, env)
         ]
         weighted, value, slope = hidden_rows(sz, *rows, in_one)
+        radials = mm(out_one, weighted)
         got = layer_backward(
             sz, part, every, angular, dist, atom, back_in, back_out,
-            [mm(out_one, weighted[:, k * sz.edges : (k + 1) * sz.edges]) for k in every],
+            [radials[:, k * sz.edges : (k + 1) * sz.edges] for k in every],
             value, slope,
             [mm(turned[k], hots[k]) for k in every],
             hots,
@@ -731,7 +757,7 @@
         rows = jnp.concatenate([grads[m] for grads in halo_grads], axis=0)
         gathered[m * ch : (m + 1) * ch, :] = rows.T.astype(bf16)
     own_rows = [
-        table[sz.outer_row(a + 2, 2) : sz.outer_row(a + 2, 2) + sz.cols_y * n, :ch]
+        table[sz.inner_row(a + 1, 1) : sz.inner_row(a + 1, 1) + sz.cols_y * n, :]
         for a in range(sz.cols_x)
     ]
     own_turned = jnp.concatenate(own_rows, axis=0).astype(f32).T.astype(bf16)
@@ -750,12 +776,16 @@
         rows = sz.cols_y * n
         mine = slice(a * rows, (a + 1) * rows)
         feature_grad[mine] = (
-            acc[inner : inner + rows] + cotangent[inner : inner + rows, :ch] + halo_acc[mine]
+            acc[inner : inner + rows] + cotangent[inner : inner + rows] + halo_acc[mine]
         )
-        extra = cotangent[inner : inner + rows, ch : ch + 16]
-        total = acc_pos[inner : inner + rows] + extra[:, :8] + extra[:, 8:] + halo_pos[mine]
+        moved = acc_pos[inner : inner + rows] + halo_pos[mine]
         for b in range(sz.cols_y):
-            forces[a, :, b, :] = -(total[b * n : (b + 1) * n].T)[:3]
+            lane = 16 * (b + 1)
+            far, start = (before[a + 1, 0], 16 * (b + 3)) if b < 1 else (after[a + 1, 2], 16 * (b - 1))
+            both = total[a + 1, 2][:, lane : lane + 16]
+            both = both + far.astype(f32)[:, start : start + 16]
+            place_grad = moved[b * n : (b + 1) * n] + both[:, :8] + both[:, 8:]
+            forces[a, :, b, :] = -(place_grad.T)[:3]
 
 
 def ring(axis):
@@ -764,33 +794,9 @@
     return up, [(j, i) for i, j in up]
 
 
-def extended(x, sides):
-    for axis, dim in sides:
-        up, down = ring(axis)
-        length = x.shape[dim]
-        last = lax.slice_in_dim(x, length - 2, length, axis=dim)
-        initial = lax.slice_in_dim(x, 0, 2, axis=dim)
-        before = lax.ppermute(last, axis, up)
-        after = lax.ppermute(initial, axis, down)
-        x = jnp.concatenate([before, x, after], axis=dim)
-    return x
-
-
-def summed(x, sides):
-    total = x.astype(f32)
-    for axis, dim in sides:
-        up, down = ring(axis)
-        length = x.shape[dim]
-        sent = total.astype(bf16)
-        last = lax.slice_in_dim(sent, length - 2, length, axis=dim)
-        initial = lax.slice_in_dim(sent, 0, 2, axis=dim)
-        before = lax.ppermute(last, axis, up).astype(f32)
-        after = lax.ppermute(initial, axis, down).astype(f32)
-        shape = list(x.shape)
-        shape[dim] = length - 4
-        parts = [before] + ([jnp.zeros(shape, f32)] if length > 4 else []) + [after]
-        total = total + jnp.concatenate(parts, axis=dim)
-    return total
+def both_ways(first, last, axis):
+    up, down = ring(axis)
+    return lax.ppermute(last, axis, up), lax.ppermute(first, axis, down)
 
 
 def shards(
@@ -806,7 +812,7 @@
     given = (features, positions.transpose(0, 2, 1, 3), species, neighbours, counts, species_gain)
     block = pl.pallas_call(
         functools.partial(block_kernel, sz, species_gain.shape[0]),
-        out_shape=jax.ShapeDtypeStruct((cols_x, cols_y, slots, 2 * channels), bf16),
+        out_shape=jax.ShapeDtypeStruct((cols_x, cols_y + 1, slots, channels), bf16),
         in_specs=[in_hbm] * 6,
         out_specs=vmem,
         scratch_shapes=[pltpu.VMEM(x.shape, x.dtype) for x in given]
@@ -814,8 +820,10 @@
         compiler_params=pltpu.CompilerParams(vmem_limit_bytes=60 * 1024 * 1024),
         name="block_of_atoms",
     )(*given)
-    sides = (("gx", 0), ("gy", 1))
-    table = extended(block, sides).reshape(-1, 2 * channels)
+    assert cols_x == 2 and cols_y == 2
+    before, after = both_ways(block, block, "gx")
+    middle = jnp.concatenate([before, block, after], axis=0)
+    before, after = both_ways(middle, middle, "gy")
 
     inner_atoms = sz.inner * slots
     owned = cols_x * cols_y
@@ -849,12 +857,14 @@
         functools.partial(first_kernel, sz),
         out_shape=[
             jax.ShapeDtypeStruct((cols_x, cols_y, slots), f32),
-            jax.ShapeDtypeStruct((inner_atoms, 2 * channels), bf16),
+            jax.ShapeDtypeStruct((sz.inner_x, sz.inner_y + 1, slots, channels), bf16),
         ]
-        + [jax.ShapeDtypeStruct(shape, f32) for shape in kept_shapes],
-        in_specs=[vmem] * 7,
-        out_specs=[vmem] * 6,
-        scratch_shapes=edge_scratch(columns)
+        + [jax.ShapeDtypeStruct(shape, f32) for shape in kept_shapes]
+        + [jax.ShapeDtypeStruct((inner_atoms, channels), bf16)],
+        in_specs=[vmem] * 9,
+        out_specs=[vmem] * 7,
+        scratch_shapes=[pltpu.VMEM(((cols_x + 4) * (cols_y + 4) * slots, 2 * channels), bf16)]
+        + edge_scratch(columns)
         + [
             pltpu.VMEM((inner_atoms, channels), bf16),
             pltpu.VMEM((2, owned, channels, edges), f32),
@@ -867,17 +877,19 @@
         + [pltpu.VMEM((inner_atoms, channels), f32), pltpu.VMEM((inner_atoms, 8), f32)],
         compiler_params=params,
         name="forward_and_second_back",
-    )(table, *weights, readout.reshape(1, -1))
-
-    back = back.reshape(sz.inner_x, sz.inner_y, slots, 2 * channels)
-    cotangent = summed(back, sides).reshape(inner_atoms, 2 * channels)
+    )(before, middle, after, *weights, readout.reshape(1, -1))
+
+    far = both_ways(back[:2], back[2:], "gx")
+    total = back.astype(f32) + jnp.concatenate(far, axis=0).astype(f32)
+    sent = total.astype(bf16)
+    far = both_ways(sent[:, :3], sent[:, 2:], "gy")
     feature_grad, forces = pl.pallas_call(
         functools.partial(second_kernel, sz),
         out_shape=(
             jax.ShapeDtypeStruct((owned * slots, channels), f32),
             jax.ShapeDtypeStruct((cols_x, 3, cols_y, slots), f32),
         ),
-        in_specs=[vmem] * 11,
+        in_specs=[vmem] * 13,
         out_specs=(vmem,) * 2,
         scratch_shapes=edge_scratch(owned)
         + grads
@@ -893,7 +905,7 @@
         ],
         compiler_params=params,
         name="first_back",
-    )(cotangent, table, *kept, *weights)
+    )(total, *far, *kept, *weights)
     return (
         energy,
         forces.transpose(0, 2, 1, 3),

time: 50.1 us -> 44.2 us (0.88); the launches traced: 49.2 us -> 43.9 us
  waiting for transfers between devices: 16.4 us -> 12.6 us
  Pallas kernels: 18.1 us -> 15.4 us
  starting transfers between devices: 10.5 us -> 11.9 us
    ppermute x8, waiting for transfers between devices: 16.4 us -> 12.6 us  [both_ways(): return (lax.ppermute(last, axis, up), lax.ppermute(first, axis, down))]
    pallas_call x1, Pallas kernels: 11.3 us -> 8.48 us  [shards(): pl.pallas_call(functools.partial(first_kernel, sz), out_shape=[jax.ShapeD...]
    ppermute x8, starting transfers between devices: 10.5 us -> 11.9 us  [both_ways(): return (lax.ppermute(last, axis, up), lax.ppermute(first, axis, down))]
where the time goes in v4:
time: 44.2 us; the launch traced here: 43.9 us
  Pallas kernels  15.4 us (35%)
  waiting for transfers between devices  12.6 us (29%)
  starting transfers between devices  11.9 us (27%)
  other arithmetic  2.9 us (7%)
  between operations  0.74 us (2%)
    ppermute x8, waiting for transfers between devices, both_ways(): return (lax.ppermute(last, axis, up), lax.ppermute(first, axis, down))  12.6 us
    ppermute x8, starting transfers between devices, both_ways(): return (lax.ppermute(last, axis, up), lax.ppermute(first, axis, down))  11.9 us
    pallas_call x1, Pallas kernels, shards(): pl.pallas_call(functools.partial(first_kernel, sz), out_shape=[jax.ShapeD...  8.48 us
    pallas_call x1, Pallas kernels, shards(): pl.pallas_call(functools.partial(second_kernel, sz), out_shape=(jax.Shape...  5.19 us
    pallas_call x1, Pallas kernels, shards(): pl.pallas_call(functools.partial(block_kernel, sz, species_gain.shape[0])...  1.72 us
    another operation x2, other arithmetic  1.65 us
    another operation x2, other arithmetic, prepared(): mix = jnp.stack([high_mix, low_mix], axis=1)  1.1 us
  transfers between devices with their start and end apart: 8, of which 6 were waited for; matrix products, arithmetic and copies ran while one was open for 7% of the time, Pallas kernels for 0%

profile of v4, /device:TPU:0, one launch (start us, length us, event | category | flops | bytes accessed | tf_op | source)
XLA Modules:
  0.0 43.9 jit_solution(1546239949569972254)
XLA Ops:
  0.6 1.7 %block_of_atoms.1 = bf16[2,3,16,128]{3,2,1,0:T(8,128)(2,1)} custom-call(bf16[2,2,16,128]{3,2,1,0:T(8,128)(2,1)} %refs_0_.1, f32[2,3,2,16]{3,2,1,0:T(2,128)} %bitcast.15, s32[2,2,16]{2,1,0:T(2,128)} %refs_2_.1, s32[2,2,16,32]{3,2,1,0:T(8,128)} %refs_3_.1, s32[2,2,16]{2,1,0:T(2,128)} %refs_4_.1, f32[6,128]{1,0:T(8,128)} %refs_5_.1), custom_call_target="tpu_custom_call" | custom-call | tf_op jit(solution)/shard_map/block_of_atoms/pallas_call | solution.py:813
  2.4 6.0 %collective-permute-start.1 = (bf16[2,3,16,128]{3,2,1,0:T(8,128)(2,1)}, bf16[2,3,16,128]{3,2,1,0:T(8,128)(2,1)S(1)}, u32[]{:S(2)}, u32[]{:S(2)}) collective-permute-start(bf16[2,3,16,128]{3,2,1,0:T(8,128)(2,1)} %block_of_atoms.1), channel_id=1, source_target_pairs={{4,0},{8,4},{12,8},{16,12},{20,16},{24,20},{28,24},{0,28},{5,1},{9... | collective-permute-start | bytes 73736 | tf_op jit(solution)/shard_map/ppermute | solution.py:799
  8.4 0.0 collective-permute-start
  8.4 0.7 %reduce-precision_convert_fusion.2 = (bf16[2,8,64]{2,1,0:T(8,128)(2,1)S(1)}, bf16[2,8,64]{2,1,0:T(8,128)(2,1)S(1)}) fusion(f32[2,8,64]{2,1,0:T(8,128)} %param.16), kind=kLoop, calls=%fused_computation.14 | loop fusion | flops 4096 | bytes 8192 | tf_op jit(solution)/shard_map/convert.9
  9.1 1.0 %reduce-precision_convert_fusion.1 = (bf16[2,64,384]{2,1,0:T(8,128)(2,1)S(1)}, bf16[2,64,384]{2,1,0:T(8,128)(2,1)S(1)}) fusion(f32[2,64,384]{2,1,0:T(8,128)} %param.17), kind=kLoop, calls=%fused_computation.6 | loop fusion | flops 196608 | bytes 393216 | tf_op jit(solution)/shard_map/convert.6
  10.0 1.1 %fusion.3 = (bf16[2,1,384,128]{3,2,1,0:T(8,128)(2,1)S(1)}, bf16[2,1,384,128]{3,2,1,0:T(8,128)(2,1)S(1)}) fusion(f32[2,384,128]{2,1,0:T(8,128)} %param.18), kind=kLoop, calls=%fused_computation.9 | loop fusion | flops 393216 | bytes 786432 | tf_op jit(solution)/shard_map/stack | solution.py:52
  11.1 0.0 copy-start.1
  11.1 0.0 copy-start
  11.1 0.1 pad.12.clone
  11.3 0.1 maximum_bitcast_fusion.1
  11.4 0.1 copy.14.wide_in
  11.5 0.2 copy.15.wide_out
  11.7 0.0 collective-permute-done.1
  11.7 3.4 %collective-permute-done = bf16[2,3,16,128]{3,2,1,0:T(8,128)(2,1)S(1)} collective-permute-done((bf16[2,3,16,128]{3,2,1,0:T(8,128)(2,1)}, bf16[2,3,16,128]{3,2,1,0:T(8,128)(2,1)S(1)}, u32[]{:S(2)}, u32[]{:S(2)}) %collective-permute-start) | collective-permute-done | bytes 24608 | tf_op jit(solution)/shard_map/ppermute | solution.py:799
  15.1 0.0 copy-done.1
  15.1 0.1 collective-permute-start.3
  15.2 0.5 %collective-permute-start.2 = (bf16[6,3,16,128]{3,2,1,0:T(8,128)(2,1)S(1)}, bf16[6,3,16,128]{3,2,1,0:T(8,128)(2,1)S(1)}, u32[]{:S(2)}, u32[]{:S(2)}) collective-permute-start(bf16[6,3,16,128]{3,2,1,0:T(8,128)(2,1)S(1)} %pad_maximum_fusion.1.middle), channel_id=1, source_target_pairs={{0,1},{1,2},{2,3},{3,0},{4,5},{5,6},{6,7},{7,4},{8,9},{9,10},{10,1... | collective-permute-start | bytes 221192 | tf_op jit(solution)/shard_map/ppermute | solution.py:799
  15.7 1.5 %collective-permute-done.3.after = bf16[6,3,16,128]{3,2,1,0:T(8,128)(2,1)S(1)} collective-permute-done((bf16[6,3,16,128]{3,2,1,0:T(8,128)(2,1)S(1)}, bf16[6,3,16,128]{3,2,1,0:T(8,128)(2,1)S(1)}, u32[]{:S(2)}, u32[]{:S(2)}) %collective-permute-start.3) | collective-permute-done | bytes 73760 | tf_op jit(solution)/shard_map/ppermute | solution.py:799
  17.2 2.6 %collective-permute-done.2.before = bf16[6,3,16,128]{3,2,1,0:T(8,128)(2,1)S(1)} collective-permute-done((bf16[6,3,16,128]{3,2,1,0:T(8,128)(2,1)S(1)}, bf16[6,3,16,128]{3,2,1,0:T(8,128)(2,1)S(1)}, u32[]{:S(2)}, u32[]{:S(2)}) %collective-permute-start.2) | collective-permute-done | bytes 73760 | tf_op jit(solution)/shard_map/ppermute | solution.py:799
  19.8 0.0 copy-done
  19.8 8.5 %forward_and_second_back.1 = (f32[2,2,16]{2,1,0:T(2,128)}, bf16[4,5,16,128]{3,2,1,0:T(8,128)(2,1)S(1)}, f32[16,144,128]{2,1,0:T(8,128)S(1)}, f32[2,16,256]{2,1,0...) custom-call(bf16[6,3,16,128]{3,2,1,0:T(8,128)(2,1)S(1)} %collective-permute-do, ...), custom_call_target="tpu_custom_call" | custom-call | tf_op jit(solution)/shard_map/forward_and_second_back/pallas_call | solution.py:856
  28.3 0.0 collective-permute-start.4
  28.3 4.7 %collective-permute-start.5 = (bf16[2,5,16,128]{3,2,1,0:T(8,128)(2,1)S(1)}, bf16[2,5,16,128]{3,2,1,0:T(8,128)(2,1)S(1)}, u32[]{:S(2)}, u32[]{:S(2)}) collective-permute-start(bf16[2,5,16,128]{3,2,1,0:T(8,128)(2,1)S(1)} %get-tuple-element.30), channel_id=1, source_target_pairs={{4,0},{8,4},{12,8},{16,12},{20,16},{24,20},{28,24},{0,28},{5,1},{9... | collective-permute-start | bytes 122888 | tf_op jit(solution)/shard_map/ppermute | solution.py:799
  33.0 2.0 %collective-permute-done.4 = bf16[2,5,16,128]{3,2,1,0:T(8,128)(2,1)S(1)} collective-permute-done((bf16[2,5,16,128]{3,2,1,0:T(8,128)(2,1)S(1)}, bf16[2,5,16,128]{3,2,1,0:T(8,128)(2,1)S(1)}, u32[]{:S(2)}, u32[]{:S(2)}) %collective-permute-start.4) | collective-permute-done | bytes 40992 | tf_op jit(solution)/shard_map/ppermute | solution.py:799
  35.0 0.0 collective-permute-done.5
  35.1 0.1 collective-permute-start.7
  35.1 0.5 %collective-permute-start.6 = (bf16[4,3,16,128]{3,2,1,0:T(8,128)(2,1)S(1)}, bf16[4,3,16,128]{3,2,1,0:T(8,128)(2,1)S(1)}, u32[]{:S(2)}, u32[]{:S(2)}) collective-permute-start(bf16[4,3,16,128]{3,2,1,0:T(8,128)(2,1)S(1)} %get-tuple-element.28), channel_id=1, source_target_pairs={{0,1},{1,2},{2,3},{3,0},{4,5},{5,6},{6,7},{7,4},{8,9},{9,10},{10,1... | collective-permute-start | bytes 147464 | tf_op jit(solution)/shard_map/ppermute | solution.py:799
  35.6 1.4 %collective-permute-done.7.after = bf16[4,3,16,128]{3,2,1,0:T(8,128)(2,1)S(1)} collective-permute-done((bf16[4,3,16,128]{3,2,1,0:T(8,128)(2,1)S(1)}, bf16[4,3,16,128]{3,2,1,0:T(8,128)(2,1)S(1)}, u32[]{:S(2)}, u32[]{:S(2)}) %collective-permute-start.7) | collective-permute-done | bytes 49184 | tf_op jit(solution)/shard_map/ppermute | solution.py:799
  37.0 1.7 %collective-permute-done.6.before = bf16[4,3,16,128]{3,2,1,0:T(8,128)(2,1)S(1)} collective-permute-done((bf16[4,3,16,128]{3,2,1,0:T(8,128)(2,1)S(1)}, bf16[4,3,16,128]{3,2,1,0:T(8,128)(2,1)S(1)}, u32[]{:S(2)}, u32[]{:S(2)}) %collective-permute-start.6) | collective-permute-done | bytes 49184 | tf_op jit(solution)/shard_map/ppermute | solution.py:799
  38.7 5.2 %first_back.1 = (f32[64,128]{1,0:T(8,128)}, f32[2,3,2,16]{3,2,1,0:T(2,128)}) custom-call(f32[4,5,16,128]{3,2,1,0:T(8,128)S(1)} %get-tuple-element.26.total, bf16[4,3,16,128]{3,2,1,0:T(8,128)(2,1)S(1)} %collective-permute-done.6.before, bf16[4,3,16,128]{3,2,1,0:T(8,128)(2,1)S(1)} %collective-permute-done.7.after, f32[16,144,128]{2,1,0:T(8,128)S(1)} %get-tuple-element.14.kept, ...), custom_call_target="tpu_custom_call" | custom-call | tf_op jit(solution)/shard_map/first_back/pallas_call | solution.py:886
  (8 shorter events, 0.1 us)
Async XLA Ops:
  2.4 9.3 %collective-permute-start.1 = (bf16[2,3,16,128]{3,2,1,0:T(8,128)(2,1)}, bf16[2,3,16,128]{3,2,1,0:T(8,128)(2,1)S(1)}, u32[]{:S(2)}, u32[]{:S(2)}) collective-permute-start(bf16[2,3,16,128]{3,2,1,0:T(8,128)(2,1)} %block_of_atoms.1), channel_id=1, source_target_pairs={{4,0},{8,4},{12,8},{16,12},{20,16},{24,20},{28,24},{0,28},{5,1},{9... | collective-permute-start | bytes 73736 | tf_op jit(solution)/shard_map/ppermute | solution.py:799
  8.4 6.7 %collective-permute-start = (bf16[2,3,16,128]{3,2,1,0:T(8,128)(2,1)}, bf16[2,3,16,128]{3,2,1,0:T(8,128)(2,1)S(1)}, u32[]{:S(2)}, u32[]{:S(2)}) collective-permute-start(bf16[2,3,16,128]{3,2,1,0:T(8,128)(2,1)} %block_of_atoms.1), channel_id=1, source_target_pairs={{0,4},{4,8},{8,12},{12,16},{16,20},{20,24},{24,28},{28,0},{1,5},{5... | collective-permute-start | bytes 73736 | tf_op jit(solution)/shard_map/ppermute | solution.py:799
  11.1 4.0 %copy-start.1 = (bf16[2,3,16,128]{3,2,1,0:T(8,128)(2,1)S(1)}, bf16[2,3,16,128]{3,2,1,0:T(8,128)(2,1)}, u32[]{:S(2)}) copy-start(bf16[2,3,16,128]{3,2,1,0:T(8,128)(2,1)} %block_of_atoms.1) | copy-start | bytes 73732
  11.1 8.7 %copy-start = (f32[128]{0:T(128)S(1)}, f32[128]{0:T(128)}, u32[]{:S(2)}) copy-start(f32[128]{0:T(128)} %param.19) | copy-start | bytes 1540
  15.1 2.0 %collective-permute-start.3 = (bf16[6,3,16,128]{3,2,1,0:T(8,128)(2,1)S(1)}, bf16[6,3,16,128]{3,2,1,0:T(8,128)(2,1)S(1)}, u32[]{:S(2)}, u32[]{:S(2)}) collective-permute-start(bf16[6,3,16,128]{3,2,1,0:T(8,128)(2,1)S(1)} %pad_maximum_fusion.1.middle), channel_id=1, source_target_pairs={{1,0},{2,1},{3,2},{0,3},{5,4},{6,5},{7,6},{4,7},{9,8},{10,9},{11,1... | collective-permute-start | bytes 221192 | tf_op jit(solution)/shard_map/ppermute | solution.py:799
  15.2 4.6 %collective-permute-start.2 = (bf16[6,3,16,128]{3,2,1,0:T(8,128)(2,1)S(1)}, bf16[6,3,16,128]{3,2,1,0:T(8,128)(2,1)S(1)}, u32[]{:S(2)}, u32[]{:S(2)}) collective-permute-start(bf16[6,3,16,128]{3,2,1,0:T(8,128)(2,1)S(1)} %pad_maximum_fusion.1.middle), channel_id=1, source_target_pairs={{0,1},{1,2},{2,3},{3,0},{4,5},{5,6},{6,7},{7,4},{8,9},{9,10},{10,1... | collective-permute-start | bytes 221192 | tf_op jit(solution)/shard_map/ppermute | solution.py:799
  28.3 6.7 %collective-permute-start.4 = (bf16[2,5,16,128]{3,2,1,0:T(8,128)(2,1)S(1)}, bf16[2,5,16,128]{3,2,1,0:T(8,128)(2,1)S(1)}, u32[]{:S(2)}, u32[]{:S(2)}) collective-permute-start(bf16[2,5,16,128]{3,2,1,0:T(8,128)(2,1)S(1)} %get-tuple-element.29), channel_id=1, source_target_pairs={{0,4},{4,8},{8,12},{12,16},{16,20},{20,24},{24,28},{28,0},{1,5},{5... | collective-permute-start | bytes 122888 | tf_op jit(solution)/shard_map/ppermute | solution.py:799
  28.3 6.7 %collective-permute-start.5 = (bf16[2,5,16,128]{3,2,1,0:T(8,128)(2,1)S(1)}, bf16[2,5,16,128]{3,2,1,0:T(8,128)(2,1)S(1)}, u32[]{:S(2)}, u32[]{:S(2)}) collective-permute-start(bf16[2,5,16,128]{3,2,1,0:T(8,128)(2,1)S(1)} %get-tuple-element.30), channel_id=1, source_target_pairs={{4,0},{8,4},{12,8},{16,12},{20,16},{24,20},{28,24},{0,28},{5,1},{9... | collective-permute-start | bytes 122888 | tf_op jit(solution)/shard_map/ppermute | solution.py:799
  35.1 2.0 %collective-permute-start.7 = (bf16[4,3,16,128]{3,2,1,0:T(8,128)(2,1)S(1)}, bf16[4,3,16,128]{3,2,1,0:T(8,128)(2,1)S(1)}, u32[]{:S(2)}, u32[]{:S(2)}) collective-permute-start(bf16[4,3,16,128]{3,2,1,0:T(8,128)(2,1)S(1)} %get-tuple-element.27), channel_id=1, source_target_pairs={{1,0},{2,1},{3,2},{0,3},{5,4},{6,5},{7,6},{4,7},{9,8},{10,9},{11,1... | collective-permute-start | bytes 147464 | tf_op jit(solution)/shard_map/ppermute | solution.py:799
  35.1 3.6 %collective-permute-start.6 = (bf16[4,3,16,128]{3,2,1,0:T(8,128)(2,1)S(1)}, bf16[4,3,16,128]{3,2,1,0:T(8,128)(2,1)S(1)}, u32[]{:S(2)}, u32[]{:S(2)}) collective-permute-start(bf16[4,3,16,128]{3,2,1,0:T(8,128)(2,1)S(1)} %get-tuple-element.28), channel_id=1, source_target_pairs={{0,1},{1,2},{2,3},{3,0},{4,5},{5,6},{6,7},{7,4},{8,9},{9,10},{10,1... | collective-permute-start | bytes 147464 | tf_op jit(solution)/shard_map/ppermute | solution.py:799

commit v5 on v4

--- a/solution.py
+++ b/solution.py
@@ -81,7 +81,9 @@
 
         cells = [(a, b) for a in range(self.inner_x) for b in range(self.inner_y)]
         self.own = [c for c in cells if self.is_own(*c)]
-        self.halo = [c for c in cells if not self.is_own(*c)]
+        last = self.inner_x - 1
+        self.halo = [c for c in cells if c[0] in (0, last)]
+        self.halo += [(a, b) for b in (0, self.inner_y - 1) for a in range(1, last)]
         self.order = self.own + self.halo
 
     def is_own(self, a, b):
@@ -96,6 +98,16 @@
 
 def each(compute):
     return lambda items: [compute(item) for item in items]
+
+
+def run_steps(*steps):
+    steps = list(steps)
+    while steps:
+        for step in list(steps):
+            try:
+                next(step)
+            except StopIteration:
+                steps.remove(step)
 
 
 def loop(count, group, compute, store):
@@ -103,18 +115,6 @@
         items = list(range(first, min(first + group, count)))
         for item, value in zip(items, compute(items)):
             store(item, value)
-
-
-def window_of(sz, table, a, b):
-    run = 3 * sz.slots
-    return jnp.concatenate(
-        [table[pl.ds(sz.outer_row(a + d, b), run), :] for d in range(3)], axis=0
-    )
-
-
-def inner_window(sz, table, a, b):
-    rows = [sz.inner_row(a - 1 + d, b - 1) for d in range(3)]
-    return jnp.concatenate([table[row : row + 3 * sz.slots, :] for row in rows], axis=0)
 
 
 def iota(shape, dim):
@@ -134,39 +134,89 @@
     return low, low + metas[:, count_lane : count_lane + 1].astype(f32)
 
 
-def gather_columns(sz, part, table, low, high, code, atom, sep, hot, xt):
-    ch, n = sz.channels, sz.slots
-    lane = iota((n, sz.edges), 1) + (part * sz.edges).astype(f32)
-    row = iota((n, sz.edges), 0)
-    slot = iota((sz.neigh, sz.edges), 0)
-    target = iota((sz.window, sz.edges), 0)
-
-    def one(col):
-        a, b = sz.order[col]
-        meta = table[pl.ds(sz.outer_row(a + 1, b + 1), n), ch : 2 * ch]
+def gather_columns(sz, part, table, low, high, code, atom, sep, xt):
+    ch, n, edges = sz.channels, sz.slots, sz.edges
+    lane = iota((n, edges), 1) + (part * edges).astype(f32)
+    row = iota((n, edges), 0)
+    slot = iota((sz.neigh, 2 * edges), 0)
+    second = (lax.broadcasted_iota(jnp.int32, (1, 2 * edges), 1) >= edges).astype(f32)
+    target = iota((12 * n, 2 * edges), 0)
+    empty = jnp.zeros((n, edges), f32)
+
+    firsts = list(range(0, sz.inner, 2))
+    ats, valids, which, atoms, spreads = [], [], [], [], []
+    for col, (a, b) in enumerate(sz.order):
         mine = slice(col * n, (col + 1) * n)
         at = ((lane >= low[mine]) & (lane < high[mine])).astype(f32)
-        valid = jnp.sum(at, axis=0, keepdims=True) - 1.0
-        which = lane[:1] - jnp.sum(at * low[mine], axis=0, keepdims=True)
-        spread = mm(meta.astype(f32).T[: 2 * code_lane].astype(bf16), at.astype(bf16))
-        picked = jnp.where(slot == which, spread[code_lane:], 0.0)
-        codes = jnp.sum(picked, axis=0, keepdims=True) + valid
-        atoms = jnp.sum(at * row, axis=0, keepdims=True) + valid
-        one_hot = (target == codes).astype(f32).astype(bf16)
-        turned = window_of(sz, table, a, b).astype(f32).T.astype(bf16)[: ch + 32]
-        found = mm(turned, one_hot)
+        ats.append(at)
+        valids.append(jnp.sum(at, axis=0, keepdims=True) - 1.0)
+        which.append(lane[:1] - jnp.sum(at * low[mine], axis=0, keepdims=True))
+        atoms.append(jnp.sum(at * row, axis=0, keepdims=True) + valids[-1])
+    for first in firsts:
+        places = [sz.outer_row(a + 1, b + 1) for a, b in sz.order[first : first + 2]]
+        metas = [table[place : place + n, ch : 2 * ch] for place in places]
+        turned = jnp.concatenate(metas, axis=0).astype(f32).T[: 2 * code_lane].astype(bf16)
+        apart = jnp.concatenate(
+            [
+                jnp.concatenate([ats[first], empty], axis=1),
+                jnp.concatenate([empty, ats[first + 1]], axis=1),
+            ],
+            axis=0,
+        )
+        spreads.append(mm(turned, apart.astype(bf16)))
+    hots, windows, codes_of = [], [], []
+    for first, spread in zip(firsts, spreads):
+        (a, b), (_, other_b) = sz.order[first : first + 2]
+        both = jnp.concatenate(which[first : first + 2], axis=1)
+        picked = jnp.where(slot == both, spread[code_lane:], 0.0)
+        codes = jnp.sum(picked, axis=0, keepdims=True)
+        codes = codes + jnp.concatenate(valids[first : first + 2], axis=1)
+        if other_b != b:
+            width, height = 4, 3
+            ahead = (codes >= 3.0 * n).astype(f32) + (codes >= 6.0 * n).astype(f32)
+            rows = codes + n * (ahead + second)
+        else:
+            width, height = 3, 4
+            rows = codes + 3.0 * n * second
+        rows = jnp.where(codes < 0.0, -1.0, rows)
+        hots.append((target == rows).astype(f32).astype(bf16))
+        window = jnp.concatenate(
+            [table[pl.ds(sz.outer_row(a + d, b), width * n), :] for d in range(height)], axis=0
+        )
+        windows.append(window.astype(f32).T.astype(bf16)[: ch + 32])
+        codes_of.append(codes)
+    founds = [mm(window, one_hot) for window, one_hot in zip(windows, hots)]
+    for first, spread, codes, found in zip(firsts, spreads, codes_of, founds):
         diff = found[ch : ch + 24] - spread[:24]
-        return codes, atoms, one_hot, found[:ch], diff[0:8] + diff[8:16] + diff[16:24]
-
-    def store(col, value):
-        code[part, pl.ds(col, 1), :], atom[part, pl.ds(col, 1), :], one_hot, found, total = value
-        if col < len(sz.own):
-            hot[part, col] = one_hot
-        xt[col] = found
-        for d in range(3):
-            sep[part, d, pl.ds(col, 1), :] = total[d : d + 1]
-
-    loop(sz.inner, 4, each(one), store)
+        total = diff[0:8] + diff[8:16] + diff[16:24]
+        for col, span in ((first, slice(0, edges)), (first + 1, slice(edges, 2 * edges))):
+            code[part, pl.ds(col, 1), :] = codes[:, span]
+            atom[part, pl.ds(col, 1), :] = atoms[col]
+            xt[col] = found[:ch, span]
+            for d in range(3):
+                sep[part, d, pl.ds(col, 1), :] = total[d : d + 1, span]
+
+
+def wide_rows(rows):
+    return jnp.concatenate([rows[k : k + 1] for k in range(rows.shape[0])], axis=1)
+
+
+def own_hot(sz, codes):
+    row = lax.broadcasted_iota(jnp.int32, codes.shape, 0)
+    place = jnp.zeros_like(row)
+    for k, (a, b) in enumerate(sz.own):
+        place = jnp.where(row == k, sz.inner_row(a - 1, b - 1), place)
+    whole = codes.astype(jnp.int32)
+    ahead = (((whole >> 4) * 11) >> 5) * (sz.slots * (sz.inner_y - 3))
+    rows = jnp.where(codes < 0.0, -1.0, (place + whole + ahead).astype(f32))
+    wide = wide_rows(rows)
+    return (iota((sz.inner * sz.slots, wide.shape[1]), 0) == wide).astype(f32).astype(bf16)
+
+
+def own_atoms(sz, atoms):
+    row = iota(atoms.shape, 0)
+    wide = wide_rows(jnp.where(atoms < 0.0, -1.0, atoms + row * float(sz.slots)))
+    return (iota((len(sz.own) * sz.slots, wide.shape[1]), 0) == wide).astype(f32).astype(bf16)
 
 
 def shifted_seps(part, code, sep):
@@ -232,29 +282,36 @@
     rows = [jnp.concatenate([ref[part, pl.ds(c, 1), :] for c in cols], axis=1) for ref in (dist, env)]
     weighted, value, slope = hidden_rows(sz, *rows, weight_in)
     radials = mm(weight_out, weighted)
+    spans = [slice(k * sz.edges, (k + 1) * sz.edges) for k in range(len(cols))]
+    sides = [message_sides(sz, part, col, angular, atom) for col in cols]
+    products = [
+        (radials[:, span] * jnp.concatenate([xt] * 3, axis=0)).astype(bf16)
+        for span, xt in zip(spans, inputs)
+    ]
+    ch = sz.channels
+    got = [
+        [nt(both, product[l * ch : (l + 1) * ch]) for l, both in enumerate(side)]
+        for side, product in zip(sides, products)
+    ]
     out = []
-    for k, (col, xt) in enumerate(zip(cols, inputs)):
-        span = slice(k * sz.edges, (k + 1) * sz.edges)
-        radial = radials[:, span]
-        message = column_messages(sz, part, col, angular, atom, radial, xt)
-        out.append((radial, value[:, span], slope[:, span], message))
+    for span, parts in zip(spans, got):
+        halves = [len(x) // 2 for x in parts]
+        rows = [parts[0]] + [x[:h] + x[h:] for x, h in zip(parts[1:], halves[1:])]
+        message = jnp.concatenate(rows, axis=0)
+        out.append((radials[:, span], value[:, span], slope[:, span], message))
     return out
 
 
-def column_messages(sz, part, col, angular, atom, radial, xt):
-    ch, n = sz.channels, sz.slots
-    product = (radial * jnp.concatenate([xt] * 3, axis=0)).astype(bf16)
+def message_sides(sz, part, col, angular, atom):
+    n = sz.slots
     at = atoms_at(sz, atom, part, col)
     blocks = jnp.concatenate(block_rows(angular, part, col, at), axis=0)
     high = blocks.astype(bf16).astype(f32)
     low = blocks - high
-    out = [nt(at.astype(bf16), product[:ch])]
-    for l, rows in ((1, slice(0, 3 * n)), (2, slice(3 * n, 8 * n))):
-        both = jnp.concatenate([high[rows], low[rows]], axis=0).astype(bf16)
-        got = nt(both, product[l * ch : (l + 1) * ch])
-        count = got.shape[0] // 2
-        out.append(got[:count] + got[count:])
-    return jnp.concatenate(out, axis=0)
+    sides = [at.astype(bf16)]
+    for rows in (slice(0, 3 * n), slice(3 * n, 8 * n)):
+        sides.append(jnp.concatenate([high[rows], low[rows]], axis=0).astype(bf16))
+    return sides
 
 
 def invariants(sz, message):
@@ -304,39 +361,55 @@
 
 
 def layer_backward(
-    sz, part, cols, angular, dist, atom, back_in, back_out, radials, value, slope, inputs, hots,
+    sz, part, cols, angular, dist, atom, back_in, back_out, radials, value, slope, inputs,
     messages, cotangents,
 ):
     ch, n = sz.channels, sz.slots
-    mine, windows, ang_grads = [], [], []
-    for k, col in enumerate(cols):
-        at = atoms_at(sz, atom, part, col)
-        blocks = jnp.concatenate([at] + block_rows(angular, part, col, at), axis=0).astype(bf16)
-        grads = message_grads(sz, messages[k], cotangents[k])
+    ats = [atoms_at(sz, atom, part, col) for col in cols]
+    grads_of = [message_grads(sz, *both) for both in zip(messages, cotangents)]
+    lhs = []
+    for grads in grads_of:
         turned = jnp.concatenate(grads, axis=0).T
         lane = lax.broadcasted_iota(jnp.int32, turned.shape, 1)
-        lhs = jnp.concatenate(
-            [
-                jnp.where(lane < n, turned, 0.0),
-                jnp.where((lane >= n) & (lane < 4 * n), turned, 0.0),
-                jnp.where(lane >= 4 * n, turned, 0.0),
-            ],
-            axis=0,
-        ).astype(bf16)
-        products, radial_grad, input_grad = radial_products(
-            sz, mm(lhs, blocks), radials[k], inputs[k]
+        lhs.append(
+            jnp.concatenate(
+                [
+                    jnp.where(lane < n, turned, 0.0),
+                    jnp.where((lane >= n) & (lane < 4 * n), turned, 0.0),
+                    jnp.where(lane >= 4 * n, turned, 0.0),
+                ],
+                axis=0,
+            ).astype(bf16)
         )
-        mine.append(radial_grad)
-        windows.append(nt(hots[k], input_grad))
-        empty = jnp.zeros((n, ch), f32)
+    blocks = [
+        jnp.concatenate([at] + block_rows(angular, part, col, at), axis=0).astype(bf16)
+        for col, at in zip(cols, ats)
+    ]
+    yield
+    product_grads = [mm(left, right) for left, right in zip(lhs, blocks)]
+    yield
+    triples = [
+        radial_products(sz, *three_of) for three_of in zip(product_grads, radials, inputs)
+    ]
+    mine = [triple[1] for triple in triples]
+    input_grads = [triple[2] for triple in triples]
+    yield
+    empty = jnp.zeros((n, ch), f32)
+    wides = []
+    for grads in grads_of:
         wide = [
             jnp.concatenate([g, empty] if m < 3 else [empty, g], axis=1)
             for m, g in enumerate(grads[1:])
         ]
-        got = mm(jnp.concatenate(wide, axis=0).astype(bf16), jnp.concatenate(products, axis=0))
-        ang_grads.append(
-            [jnp.sum(got[m * n : (m + 1) * n] * at, axis=0, keepdims=True) for m in range(8)]
-        )
+        wides.append(jnp.concatenate(wide, axis=0).astype(bf16))
+    gots = [
+        mm(wide, jnp.concatenate(triple[0], axis=0)) for wide, triple in zip(wides, triples)
+    ]
+    yield
+    ang_grads = [
+        [jnp.sum(got[m * n : (m + 1) * n] * at, axis=0, keepdims=True) for m in range(8)]
+        for got, at in zip(gots, ats)
+    ]
     dist_row = jnp.concatenate([dist[part, pl.ds(col, 1), :] for col in cols], axis=1)
     dist_row_grad, env_row_grad = radial_backward(
         sz, dist_row, jnp.concatenate(mine, axis=1), value, slope, back_in, back_out
@@ -344,24 +417,17 @@
     out = []
     for k in range(len(cols)):
         span = slice(k * sz.edges, (k + 1) * sz.edges)
-        out.append((windows[k], ang_grads[k], dist_row_grad[:, span], env_row_grad[:, span]))
-    return out
-
-
-def store_grads(sz, col, value, ang_grad, dist_grad, env_grad, acc):
-    window, ang_grads, dist_row_grad, env_row_grad = value
+        out.append((ang_grads[k], dist_row_grad[:, span], env_row_grad[:, span]))
+    yield
+    return jnp.concatenate(input_grads, axis=1), out
+
+
+def store_grads(sz, col, value, ang_grad, dist_grad, env_grad):
+    ang_grads, dist_row_grad, env_row_grad = value
     for m in range(8):
         ang_grad[m + 1, pl.ds(col, 1), :] = ang_grads[m]
     dist_grad[pl.ds(col, 1), :] = dist_row_grad
     env_grad[pl.ds(col, 1), :] = env_row_grad
-    add_window(sz, sz.own[col], window, acc)
-
-
-def add_window(sz, place, window, acc):
-    a, b = place
-    run = 3 * sz.slots
-    for d in range(3):
-        acc[pl.ds(sz.inner_row(a - 1 + d, b - 1), run), :] += window[d * run : (d + 1) * run]
 
 
 def separation_grads(live, sep, dist, ang_grad, dist_grad, env_grad):
@@ -388,10 +454,8 @@
     return jnp.concatenate([high, full - high], axis=0).astype(bf16)
 
 
-def own_positions(
-    sz, part, code, atom, sep, dist, hot, ang_grad, dist_grad, env_grad, sep_grad, acc_pos
-):
-    owned = len(sz.own)
+def own_positions(sz, part, code, atom, sep, dist, hot, ang_grad, dist_grad, env_grad, acc_pos):
+    owned, n = len(sz.own), sz.slots
     grads = separation_grads(
         live_rows(code[part, :owned]),
         [sep[part, d, :owned] for d in range(3)],
@@ -400,21 +464,14 @@
         dist_grad[...],
         env_grad[...],
     )
-    for d in range(3):
-        sep_grad[d] = grads[d]
-    for k, place in enumerate(sz.own):
-        rows = [sep_grad[d, pl.ds(k, 1), :] for d in range(3)]
-        signed = signed_hot(sz, hot[part, k], atoms_at(sz, atom, part, k).astype(bf16))
-        got = nt(signed, stacked_seps(rows))
-        add_window(sz, place, got[:, :8] + got[:, 8:], acc_pos)
-
-
-def signed_hot(sz, one_hot, mask_bf):
-    first = 4 * sz.slots
-    return jnp.concatenate(
-        [one_hot[:first], one_hot[first : first + sz.slots] - mask_bf, one_hot[first + sz.slots :]],
-        axis=0,
-    )
+    ends = jnp.concatenate([hot, own_atoms(sz, atom[part, :owned])], axis=0)
+    got = nt(ends, stacked_seps([wide_rows(grad) for grad in grads]))
+    got = got[:, :8] + got[:, 8:]
+    atoms = sz.inner * n
+    acc_pos[...] += got[:atoms]
+    for k, (a, b) in enumerate(sz.own):
+        row = sz.inner_row(a, b)
+        acc_pos[row : row + n] -= got[atoms + k * n : atoms + (k + 1) * n]
 
 
 def fetch(sources, targets, sems):
@@ -478,7 +535,7 @@
     sz, before, middle, after, wide_in, wide_out, turned_in, turned_out, mixing, readout,
     energy, back, kept, code, atom, sep, inputs_kept, table,
     hot, xt, angular, dist, env, second, second_xt, second_msg, second_radial,
-    second_value, second_slope, ang_grad, dist_grad, env_grad, sep_grad, acc, acc_pos,
+    second_value, second_slope, ang_grad, dist_grad, env_grad, acc, acc_pos,
 ):
     ch, n = sz.channels, sz.slots
     owned = len(sz.own)
@@ -491,7 +548,7 @@
     kept[...] = jnp.zeros_like(kept)
 
     def first_part(part, carry):
-        gather_columns(sz, part, table, low, high, code, atom, sep, hot, xt)
+        gather_columns(sz, part, table, low, high, code, atom, sep, xt)
         shifted_seps(part, code, sep)
         seps = [sep[part, d] for d in range(3)]
         store_geometry(part, live_rows(code[part]), seps, dist, env, angular)
@@ -524,14 +581,14 @@
     in_two, out_two = wide_in[1], wide_out[1]
     back_in, back_out = turned_in[1], turned_out[1]
     second_msg[...] = jnp.zeros_like(second_msg)
+    second_turned = second[...].astype(f32).T.astype(bf16)
     every = list(range(owned))
 
     def second_part(part, carry):
-        def second_input(k):
-            window = inner_window(sz, second, *sz.own[k])
-            return mm(window.astype(f32).T.astype(bf16), hot[part, k])
-
-        inputs = [second_input(k) for k in every]
+        one_hot = own_hot(sz, code[part, :owned])
+        hot[part] = one_hot
+        found = mm(second_turned, one_hot)
+        inputs = [found[:, k * sz.edges : (k + 1) * sz.edges] for k in every]
         got = layer_forward(sz, part, every, angular, dist, env, atom, in_two, out_two, inputs)
         for k, (radial, value, slope, message) in zip(every, got):
             second_xt[part, k], second_radial[part, k] = inputs[k], radial
@@ -559,22 +616,25 @@
         first = ((a + 1) * sz.inner_y + 1) * n
         acc[first : first + sz.cols_y * n] = out_grad[a * sz.cols_y * n : (a + 1) * sz.cols_y * n]
 
-    def back_part(part, carry):
-        got = layer_backward(
+    def back_steps(part):
+        input_grad, got = yield from layer_backward(
             sz, part, every, angular, dist, atom, back_in, back_out,
             [second_radial[part, k] for k in every],
             jnp.concatenate([second_value[part, k] for k in every], axis=1),
             jnp.concatenate([second_slope[part, k] for k in every], axis=1),
             [second_xt[part, k] for k in every],
-            [hot[part, k] for k in every],
             [second_msg[k] for k in every],
             [cotangents[k * n : (k + 1) * n] for k in every],
         )
         for k, value in zip(every, got):
-            store_grads(sz, k, value, ang_grad, dist_grad, env_grad, acc)
+            store_grads(sz, k, value, ang_grad, dist_grad, env_grad)
+        acc[...] += nt(hot[part], input_grad)
         own_positions(
-            sz, part, code, atom, sep, dist, hot, ang_grad, dist_grad, env_grad, sep_grad, acc_pos
+            sz, part, code, atom, sep, dist, hot[part], ang_grad, dist_grad, env_grad, acc_pos
         )
+
+    def back_part(part, carry):
+        run_steps(back_steps(part))
         return carry
 
     lax.fori_loop(0, parts, back_part, 0)
@@ -627,7 +687,7 @@
     ch, n, lanes = sz.channels, sz.slots, sz.edges
     first = len(sz.own)
     count = len(sz.halo) * n
-    wanted = iota((lanes, lanes), 0) + (part * lanes).astype(f32)
+    wanted = iota((lanes, lanes), 0) + jnp.asarray(part * lanes).astype(f32)
     ones, zeros = jnp.ones((1, lanes), f32), jnp.zeros((2, lanes), f32)
 
     def packed(edge_part, total):
@@ -652,18 +712,24 @@
             )
         return total + nt(jnp.concatenate(sides, axis=1), jnp.concatenate(picks, axis=1))
 
-    got = lax.fori_loop(0, edge_parts, packed, jnp.zeros((24, lanes), f32))
+    got = packed(0, jnp.zeros((24, lanes), f32))
+    yield
+    got = lax.fori_loop(1, edge_parts, packed, got)
     got = got[0:8] + got[8:16] + got[16:24]
     seps = [got[d : d + 1] for d in range(3)]
     target_row, atom_row, valid = got[3:4], got[4:5], got[5:6]
     dist_row, env_row, angular = geometry(valid, seps)
+    yield
     weighted, value, slope = hidden_rows(sz, dist_row, env_row, in_one)
+    yield
     radial = mm(out_one, weighted)
     chosen = iota((first * n, lanes), 0) == target_row
     one_hot = jnp.where(chosen, valid, 0.0).astype(bf16)
     xt = mm(own_turned, one_hot)
     sources = jnp.where(iota((count, lanes), 0) == atom_row, valid, 0.0).astype(bf16)
+    yield
     spread = mm(gathered[...], sources)
+    yield
     parts = [spread[m * ch : (m + 1) * ch] for m in range(9)]
     vector = angular[1] * parts[1] + angular[2] * parts[2] + angular[3] * parts[3]
     tensor = angular[4] * parts[4]
@@ -676,10 +742,12 @@
         jnp.sum(parts[m] * products[1 if m < 4 else 2], axis=0, keepdims=True)
         for m in range(1, 9)
     ]
+    yield
     dist_grad, env_grad = radial_backward(
         sz, dist_row, radial_grad, value, slope, back_in, back_out
     )
     grads = separation_grads(valid, seps, dist_row, ang_grad, dist_grad, env_grad)
+    yield
     feature_acc[...] += nt(one_hot, input_grad)
     got = nt(one_hot, stacked_seps(list(grads)))
     pos_acc[...] += got[:, :8] + got[:, 8:]
@@ -689,7 +757,7 @@
     sz, total, before, after, kept, code, atom, sep, table,
     wide_in, wide_out, turned_in, turned_out, mixing,
     feature_grad, forces,
-    hot, xt, angular, dist, env, ang_grad, dist_grad, env_grad, sep_grad,
+    angular, dist, env, ang_grad, dist_grad, env_grad,
     acc, acc_pos, halo_acc, halo_pos, target, place, gathered,
 ):
     ch, n = sz.channels, sz.slots
@@ -707,7 +775,6 @@
     back_in, back_out = turned_in[0], turned_out[0]
     owned = len(sz.own)
     every = list(range(owned))
-    index = iota((sz.window, sz.edges), 0)
     acc[...] = jnp.zeros_like(acc)
     acc_pos[...] = jnp.zeros_like(acc_pos)
     halo_acc[...] = jnp.zeros_like(halo_acc)
@@ -717,39 +784,41 @@
         row = sz.inner_row(a, b)
         return inv[row : row + n]
 
-    turned = [inner_window(sz, table, a, b).astype(f32).T.astype(bf16) for a, b in sz.own]
-
-    def back_part(part, carry):
+    turned = table[...].astype(f32).T.astype(bf16)
+
+    def back_steps(part):
         seps = [sep[part, d, :owned] for d in range(3)]
         store_geometry(part, live_rows(code[part, :owned]), seps, dist, env, angular)
-        hots = [
-            (index == code[part, pl.ds(k, 1), :]).astype(f32).astype(bf16) for k in every
-        ]
-        for k in every:
-            hot[part, k] = hots[k]
+        one_hot = own_hot(sz, code[part, :owned])
+        found = mm(turned, one_hot)
         rows = [
             jnp.concatenate([ref[part, pl.ds(k, 1), :] for k in every], axis=1)
             for ref in (dist, env)
         ]
+        yield
         weighted, value, slope = hidden_rows(sz, *rows, in_one)
+        yield
         radials = mm(out_one, weighted)
-        got = layer_backward(
+        yield
+        input_grad, got = yield from layer_backward(
             sz, part, every, angular, dist, atom, back_in, back_out,
             [radials[:, k * sz.edges : (k + 1) * sz.edges] for k in every],
             value, slope,
-            [mm(turned[k], hots[k]) for k in every],
-            hots,
+            [found[:, k * sz.edges : (k + 1) * sz.edges] for k in every],
             [kept[k] for k in every],
             [inv_rows(*sz.own[k]) for k in every],
         )
         for k, value in zip(every, got):
-            store_grads(sz, k, value, ang_grad, dist_grad, env_grad, acc)
+            store_grads(sz, k, value, ang_grad, dist_grad, env_grad)
+        acc[...] += nt(one_hot, input_grad)
         own_positions(
-            sz, part, code, atom, sep, dist, hot, ang_grad, dist_grad, env_grad, sep_grad, acc_pos
+            sz, part, code, atom, sep, dist, one_hot, ang_grad, dist_grad, env_grad, acc_pos
         )
+
+    def back_part(part, carry):
+        run_steps(back_steps(part))
         return carry
 
-    lax.fori_loop(0, edge_parts, back_part, 0)
     halo_grads = [
         message_grads(sz, kept[owned + h], inv_rows(a, b)) for h, (a, b) in enumerate(sz.halo)
     ]
@@ -763,14 +832,19 @@
     own_turned = jnp.concatenate(own_rows, axis=0).astype(f32).T.astype(bf16)
     weights = (in_one, out_one, back_in, back_out)
 
-    def halo_part(part, carry):
-        halo_back(
+    def halo_steps(part):
+        return halo_back(
             sz, part, edge_parts, own_turned, atom, sep, gathered, weights, target, place,
             halo_acc, halo_pos,
         )
+
+    def halo_part(part, carry):
+        run_steps(halo_steps(part))
         return carry
 
-    lax.fori_loop(0, halo_parts, halo_part, 0)
+    run_steps(back_steps(0), halo_steps(0))
+    lax.fori_loop(1, edge_parts, back_part, 0)
+    lax.fori_loop(1, halo_parts, halo_part, 0)
     for a in range(sz.cols_x):
         inner = sz.inner_row(a + 1, 1)
         rows = sz.cols_y * n
@@ -833,7 +907,6 @@
         pltpu.VMEM((9, owned, edges), f32),
         pltpu.VMEM((owned, edges), f32),
         pltpu.VMEM((owned, edges), f32),
-        pltpu.VMEM((3, owned, edges), f32),
     ]
     weights = prepared(radial_in, radial_out, mixing)
     assert slots * neigh <= 2 * edges
@@ -846,8 +919,6 @@
 
     def edge_scratch(count):
         return [
-            pltpu.VMEM((2, owned, sz.window, edges), bf16),
-            pltpu.VMEM((count, channels, edges), f32),
             pltpu.VMEM((2, 9, count, edges), f32),
             pltpu.VMEM((2, count, edges), f32),
             pltpu.VMEM((2, count, edges), f32),
@@ -864,6 +935,10 @@
         in_specs=[vmem] * 9,
         out_specs=[vmem] * 7,
         scratch_shapes=[pltpu.VMEM(((cols_x + 4) * (cols_y + 4) * slots, 2 * channels), bf16)]
+        + [
+            pltpu.VMEM((2, inner_atoms, owned * edges), bf16),
+            pltpu.VMEM((columns, channels, edges), f32),
+        ]
         + edge_scratch(columns)
         + [
             pltpu.VMEM((inner_atoms, channels), bf16),

time: 44.2 us -> 42.3 us (0.957)
  Pallas kernels: 15.4 us -> 13.5 us
    pallas_call x1, Pallas kernels: 8.48 us -> 7.46 us  [shards(): pl.pallas_call(functools.partial(first_kernel, sz), out_shape=[jax.ShapeD...]
    pallas_call x1, Pallas kernels: 5.19 us -> 4.33 us  [shards(): pl.pallas_call(functools.partial(second_kernel, sz), out_shape=(jax.Shape...]
  transfers between devices with their start and end apart: 8 -> 8, of which waited for: 6 -> 6; matrix products, arithmetic and copies ran while one was open for 7% -> 8% of each run, Pallas kernels for 0% -> 0%
where the time goes in v5:
time: 42.3 us; the launch traced here: 42 us
  Pallas kernels  13.5 us (32%)
  waiting for transfers between devices  12.6 us (30%)
  starting transfers between devices  11.9 us (28%)
  other arithmetic  2.9 us (7%)
  between operations  0.74 us (2%)
    ppermute x8, waiting for transfers between devices, both_ways(): return (lax.ppermute(last, axis, up), lax.ppermute(first, axis, down))  12.6 us
    ppermute x8, starting transfers between devices, both_ways(): return (lax.ppermute(last, axis, up), lax.ppermute(first, axis, down))  11.9 us
    pallas_call x1, Pallas kernels, shards(): pl.pallas_call(functools.partial(first_kernel, sz), out_shape=[jax.ShapeD...  7.46 us
    pallas_call x1, Pallas kernels, shards(): pl.pallas_call(functools.partial(second_kernel, sz), out_shape=(jax.Shape...  4.33 us
    pallas_call x1, Pallas kernels, shards(): pl.pallas_call(functools.partial(block_kernel, sz, species_gain.shape[0])...  1.72 us
    another operation x2, other arithmetic  1.65 us
    another operation x2, other arithmetic, prepared(): mix = jnp.stack([high_mix, low_mix], axis=1)  1.1 us
  transfers between devices with their start and end apart: 8, of which 6 were waited for; matrix products, arithmetic and copies ran while one was open for 8% of the time, Pallas kernels for 0%

profile of v5, /device:TPU:0, one launch (start us, length us, event | category | flops | bytes accessed | tf_op | source)
XLA Modules:
  0.0 42.0 jit_solution(13313551069211268457)
XLA Ops:
  0.6 1.7 %block_of_atoms.1 = bf16[2,3,16,128]{3,2,1,0:T(8,128)(2,1)} custom-call(bf16[2,2,16,128]{3,2,1,0:T(8,128)(2,1)} %refs_0_.1, f32[2,3,2,16]{3,2,1,0:T(2,128)} %bitcast.15, s32[2,2,16]{2,1,0:T(2,128)} %refs_2_.1, s32[2,2,16,32]{3,2,1,0:T(8,128)} %refs_3_.1, s32[2,2,16]{2,1,0:T(2,128)} %refs_4_.1, f32[6,128]{1,0:T(8,128)} %refs_5_.1), custom_call_target="tpu_custom_call" | custom-call | tf_op jit(solution)/shard_map/block_of_atoms/pallas_call | solution.py:887
  2.4 6.0 %collective-permute-start.1 = (bf16[2,3,16,128]{3,2,1,0:T(8,128)(2,1)}, bf16[2,3,16,128]{3,2,1,0:T(8,128)(2,1)S(1)}, u32[]{:S(2)}, u32[]{:S(2)}) collective-permute-start(bf16[2,3,16,128]{3,2,1,0:T(8,128)(2,1)} %block_of_atoms.1), channel_id=1, source_target_pairs={{4,0},{8,4},{12,8},{16,12},{20,16},{24,20},{28,24},{0,28},{5,1},{9... | collective-permute-start | bytes 73736 | tf_op jit(solution)/shard_map/ppermute | solution.py:873
  8.4 0.0 collective-permute-start
  8.4 0.7 %reduce-precision_convert_fusion.2 = (bf16[2,8,64]{2,1,0:T(8,128)(2,1)S(1)}, bf16[2,8,64]{2,1,0:T(8,128)(2,1)S(1)}) fusion(f32[2,8,64]{2,1,0:T(8,128)} %param.16), kind=kLoop, calls=%fused_computation.14 | loop fusion | flops 4096 | bytes 8192 | tf_op jit(solution)/shard_map/convert.9
  9.1 1.0 %reduce-precision_convert_fusion.1 = (bf16[2,64,384]{2,1,0:T(8,128)(2,1)S(1)}, bf16[2,64,384]{2,1,0:T(8,128)(2,1)S(1)}) fusion(f32[2,64,384]{2,1,0:T(8,128)} %param.17), kind=kLoop, calls=%fused_computation.6 | loop fusion | flops 196608 | bytes 393216 | tf_op jit(solution)/shard_map/convert.6
  10.0 1.1 %fusion.3 = (bf16[2,1,384,128]{3,2,1,0:T(8,128)(2,1)S(1)}, bf16[2,1,384,128]{3,2,1,0:T(8,128)(2,1)S(1)}) fusion(f32[2,384,128]{2,1,0:T(8,128)} %param.18), kind=kLoop, calls=%fused_computation.9 | loop fusion | flops 393216 | bytes 786432 | tf_op jit(solution)/shard_map/stack | solution.py:52
  11.1 0.0 copy-start.1
  11.1 0.0 copy-start
  11.1 0.1 pad.12.clone
  11.3 0.1 maximum_bitcast_fusion.1
  11.4 0.1 copy.14.wide_in
  11.5 0.2 copy.15.wide_out
  11.7 0.0 collective-permute-done.1
  11.7 3.4 %collective-permute-done = bf16[2,3,16,128]{3,2,1,0:T(8,128)(2,1)S(1)} collective-permute-done((bf16[2,3,16,128]{3,2,1,0:T(8,128)(2,1)}, bf16[2,3,16,128]{3,2,1,0:T(8,128)(2,1)S(1)}, u32[]{:S(2)}, u32[]{:S(2)}) %collective-permute-start) | collective-permute-done | bytes 24608 | tf_op jit(solution)/shard_map/ppermute | solution.py:873
  15.1 0.0 copy-done.1
  15.1 0.1 collective-permute-start.3
  15.2 0.5 %collective-permute-start.2 = (bf16[6,3,16,128]{3,2,1,0:T(8,128)(2,1)S(1)}, bf16[6,3,16,128]{3,2,1,0:T(8,128)(2,1)S(1)}, u32[]{:S(2)}, u32[]{:S(2)}) collective-permute-start(bf16[6,3,16,128]{3,2,1,0:T(8,128)(2,1)S(1)} %pad_maximum_fusion.1.middle), channel_id=1, source_target_pairs={{0,1},{1,2},{2,3},{3,0},{4,5},{5,6},{6,7},{7,4},{8,9},{9,10},{10,1... | collective-permute-start | bytes 221192 | tf_op jit(solution)/shard_map/ppermute | solution.py:873
  15.7 1.5 %collective-permute-done.3.after = bf16[6,3,16,128]{3,2,1,0:T(8,128)(2,1)S(1)} collective-permute-done((bf16[6,3,16,128]{3,2,1,0:T(8,128)(2,1)S(1)}, bf16[6,3,16,128]{3,2,1,0:T(8,128)(2,1)S(1)}, u32[]{:S(2)}, u32[]{:S(2)}) %collective-permute-start.3) | collective-permute-done | bytes 73760 | tf_op jit(solution)/shard_map/ppermute | solution.py:873
  17.2 2.6 %collective-permute-done.2.before = bf16[6,3,16,128]{3,2,1,0:T(8,128)(2,1)S(1)} collective-permute-done((bf16[6,3,16,128]{3,2,1,0:T(8,128)(2,1)S(1)}, bf16[6,3,16,128]{3,2,1,0:T(8,128)(2,1)S(1)}, u32[]{:S(2)}, u32[]{:S(2)}) %collective-permute-start.2) | collective-permute-done | bytes 73760 | tf_op jit(solution)/shard_map/ppermute | solution.py:873
  19.8 0.0 copy-done
  19.8 7.5 %forward_and_second_back.1 = (f32[2,2,16]{2,1,0:T(2,128)}, bf16[4,5,16,128]{3,2,1,0:T(8,128)(2,1)S(1)}, f32[16,144,128]{2,1,0:T(8,128)S(1)}, f32[2,16,256]{2,1,0...) custom-call(bf16[6,3,16,128]{3,2,1,0:T(8,128)(2,1)S(1)} %collective-permute-do, ...), custom_call_target="tpu_custom_call" | custom-call | tf_op jit(solution)/shard_map/forward_and_second_back/pallas_call | solution.py:927
  27.3 0.0 collective-permute-start.4
  27.3 4.7 %collective-permute-start.5 = (bf16[2,5,16,128]{3,2,1,0:T(8,128)(2,1)S(1)}, bf16[2,5,16,128]{3,2,1,0:T(8,128)(2,1)S(1)}, u32[]{:S(2)}, u32[]{:S(2)}) collective-permute-start(bf16[2,5,16,128]{3,2,1,0:T(8,128)(2,1)S(1)} %get-tuple-element.30), channel_id=1, source_target_pairs={{4,0},{8,4},{12,8},{16,12},{20,16},{24,20},{28,24},{0,28},{5,1},{9... | collective-permute-start | bytes 122888 | tf_op jit(solution)/shard_map/ppermute | solution.py:873
  32.0 2.0 %collective-permute-done.4 = bf16[2,5,16,128]{3,2,1,0:T(8,128)(2,1)S(1)} collective-permute-done((bf16[2,5,16,128]{3,2,1,0:T(8,128)(2,1)S(1)}, bf16[2,5,16,128]{3,2,1,0:T(8,128)(2,1)S(1)}, u32[]{:S(2)}, u32[]{:S(2)}) %collective-permute-start.4) | collective-permute-done | bytes 40992 | tf_op jit(solution)/shard_map/ppermute | solution.py:873
  34.0 0.0 collective-permute-done.5
  34.0 0.1 collective-permute-start.7
  34.1 0.5 %collective-permute-start.6 = (bf16[4,3,16,128]{3,2,1,0:T(8,128)(2,1)S(1)}, bf16[4,3,16,128]{3,2,1,0:T(8,128)(2,1)S(1)}, u32[]{:S(2)}, u32[]{:S(2)}) collective-permute-start(bf16[4,3,16,128]{3,2,1,0:T(8,128)(2,1)S(1)} %get-tuple-element.28), channel_id=1, source_target_pairs={{0,1},{1,2},{2,3},{3,0},{4,5},{5,6},{6,7},{7,4},{8,9},{9,10},{10,1... | collective-permute-start | bytes 147464 | tf_op jit(solution)/shard_map/ppermute | solution.py:873
  34.6 1.4 %collective-permute-done.7.after = bf16[4,3,16,128]{3,2,1,0:T(8,128)(2,1)S(1)} collective-permute-done((bf16[4,3,16,128]{3,2,1,0:T(8,128)(2,1)S(1)}, bf16[4,3,16,128]{3,2,1,0:T(8,128)(2,1)S(1)}, u32[]{:S(2)}, u32[]{:S(2)}) %collective-permute-start.7) | collective-permute-done | bytes 49184 | tf_op jit(solution)/shard_map/ppermute | solution.py:873
  36.0 1.7 %collective-permute-done.6.before = bf16[4,3,16,128]{3,2,1,0:T(8,128)(2,1)S(1)} collective-permute-done((bf16[4,3,16,128]{3,2,1,0:T(8,128)(2,1)S(1)}, bf16[4,3,16,128]{3,2,1,0:T(8,128)(2,1)S(1)}, u32[]{:S(2)}, u32[]{:S(2)}) %collective-permute-start.6) | collective-permute-done | bytes 49184 | tf_op jit(solution)/shard_map/ppermute | solution.py:873
  37.7 4.3 %first_back.1 = (f32[64,128]{1,0:T(8,128)}, f32[2,3,2,16]{3,2,1,0:T(2,128)}) custom-call(f32[4,5,16,128]{3,2,1,0:T(8,128)S(1)} %get-tuple-element.26.total, bf16[4,3,16,128]{3,2,1,0:T(8,128)(2,1)S(1)} %collective-permute-done.6.before, bf16[4,3,16,128]{3,2,1,0:T(8,128)(2,1)S(1)} %collective-permute-done.7.after, f32[16,144,128]{2,1,0:T(8,128)S(1)} %get-tuple-element.14.kept, ...), custom_call_target="tpu_custom_call" | custom-call | tf_op jit(solution)/shard_map/first_back/pallas_call | solution.py:961
  (8 shorter events, 0.1 us)
Async XLA Ops:
  2.4 9.3 %collective-permute-start.1 = (bf16[2,3,16,128]{3,2,1,0:T(8,128)(2,1)}, bf16[2,3,16,128]{3,2,1,0:T(8,128)(2,1)S(1)}, u32[]{:S(2)}, u32[]{:S(2)}) collective-permute-start(bf16[2,3,16,128]{3,2,1,0:T(8,128)(2,1)} %block_of_atoms.1), channel_id=1, source_target_pairs={{4,0},{8,4},{12,8},{16,12},{20,16},{24,20},{28,24},{0,28},{5,1},{9... | collective-permute-start | bytes 73736 | tf_op jit(solution)/shard_map/ppermute | solution.py:873
  8.4 6.7 %collective-permute-start = (bf16[2,3,16,128]{3,2,1,0:T(8,128)(2,1)}, bf16[2,3,16,128]{3,2,1,0:T(8,128)(2,1)S(1)}, u32[]{:S(2)}, u32[]{:S(2)}) collective-permute-start(bf16[2,3,16,128]{3,2,1,0:T(8,128)(2,1)} %block_of_atoms.1), channel_id=1, source_target_pairs={{0,4},{4,8},{8,12},{12,16},{16,20},{20,24},{24,28},{28,0},{1,5},{5... | collective-permute-start | bytes 73736 | tf_op jit(solution)/shard_map/ppermute | solution.py:873
  11.1 4.0 %copy-start.1 = (bf16[2,3,16,128]{3,2,1,0:T(8,128)(2,1)S(1)}, bf16[2,3,16,128]{3,2,1,0:T(8,128)(2,1)}, u32[]{:S(2)}) copy-start(bf16[2,3,16,128]{3,2,1,0:T(8,128)(2,1)} %block_of_atoms.1) | copy-start | bytes 73732
  11.1 8.7 %copy-start = (f32[128]{0:T(128)S(1)}, f32[128]{0:T(128)}, u32[]{:S(2)}) copy-start(f32[128]{0:T(128)} %param.19) | copy-start | bytes 1540
  15.1 2.0 %collective-permute-start.3 = (bf16[6,3,16,128]{3,2,1,0:T(8,128)(2,1)S(1)}, bf16[6,3,16,128]{3,2,1,0:T(8,128)(2,1)S(1)}, u32[]{:S(2)}, u32[]{:S(2)}) collective-permute-start(bf16[6,3,16,128]{3,2,1,0:T(8,128)(2,1)S(1)} %pad_maximum_fusion.1.middle), channel_id=1, source_target_pairs={{1,0},{2,1},{3,2},{0,3},{5,4},{6,5},{7,6},{4,7},{9,8},{10,9},{11,1... | collective-permute-start | bytes 221192 | tf_op jit(solution)/shard_map/ppermute | solution.py:873
  15.2 4.6 %collective-permute-start.2 = (bf16[6,3,16,128]{3,2,1,0:T(8,128)(2,1)S(1)}, bf16[6,3,16,128]{3,2,1,0:T(8,128)(2,1)S(1)}, u32[]{:S(2)}, u32[]{:S(2)}) collective-permute-start(bf16[6,3,16,128]{3,2,1,0:T(8,128)(2,1)S(1)} %pad_maximum_fusion.1.middle), channel_id=1, source_target_pairs={{0,1},{1,2},{2,3},{3,0},{4,5},{5,6},{6,7},{7,4},{8,9},{9,10},{10,1... | collective-permute-start | bytes 221192 | tf_op jit(solution)/shard_map/ppermute | solution.py:873
  27.3 6.7 %collective-permute-start.4 = (bf16[2,5,16,128]{3,2,1,0:T(8,128)(2,1)S(1)}, bf16[2,5,16,128]{3,2,1,0:T(8,128)(2,1)S(1)}, u32[]{:S(2)}, u32[]{:S(2)}) collective-permute-start(bf16[2,5,16,128]{3,2,1,0:T(8,128)(2,1)S(1)} %get-tuple-element.29), channel_id=1, source_target_pairs={{0,4},{4,8},{8,12},{12,16},{16,20},{20,24},{24,28},{28,0},{1,5},{5... | collective-permute-start | bytes 122888 | tf_op jit(solution)/shard_map/ppermute | solution.py:873
  27.3 6.7 %collective-permute-start.5 = (bf16[2,5,16,128]{3,2,1,0:T(8,128)(2,1)S(1)}, bf16[2,5,16,128]{3,2,1,0:T(8,128)(2,1)S(1)}, u32[]{:S(2)}, u32[]{:S(2)}) collective-permute-start(bf16[2,5,16,128]{3,2,1,0:T(8,128)(2,1)S(1)} %get-tuple-element.30), channel_id=1, source_target_pairs={{4,0},{8,4},{12,8},{16,12},{20,16},{24,20},{28,24},{0,28},{5,1},{9... | collective-permute-start | bytes 122888 | tf_op jit(solution)/shard_map/ppermute | solution.py:873
  34.0 2.0 %collective-permute-start.7 = (bf16[4,3,16,128]{3,2,1,0:T(8,128)(2,1)S(1)}, bf16[4,3,16,128]{3,2,1,0:T(8,128)(2,1)S(1)}, u32[]{:S(2)}, u32[]{:S(2)}) collective-permute-start(bf16[4,3,16,128]{3,2,1,0:T(8,128)(2,1)S(1)} %get-tuple-element.27), channel_id=1, source_target_pairs={{1,0},{2,1},{3,2},{0,3},{5,4},{6,5},{7,6},{4,7},{9,8},{10,9},{11,1... | collective-permute-start | bytes 147464 | tf_op jit(solution)/shard_map/ppermute | solution.py:873
  34.1 3.6 %collective-permute-start.6 = (bf16[4,3,16,128]{3,2,1,0:T(8,128)(2,1)S(1)}, bf16[4,3,16,128]{3,2,1,0:T(8,128)(2,1)S(1)}, u32[]{:S(2)}, u32[]{:S(2)}) collective-permute-start(bf16[4,3,16,128]{3,2,1,0:T(8,128)(2,1)S(1)} %get-tuple-element.28), channel_id=1, source_target_pairs={{0,1},{1,2},{2,3},{3,0},{4,5},{5,6},{6,7},{7,4},{8,9},{9,10},{10,1... | collective-permute-start | bytes 147464 | tf_op jit(solution)/shard_map/ppermute | solution.py:873

commit v6 on v5

--- a/solution.py
+++ b/solution.py
@@ -710,7 +710,12 @@
             sides.append(
                 jnp.concatenate([high, middle, rows - high - middle], axis=0).astype(bf16)
             )
-        return total + nt(jnp.concatenate(sides, axis=1), jnp.concatenate(picks, axis=1))
+        middle = len(picks) // 2
+        for span in (slice(0, middle), slice(middle, None)):
+            total = total + nt(
+                jnp.concatenate(sides[span], axis=1), jnp.concatenate(picks[span], axis=1)
+            )
+        return total
 
     got = packed(0, jnp.zeros((24, lanes), f32))
     yield
@@ -728,7 +733,8 @@
     xt = mm(own_turned, one_hot)
     sources = jnp.where(iota((count, lanes), 0) == atom_row, valid, 0.0).astype(bf16)
     yield
-    spread = mm(gathered[...], sources)
+    rows = gathered.shape[0] // 2
+    spread = jnp.concatenate([mm(gathered[:rows], sources), mm(gathered[rows:], sources)], axis=0)
     yield
     parts = [spread[m * ch : (m + 1) * ch] for m in range(9)]
     vector = angular[1] * parts[1] + angular[2] * parts[2] + angular[3] * parts[3]
@@ -862,15 +868,18 @@
             forces[a, :, b, :] = -(place_grad.T)[:3]
 
 
-def ring(axis):
+def both_ways(first, last, axis):
     devices = lax.axis_size(axis)
-    up = [(i, (i + 1) % devices) for i in range(devices)]
-    return up, [(j, i) for i, j in up]
-
-
-def both_ways(first, last, axis):
-    up, down = ring(axis)
-    return lax.ppermute(last, axis, up), lax.ppermute(first, axis, down)
+    near = [(i, i ^ 1) for i in range(devices)]
+    far = [(i, (i + 1 if i % 2 else i - 1) % devices) for i in range(devices)]
+    even = lax.axis_index(axis) % 2 == 0
+    if first is last:
+        to_near = to_far = first
+    else:
+        to_near, to_far = jnp.where(even, last, first), jnp.where(even, first, last)
+    from_far = lax.ppermute(to_far, axis, far)
+    from_near = lax.ppermute(to_near, axis, near)
+    return jnp.where(even, from_far, from_near), jnp.where(even, from_near, from_far)
 
 
 def shards(

time: 42.3 us -> 40 us (0.946)
  waiting for transfers between devices: 12.6 us -> 8.58 us
  starting transfers between devices: 11.9 us -> 13.3 us
    ppermute x8, waiting for transfers between devices: 12.6 us -> 8.58 us  [the longest x4 7.85 us: both_ways(): from_far = lax.ppermute(to_far, axis, far)]
    ppermute x8, starting transfers between devices: 11.9 us -> 13.3 us  [the longest x4 10.2 us: both_ways(): from_far = lax.ppermute(to_far, axis, far)]
  transfers between devices with their start and end apart: 8 -> 8, of which waited for: 6 -> 4; matrix products, arithmetic and copies ran while one was open for 8% -> 8% of each run, Pallas kernels for 0% -> 0%
where the time goes in v6:
time: 40 us; the launch traced here: 39.7 us
  Pallas kernels  13.5 us (34%)
  starting transfers between devices  13.3 us (33%)
  waiting for transfers between devices  8.58 us (21%)
  other arithmetic  2.98 us (7%)
  between operations  0.79 us (2%)
  local copies, waits for them, and re-layouts  0.51 us (1%)
    ppermute x4, starting transfers between devices, both_ways(): from_far = lax.ppermute(to_far, axis, far)  10.2 us
    ppermute x4, waiting for transfers between devices, both_ways(): from_far = lax.ppermute(to_far, axis, far)  7.85 us
    pallas_call x1, Pallas kernels, shards(): pl.pallas_call(functools.partial(first_kernel, sz), out_shape=[jax.ShapeD...  7.56 us
    pallas_call x1, Pallas kernels, shards(): pl.pallas_call(functools.partial(second_kernel, sz), out_shape=(jax.Shape...  4.25 us
    ppermute x4, starting transfers between devices, both_ways(): from_near = lax.ppermute(to_near, axis, near)  3.15 us
    pallas_call x1, Pallas kernels, shards(): pl.pallas_call(functools.partial(block_kernel, sz, species_gain.shape[0])...  1.72 us
    another operation x2, other arithmetic  1.65 us
    another operation x2, other arithmetic, prepared(): mix = jnp.stack([high_mix, low_mix], axis=1)  1.1 us
  transfers between devices with their start and end apart: 8, of which 4 were waited for; matrix products, arithmetic and copies ran while one was open for 8% of the time, Pallas kernels for 0%

profile of v6, /device:TPU:0, one launch (start us, length us, event | category | flops | bytes accessed | tf_op | source)
XLA Modules:
  0.0 39.7 jit_solution(1410044255534883121)
XLA Ops:
  0.6 1.7 %block_of_atoms.1 = bf16[2,3,16,128]{3,2,1,0:T(8,128)(2,1)} custom-call(bf16[2,2,16,128]{3,2,1,0:T(8,128)(2,1)} %refs_0_.1, f32[2,3,2,16]{3,2,1,0:T(2,128)} %bitcast.15, s32[2,2,16]{2,1,0:T(2,128)} %refs_2_.1, s32[2,2,16,32]{3,2,1,0:T(8,128)} %refs_3_.1, s32[2,2,16]{2,1,0:T(2,128)} %refs_4_.1, f32[6,128]{1,0:T(8,128)} %refs_5_.1), custom_call_target="tpu_custom_call" | custom-call | tf_op jit(solution)/shard_map/block_of_atoms/pallas_call | solution.py:896
  2.4 3.0 %collective-permute-start.1 = (bf16[2,3,16,128]{3,2,1,0:T(8,128)(2,1)}, bf16[2,3,16,128]{3,2,1,0:T(8,128)(2,1)S(1)}, u32[]{:S(2)}, u32[]{:S(2)}) collective-permute-start(bf16[2,3,16,128]{3,2,1,0:T(8,128)(2,1)} %block_of_atoms.1), channel_id=1, source_target_pairs={{0,4},{4,0},{8,12},{12,8},{16,20},{20,16},{24,28},{28,24},{1,5},{5... | collective-permute-start | bytes 73736 | tf_op jit(solution)/shard_map/ppermute | solution.py:881
  5.4 3.6 %collective-permute-start = (bf16[2,3,16,128]{3,2,1,0:T(8,128)(2,1)}, bf16[2,3,16,128]{3,2,1,0:T(8,128)(2,1)S(1)}, u32[]{:S(2)}, u32[]{:S(2)}) collective-permute-start(bf16[2,3,16,128]{3,2,1,0:T(8,128)(2,1)} %block_of_atoms.1), channel_id=1, source_target_pairs={{0,28},{4,8},{8,4},{12,16},{16,12},{20,24},{24,20},{28,0},{1,29},{... | collective-permute-start | bytes 73736 | tf_op jit(solution)/shard_map/ppermute | solution.py:880
  8.9 0.7 %reduce-precision_convert_fusion.2 = (bf16[2,8,64]{2,1,0:T(8,128)(2,1)S(1)}, bf16[2,8,64]{2,1,0:T(8,128)(2,1)S(1)}) fusion(f32[2,8,64]{2,1,0:T(8,128)} %param.16), kind=kLoop, calls=%fused_computation.26 | loop fusion | flops 4096 | bytes 8192 | tf_op jit(solution)/shard_map/convert.9
  9.6 1.0 %reduce-precision_convert_fusion.1 = (bf16[2,64,384]{2,1,0:T(8,128)(2,1)S(1)}, bf16[2,64,384]{2,1,0:T(8,128)(2,1)S(1)}) fusion(f32[2,64,384]{2,1,0:T(8,128)} %param.17), kind=kLoop, calls=%fused_computation.6 | loop fusion | flops 196608 | bytes 393216 | tf_op jit(solution)/shard_map/convert.6
  10.6 1.1 %fusion.3 = (bf16[2,1,384,128]{3,2,1,0:T(8,128)(2,1)S(1)}, bf16[2,1,384,128]{3,2,1,0:T(8,128)(2,1)S(1)}) fusion(f32[2,384,128]{2,1,0:T(8,128)} %param.18), kind=kLoop, calls=%fused_computation.9 | loop fusion | flops 393216 | bytes 786432 | tf_op jit(solution)/shard_map/stack | solution.py:52
  11.7 0.0 copy-start.1
  11.7 0.1 pad.12.clone
  11.8 0.0 copy-start
  11.8 0.1 maximum_bitcast_fusion.1
  11.9 0.1 copy.14.wide_in
  12.0 0.2 copy.15.wide_out
  12.2 0.0 collective-permute-done.1
  12.2 0.0 collective-permute-done
  12.3 0.1 copy-done.1
  12.4 0.1 collective-permute-start.3
  12.5 1.6 %collective-permute-start.2 = (bf16[6,3,16,128]{3,2,1,0:T(8,128)(2,1)S(1)}, bf16[6,3,16,128]{3,2,1,0:T(8,128)(2,1)S(1)}, u32[]{:S(2)}, u32[]{:S(2)}) collective-permute-start(bf16[6,3,16,128]{3,2,1,0:T(8,128)(2,1)S(1)} %pad_maximum_fusion.1.middle), channel_id=1, source_target_pairs={{0,3},{1,2},{2,1},{3,0},{4,7},{5,6},{6,5},{7,4},{8,11},{9,10},{10,... | collective-permute-start | bytes 221192 | tf_op jit(solution)/shard_map/ppermute | solution.py:880
  14.1 0.0 collective-permute-done.3
  14.1 2.4 %collective-permute-done.2 = bf16[6,3,16,128]{3,2,1,0:T(8,128)(2,1)S(1)} collective-permute-done((bf16[6,3,16,128]{3,2,1,0:T(8,128)(2,1)S(1)}, bf16[6,3,16,128]{3,2,1,0:T(8,128)(2,1)S(1)}, u32[]{:S(2)}, u32[]{:S(2)}) %collective-permute-start.2) | collective-permute-done | bytes 73760 | tf_op jit(solution)/shard_map/ppermute | solution.py:880
  16.6 0.0 copy-done
  16.6 7.6 %forward_and_second_back.1 = (f32[2,2,16]{2,1,0:T(2,128)}, bf16[4,5,16,128]{3,2,1,0:T(8,128)(2,1)S(1)}, f32[16,144,128]{2,1,0:T(8,128)S(1)}, f32[2,16,256]{2,1,0...) custom-call(bf16[6,3,16,128]{3,2,1,0:T(8,128)(2,1)S(1)} %get-tuple-element.28., ...), custom_call_target="tpu_custom_call" | custom-call | tf_op jit(solution)/shard_map/forward_and_second_back/pallas_call | solution.py:936
  24.2 3.4 %collective-permute-start.4 = (bf16[2,5,16,128]{3,2,1,0:T(8,128)(2,1)S(1)}, bf16[2,5,16,128]{3,2,1,0:T(8,128)(2,1)S(1)}, u32[]{:S(2)}, u32[]{:S(2)}) collective-permute-start(bf16[2,5,16,128]{3,2,1,0:T(8,128)(2,1)S(1)} %get-tuple-element.35), channel_id=1, source_target_pairs={{0,28},{4,8},{8,4},{12,16},{16,12},{20,24},{24,20},{28,0},{1,29},{... | collective-permute-start | bytes 122888 | tf_op jit(solution)/shard_map/ppermute | solution.py:880
  27.5 0.0 collective-permute-start.5
  27.5 3.4 %collective-permute-done.4 = bf16[2,5,16,128]{3,2,1,0:T(8,128)(2,1)S(1)} collective-permute-done((bf16[2,5,16,128]{3,2,1,0:T(8,128)(2,1)S(1)}, bf16[2,5,16,128]{3,2,1,0:T(8,128)(2,1)S(1)}, u32[]{:S(2)}, u32[]{:S(2)}) %collective-permute-start.4) | collective-permute-done | bytes 40992 | tf_op jit(solution)/shard_map/ppermute | solution.py:880
  31.0 0.7 %collective-permute-done.5 = bf16[2,5,16,128]{3,2,1,0:T(8,128)(2,1)S(1)} collective-permute-done((bf16[2,5,16,128]{3,2,1,0:T(8,128)(2,1)S(1)}, bf16[2,5,16,128]{3,2,1,0:T(8,128)(2,1)S(1)}, u32[]{:S(2)}, u32[]{:S(2)}) %collective-permute-start.5) | collective-permute-done | bytes 40992 | tf_op jit(solution)/shard_map/ppermute | solution.py:881
  31.8 0.1 collective-permute-start.7
  31.8 1.6 %collective-permute-start.6 = (bf16[4,3,16,128]{3,2,1,0:T(8,128)(2,1)S(1)}, bf16[4,3,16,128]{3,2,1,0:T(8,128)(2,1)S(1)}, u32[]{:S(2)}, u32[]{:S(2)}) collective-permute-start(bf16[4,3,16,128]{3,2,1,0:T(8,128)(2,1)S(1)} %get-tuple-element.32), channel_id=1, source_target_pairs={{0,3},{1,2},{2,1},{3,0},{4,7},{5,6},{6,5},{7,4},{8,11},{9,10},{10,... | collective-permute-start | bytes 147464 | tf_op jit(solution)/shard_map/ppermute | solution.py:880
  33.4 0.0 collective-permute-done.7
  33.4 2.0 %collective-permute-done.6 = bf16[4,3,16,128]{3,2,1,0:T(8,128)(2,1)S(1)} collective-permute-done((bf16[4,3,16,128]{3,2,1,0:T(8,128)(2,1)S(1)}, bf16[4,3,16,128]{3,2,1,0:T(8,128)(2,1)S(1)}, u32[]{:S(2)}, u32[]{:S(2)}) %collective-permute-start.6) | collective-permute-done | bytes 49184 | tf_op jit(solution)/shard_map/ppermute | solution.py:880
  35.4 4.2 %first_back.1 = (f32[64,128]{1,0:T(8,128)}, f32[2,3,2,16]{3,2,1,0:T(2,128)}) custom-call(f32[4,5,16,128]{3,2,1,0:T(8,128)S(1)} %get-tuple-element.26.total, bf16[4,3,16,128]{3,2,1,0:T(8,128)(2,1)S(1)} %get-tuple-element.30.before, bf16[4,3,16,128]{3,2,1,0:T(8,128)(2,1)S(1)} %get-tuple-element.29.after, f32[16,144,128]{2,1,0:T(8,128)S(1)} %get-tuple-element.14.kept, ...), custom_call_target="tpu_custom_call" | custom-call | tf_op jit(solution)/shard_map/first_back/pallas_call | solution.py:970
  (12 shorter events, 0.2 us)
Async XLA Ops:
  2.4 9.9 %collective-permute-start.1 = (bf16[2,3,16,128]{3,2,1,0:T(8,128)(2,1)}, bf16[2,3,16,128]{3,2,1,0:T(8,128)(2,1)S(1)}, u32[]{:S(2)}, u32[]{:S(2)}) collective-permute-start(bf16[2,3,16,128]{3,2,1,0:T(8,128)(2,1)} %block_of_atoms.1), channel_id=1, source_target_pairs={{0,4},{4,0},{8,12},{12,8},{16,20},{20,16},{24,28},{28,24},{1,5},{5... | collective-permute-start | bytes 73736 | tf_op jit(solution)/shard_map/ppermute | solution.py:881
  5.4 6.9 %collective-permute-start = (bf16[2,3,16,128]{3,2,1,0:T(8,128)(2,1)}, bf16[2,3,16,128]{3,2,1,0:T(8,128)(2,1)S(1)}, u32[]{:S(2)}, u32[]{:S(2)}) collective-permute-start(bf16[2,3,16,128]{3,2,1,0:T(8,128)(2,1)} %block_of_atoms.1), channel_id=1, source_target_pairs={{0,28},{4,8},{8,4},{12,16},{16,12},{20,24},{24,20},{28,0},{1,29},{... | collective-permute-start | bytes 73736 | tf_op jit(solution)/shard_map/ppermute | solution.py:880
  11.7 0.7 %copy-start.1 = (bf16[2,3,16,128]{3,2,1,0:T(8,128)(2,1)S(1)}, bf16[2,3,16,128]{3,2,1,0:T(8,128)(2,1)}, u32[]{:S(2)}) copy-start(bf16[2,3,16,128]{3,2,1,0:T(8,128)(2,1)} %block_of_atoms.1) | copy-start | bytes 73732
  11.8 4.8 %copy-start = (f32[128]{0:T(128)S(1)}, f32[128]{0:T(128)}, u32[]{:S(2)}) copy-start(f32[128]{0:T(128)} %param.19) | copy-start | bytes 1540
  12.4 1.7 %collective-permute-start.3 = (bf16[6,3,16,128]{3,2,1,0:T(8,128)(2,1)S(1)}, bf16[6,3,16,128]{3,2,1,0:T(8,128)(2,1)S(1)}, u32[]{:S(2)}, u32[]{:S(2)}) collective-permute-start(bf16[6,3,16,128]{3,2,1,0:T(8,128)(2,1)S(1)} %pad_maximum_fusion.1.middle), channel_id=1, source_target_pairs={{0,1},{1,0},{2,3},{3,2},{4,5},{5,4},{6,7},{7,6},{8,9},{9,8},{10,11... | collective-permute-start | bytes 221192 | tf_op jit(solution)/shard_map/ppermute | solution.py:881
  12.5 4.1 %collective-permute-start.2 = (bf16[6,3,16,128]{3,2,1,0:T(8,128)(2,1)S(1)}, bf16[6,3,16,128]{3,2,1,0:T(8,128)(2,1)S(1)}, u32[]{:S(2)}, u32[]{:S(2)}) collective-permute-start(bf16[6,3,16,128]{3,2,1,0:T(8,128)(2,1)S(1)} %pad_maximum_fusion.1.middle), channel_id=1, source_target_pairs={{0,3},{1,2},{2,1},{3,0},{4,7},{5,6},{6,5},{7,4},{8,11},{9,10},{10,... | collective-permute-start | bytes 221192 | tf_op jit(solution)/shard_map/ppermute | solution.py:880
  24.2 6.8 %collective-permute-start.4 = (bf16[2,5,16,128]{3,2,1,0:T(8,128)(2,1)S(1)}, bf16[2,5,16,128]{3,2,1,0:T(8,128)(2,1)S(1)}, u32[]{:S(2)}, u32[]{:S(2)}) collective-permute-start(bf16[2,5,16,128]{3,2,1,0:T(8,128)(2,1)S(1)} %get-tuple-element.35), channel_id=1, source_target_pairs={{0,28},{4,8},{8,4},{12,16},{16,12},{20,24},{24,20},{28,0},{1,29},{... | collective-permute-start | bytes 122888 | tf_op jit(solution)/shard_map/ppermute | solution.py:880
  27.5 4.2 %collective-permute-start.5 = (bf16[2,5,16,128]{3,2,1,0:T(8,128)(2,1)S(1)}, bf16[2,5,16,128]{3,2,1,0:T(8,128)(2,1)S(1)}, u32[]{:S(2)}, u32[]{:S(2)}) collective-permute-start(bf16[2,5,16,128]{3,2,1,0:T(8,128)(2,1)S(1)} %get-tuple-element.36), channel_id=1, source_target_pairs={{0,4},{4,0},{8,12},{12,8},{16,20},{20,16},{24,28},{28,24},{1,5},{5... | collective-permute-start | bytes 122888 | tf_op jit(solution)/shard_map/ppermute | solution.py:881
  31.8 1.7 %collective-permute-start.7 = (bf16[4,3,16,128]{3,2,1,0:T(8,128)(2,1)S(1)}, bf16[4,3,16,128]{3,2,1,0:T(8,128)(2,1)S(1)}, u32[]{:S(2)}, u32[]{:S(2)}) collective-permute-start(bf16[4,3,16,128]{3,2,1,0:T(8,128)(2,1)S(1)} %get-tuple-element.31), channel_id=1, source_target_pairs={{0,1},{1,0},{2,3},{3,2},{4,5},{5,4},{6,7},{7,6},{8,9},{9,8},{10,11... | collective-permute-start | bytes 147464 | tf_op jit(solution)/shard_map/ppermute | solution.py:881
  31.8 3.6 %collective-permute-start.6 = (bf16[4,3,16,128]{3,2,1,0:T(8,128)(2,1)S(1)}, bf16[4,3,16,128]{3,2,1,0:T(8,128)(2,1)S(1)}, u32[]{:S(2)}, u32[]{:S(2)}) collective-permute-start(bf16[4,3,16,128]{3,2,1,0:T(8,128)(2,1)S(1)} %get-tuple-element.32), channel_id=1, source_target_pairs={{0,3},{1,2},{2,1},{3,0},{4,7},{5,6},{6,5},{7,4},{8,11},{9,10},{10,... | collective-permute-start | bytes 147464 | tf_op jit(solution)/shard_map/ppermute | solution.py:880

commit v7 on v6

--- a/solution.py
+++ b/solution.py
@@ -605,9 +605,6 @@
     out = three(mm, inv, mixing[1]) + jnp.concatenate(own_rows, axis=0).astype(f32)
     gate = sigmoid(out)
     weights = readout[...]
-    total = three(nt, jnp.ones((8, ch), f32), out * gate * weights)
-    for k, (a, b) in enumerate(sz.own):
-        energy[a - 1, b - 1 : b, :] = total[0:1, k * n : (k + 1) * n]
     out_grad = gate * (1.0 + out * (1.0 - gate)) * weights
     cotangents = three(nt, out_grad, mixing[1])
     acc[...] = jnp.zeros_like(acc)
@@ -633,8 +630,15 @@
             sz, part, code, atom, sep, dist, hot[part], ang_grad, dist_grad, env_grad, acc_pos
         )
 
+    def energy_steps():
+        yield
+        total = three(nt, jnp.ones((8, ch), f32), out * gate * weights)
+        yield
+        for k, (a, b) in enumerate(sz.own):
+            energy[a - 1, b - 1 : b, :] = total[0:1, k * n : (k + 1) * n]
+
     def back_part(part, carry):
-        run_steps(back_steps(part))
+        run_steps(back_steps(part), energy_steps())
         return carry
 
     lax.fori_loop(0, parts, back_part, 0)

time: 40 us -> 40.1 us (level)
  no operation moved by 1% of the time
where the time goes in v7:
time: 40.1 us; the launch traced here: 39.7 us
  Pallas kernels  13.6 us (34%)
  starting transfers between devices  13.3 us (33%)
  waiting for transfers between devices  8.58 us (21%)
  other arithmetic  2.98 us (7%)
  between operations  0.79 us (2%)
  local copies, waits for them, and re-layouts  0.51 us (1%)
    ppermute x4, starting transfers between devices, both_ways(): from_far = lax.ppermute(to_far, axis, far)  10.2 us
    ppermute x4, waiting for transfers between devices, both_ways(): from_far = lax.ppermute(to_far, axis, far)  7.85 us
    pallas_call x1, Pallas kernels, shards(): pl.pallas_call(functools.partial(first_kernel, sz), out_shape=[jax.ShapeD...  7.61 us
    pallas_call x1, Pallas kernels, shards(): pl.pallas_call(functools.partial(second_kernel, sz), out_shape=(jax.Shape...  4.24 us
    ppermute x4, starting transfers between devices, both_ways(): from_near = lax.ppermute(to_near, axis, near)  3.15 us
    pallas_call x1, Pallas kernels, shards(): pl.pallas_call(functools.partial(block_kernel, sz, species_gain.shape[0])...  1.72 us
    another operation x2, other arithmetic  1.65 us
    another operation x2, other arithmetic, prepared(): mix = jnp.stack([high_mix, low_mix], axis=1)  1.1 us
  transfers between devices with their start and end apart: 8, of which 4 were waited for; matrix products, arithmetic and copies ran while one was open for 8% of the time, Pallas kernels for 0%

profile of v7, /device:TPU:0, one launch (start us, length us, event | category | flops | bytes accessed | tf_op | source)
XLA Modules:
  0.0 39.7 jit_solution(7396866101243262437)
XLA Ops:
  0.6 1.7 %block_of_atoms.1 = bf16[2,3,16,128]{3,2,1,0:T(8,128)(2,1)} custom-call(bf16[2,2,16,128]{3,2,1,0:T(8,128)(2,1)} %refs_0_.1, f32[2,3,2,16]{3,2,1,0:T(2,128)} %bitcast.15, s32[2,2,16]{2,1,0:T(2,128)} %refs_2_.1, s32[2,2,16,32]{3,2,1,0:T(8,128)} %refs_3_.1, s32[2,2,16]{2,1,0:T(2,128)} %refs_4_.1, f32[6,128]{1,0:T(8,128)} %refs_5_.1), custom_call_target="tpu_custom_call" | custom-call | tf_op jit(solution)/shard_map/block_of_atoms/pallas_call | solution.py:900
  2.4 3.0 %collective-permute-start.1 = (bf16[2,3,16,128]{3,2,1,0:T(8,128)(2,1)}, bf16[2,3,16,128]{3,2,1,0:T(8,128)(2,1)S(1)}, u32[]{:S(2)}, u32[]{:S(2)}) collective-permute-start(bf16[2,3,16,128]{3,2,1,0:T(8,128)(2,1)} %block_of_atoms.1), channel_id=1, source_target_pairs={{0,4},{4,0},{8,12},{12,8},{16,20},{20,16},{24,28},{28,24},{1,5},{5... | collective-permute-start | bytes 73736 | tf_op jit(solution)/shard_map/ppermute | solution.py:885
  5.4 3.6 %collective-permute-start = (bf16[2,3,16,128]{3,2,1,0:T(8,128)(2,1)}, bf16[2,3,16,128]{3,2,1,0:T(8,128)(2,1)S(1)}, u32[]{:S(2)}, u32[]{:S(2)}) collective-permute-start(bf16[2,3,16,128]{3,2,1,0:T(8,128)(2,1)} %block_of_atoms.1), channel_id=1, source_target_pairs={{0,28},{4,8},{8,4},{12,16},{16,12},{20,24},{24,20},{28,0},{1,29},{... | collective-permute-start | bytes 73736 | tf_op jit(solution)/shard_map/ppermute | solution.py:884
  8.9 0.7 %reduce-precision_convert_fusion.2 = (bf16[2,8,64]{2,1,0:T(8,128)(2,1)S(1)}, bf16[2,8,64]{2,1,0:T(8,128)(2,1)S(1)}) fusion(f32[2,8,64]{2,1,0:T(8,128)} %param.16), kind=kLoop, calls=%fused_computation.26 | loop fusion | flops 4096 | bytes 8192 | tf_op jit(solution)/shard_map/convert.9
  9.6 1.0 %reduce-precision_convert_fusion.1 = (bf16[2,64,384]{2,1,0:T(8,128)(2,1)S(1)}, bf16[2,64,384]{2,1,0:T(8,128)(2,1)S(1)}) fusion(f32[2,64,384]{2,1,0:T(8,128)} %param.17), kind=kLoop, calls=%fused_computation.6 | loop fusion | flops 196608 | bytes 393216 | tf_op jit(solution)/shard_map/convert.6
  10.6 1.1 %fusion.3 = (bf16[2,1,384,128]{3,2,1,0:T(8,128)(2,1)S(1)}, bf16[2,1,384,128]{3,2,1,0:T(8,128)(2,1)S(1)}) fusion(f32[2,384,128]{2,1,0:T(8,128)} %param.18), kind=kLoop, calls=%fused_computation.9 | loop fusion | flops 393216 | bytes 786432 | tf_op jit(solution)/shard_map/stack | solution.py:52
  11.7 0.0 copy-start.1
  11.7 0.1 pad.12.clone
  11.8 0.0 copy-start
  11.8 0.1 maximum_bitcast_fusion.1
  11.9 0.1 copy.14.wide_in
  12.0 0.2 copy.15.wide_out
  12.2 0.0 collective-permute-done.1
  12.2 0.0 collective-permute-done
  12.3 0.1 copy-done.1
  12.4 0.1 collective-permute-start.3
  12.5 1.6 %collective-permute-start.2 = (bf16[6,3,16,128]{3,2,1,0:T(8,128)(2,1)S(1)}, bf16[6,3,16,128]{3,2,1,0:T(8,128)(2,1)S(1)}, u32[]{:S(2)}, u32[]{:S(2)}) collective-permute-start(bf16[6,3,16,128]{3,2,1,0:T(8,128)(2,1)S(1)} %pad_maximum_fusion.1.middle), channel_id=1, source_target_pairs={{0,3},{1,2},{2,1},{3,0},{4,7},{5,6},{6,5},{7,4},{8,11},{9,10},{10,... | collective-permute-start | bytes 221192 | tf_op jit(solution)/shard_map/ppermute | solution.py:884
  14.1 0.0 collective-permute-done.3
  14.1 2.4 %collective-permute-done.2 = bf16[6,3,16,128]{3,2,1,0:T(8,128)(2,1)S(1)} collective-permute-done((bf16[6,3,16,128]{3,2,1,0:T(8,128)(2,1)S(1)}, bf16[6,3,16,128]{3,2,1,0:T(8,128)(2,1)S(1)}, u32[]{:S(2)}, u32[]{:S(2)}) %collective-permute-start.2) | collective-permute-done | bytes 73760 | tf_op jit(solution)/shard_map/ppermute | solution.py:884
  16.6 0.0 copy-done
  16.6 7.6 %forward_and_second_back.1 = (f32[2,2,16]{2,1,0:T(2,128)}, bf16[4,5,16,128]{3,2,1,0:T(8,128)(2,1)S(1)}, f32[16,144,128]{2,1,0:T(8,128)S(1)}, f32[2,16,256]{2,1,0...) custom-call(bf16[6,3,16,128]{3,2,1,0:T(8,128)(2,1)S(1)} %get-tuple-element.28., ...), custom_call_target="tpu_custom_call" | custom-call | tf_op jit(solution)/shard_map/forward_and_second_back/pallas_call | solution.py:940
  24.2 3.4 %collective-permute-start.4 = (bf16[2,5,16,128]{3,2,1,0:T(8,128)(2,1)S(1)}, bf16[2,5,16,128]{3,2,1,0:T(8,128)(2,1)S(1)}, u32[]{:S(2)}, u32[]{:S(2)}) collective-permute-start(bf16[2,5,16,128]{3,2,1,0:T(8,128)(2,1)S(1)} %get-tuple-element.35), channel_id=1, source_target_pairs={{0,28},{4,8},{8,4},{12,16},{16,12},{20,24},{24,20},{28,0},{1,29},{... | collective-permute-start | bytes 122888 | tf_op jit(solution)/shard_map/ppermute | solution.py:884
  27.6 0.0 collective-permute-start.5
  27.6 3.4 %collective-permute-done.4 = bf16[2,5,16,128]{3,2,1,0:T(8,128)(2,1)S(1)} collective-permute-done((bf16[2,5,16,128]{3,2,1,0:T(8,128)(2,1)S(1)}, bf16[2,5,16,128]{3,2,1,0:T(8,128)(2,1)S(1)}, u32[]{:S(2)}, u32[]{:S(2)}) %collective-permute-start.4) | collective-permute-done | bytes 40992 | tf_op jit(solution)/shard_map/ppermute | solution.py:884
  31.0 0.7 %collective-permute-done.5 = bf16[2,5,16,128]{3,2,1,0:T(8,128)(2,1)S(1)} collective-permute-done((bf16[2,5,16,128]{3,2,1,0:T(8,128)(2,1)S(1)}, bf16[2,5,16,128]{3,2,1,0:T(8,128)(2,1)S(1)}, u32[]{:S(2)}, u32[]{:S(2)}) %collective-permute-start.5) | collective-permute-done | bytes 40992 | tf_op jit(solution)/shard_map/ppermute | solution.py:885
  31.8 0.1 collective-permute-start.7
  31.9 1.6 %collective-permute-start.6 = (bf16[4,3,16,128]{3,2,1,0:T(8,128)(2,1)S(1)}, bf16[4,3,16,128]{3,2,1,0:T(8,128)(2,1)S(1)}, u32[]{:S(2)}, u32[]{:S(2)}) collective-permute-start(bf16[4,3,16,128]{3,2,1,0:T(8,128)(2,1)S(1)} %get-tuple-element.32), channel_id=1, source_target_pairs={{0,3},{1,2},{2,1},{3,0},{4,7},{5,6},{6,5},{7,4},{8,11},{9,10},{10,... | collective-permute-start | bytes 147464 | tf_op jit(solution)/shard_map/ppermute | solution.py:884
  33.5 0.0 collective-permute-done.7
  33.5 2.0 %collective-permute-done.6 = bf16[4,3,16,128]{3,2,1,0:T(8,128)(2,1)S(1)} collective-permute-done((bf16[4,3,16,128]{3,2,1,0:T(8,128)(2,1)S(1)}, bf16[4,3,16,128]{3,2,1,0:T(8,128)(2,1)S(1)}, u32[]{:S(2)}, u32[]{:S(2)}) %collective-permute-start.6) | collective-permute-done | bytes 49184 | tf_op jit(solution)/shard_map/ppermute | solution.py:884
  35.5 4.2 %first_back.1 = (f32[64,128]{1,0:T(8,128)}, f32[2,3,2,16]{3,2,1,0:T(2,128)}) custom-call(f32[4,5,16,128]{3,2,1,0:T(8,128)S(1)} %get-tuple-element.26.total, bf16[4,3,16,128]{3,2,1,0:T(8,128)(2,1)S(1)} %get-tuple-element.30.before, bf16[4,3,16,128]{3,2,1,0:T(8,128)(2,1)S(1)} %get-tuple-element.29.after, f32[16,144,128]{2,1,0:T(8,128)S(1)} %get-tuple-element.14.kept, ...), custom_call_target="tpu_custom_call" | custom-call | tf_op jit(solution)/shard_map/first_back/pallas_call | solution.py:974
  (12 shorter events, 0.2 us)
Async XLA Ops:
  2.4 9.9 %collective-permute-start.1 = (bf16[2,3,16,128]{3,2,1,0:T(8,128)(2,1)}, bf16[2,3,16,128]{3,2,1,0:T(8,128)(2,1)S(1)}, u32[]{:S(2)}, u32[]{:S(2)}) collective-permute-start(bf16[2,3,16,128]{3,2,1,0:T(8,128)(2,1)} %block_of_atoms.1), channel_id=1, source_target_pairs={{0,4},{4,0},{8,12},{12,8},{16,20},{20,16},{24,28},{28,24},{1,5},{5... | collective-permute-start | bytes 73736 | tf_op jit(solution)/shard_map/ppermute | solution.py:885
  5.4 6.9 %collective-permute-start = (bf16[2,3,16,128]{3,2,1,0:T(8,128)(2,1)}, bf16[2,3,16,128]{3,2,1,0:T(8,128)(2,1)S(1)}, u32[]{:S(2)}, u32[]{:S(2)}) collective-permute-start(bf16[2,3,16,128]{3,2,1,0:T(8,128)(2,1)} %block_of_atoms.1), channel_id=1, source_target_pairs={{0,28},{4,8},{8,4},{12,16},{16,12},{20,24},{24,20},{28,0},{1,29},{... | collective-permute-start | bytes 73736 | tf_op jit(solution)/shard_map/ppermute | solution.py:884
  11.7 0.7 %copy-start.1 = (bf16[2,3,16,128]{3,2,1,0:T(8,128)(2,1)S(1)}, bf16[2,3,16,128]{3,2,1,0:T(8,128)(2,1)}, u32[]{:S(2)}) copy-start(bf16[2,3,16,128]{3,2,1,0:T(8,128)(2,1)} %block_of_atoms.1) | copy-start | bytes 73732
  11.8 4.8 %copy-start = (f32[128]{0:T(128)S(1)}, f32[128]{0:T(128)}, u32[]{:S(2)}) copy-start(f32[128]{0:T(128)} %param.19) | copy-start | bytes 1540
  12.4 1.7 %collective-permute-start.3 = (bf16[6,3,16,128]{3,2,1,0:T(8,128)(2,1)S(1)}, bf16[6,3,16,128]{3,2,1,0:T(8,128)(2,1)S(1)}, u32[]{:S(2)}, u32[]{:S(2)}) collective-permute-start(bf16[6,3,16,128]{3,2,1,0:T(8,128)(2,1)S(1)} %pad_maximum_fusion.1.middle), channel_id=1, source_target_pairs={{0,1},{1,0},{2,3},{3,2},{4,5},{5,4},{6,7},{7,6},{8,9},{9,8},{10,11... | collective-permute-start | bytes 221192 | tf_op jit(solution)/shard_map/ppermute | solution.py:885
  12.5 4.1 %collective-permute-start.2 = (bf16[6,3,16,128]{3,2,1,0:T(8,128)(2,1)S(1)}, bf16[6,3,16,128]{3,2,1,0:T(8,128)(2,1)S(1)}, u32[]{:S(2)}, u32[]{:S(2)}) collective-permute-start(bf16[6,3,16,128]{3,2,1,0:T(8,128)(2,1)S(1)} %pad_maximum_fusion.1.middle), channel_id=1, source_target_pairs={{0,3},{1,2},{2,1},{3,0},{4,7},{5,6},{6,5},{7,4},{8,11},{9,10},{10,... | collective-permute-start | bytes 221192 | tf_op jit(solution)/shard_map/ppermute | solution.py:884
  24.2 6.8 %collective-permute-start.4 = (bf16[2,5,16,128]{3,2,1,0:T(8,128)(2,1)S(1)}, bf16[2,5,16,128]{3,2,1,0:T(8,128)(2,1)S(1)}, u32[]{:S(2)}, u32[]{:S(2)}) collective-permute-start(bf16[2,5,16,128]{3,2,1,0:T(8,128)(2,1)S(1)} %get-tuple-element.35), channel_id=1, source_target_pairs={{0,28},{4,8},{8,4},{12,16},{16,12},{20,24},{24,20},{28,0},{1,29},{... | collective-permute-start | bytes 122888 | tf_op jit(solution)/shard_map/ppermute | solution.py:884
  27.6 4.2 %collective-permute-start.5 = (bf16[2,5,16,128]{3,2,1,0:T(8,128)(2,1)S(1)}, bf16[2,5,16,128]{3,2,1,0:T(8,128)(2,1)S(1)}, u32[]{:S(2)}, u32[]{:S(2)}) collective-permute-start(bf16[2,5,16,128]{3,2,1,0:T(8,128)(2,1)S(1)} %get-tuple-element.36), channel_id=1, source_target_pairs={{0,4},{4,0},{8,12},{12,8},{16,20},{20,16},{24,28},{28,24},{1,5},{5... | collective-permute-start | bytes 122888 | tf_op jit(solution)/shard_map/ppermute | solution.py:885
  31.8 1.7 %collective-permute-start.7 = (bf16[4,3,16,128]{3,2,1,0:T(8,128)(2,1)S(1)}, bf16[4,3,16,128]{3,2,1,0:T(8,128)(2,1)S(1)}, u32[]{:S(2)}, u32[]{:S(2)}) collective-permute-start(bf16[4,3,16,128]{3,2,1,0:T(8,128)(2,1)S(1)} %get-tuple-element.31), channel_id=1, source_target_pairs={{0,1},{1,0},{2,3},{3,2},{4,5},{5,4},{6,7},{7,6},{8,9},{9,8},{10,11... | collective-permute-start | bytes 147464 | tf_op jit(solution)/shard_map/ppermute | solution.py:885
  31.9 3.6 %collective-permute-start.6 = (bf16[4,3,16,128]{3,2,1,0:T(8,128)(2,1)S(1)}, bf16[4,3,16,128]{3,2,1,0:T(8,128)(2,1)S(1)}, u32[]{:S(2)}, u32[]{:S(2)}) collective-permute-start(bf16[4,3,16,128]{3,2,1,0:T(8,128)(2,1)S(1)} %get-tuple-element.32), channel_id=1, source_target_pairs={{0,3},{1,2},{2,1},{3,0},{4,7},{5,6},{6,5},{7,4},{8,11},{9,10},{10,... | collective-permute-start | bytes 147464 | tf_op jit(solution)/shard_map/ppermute | solution.py:884
